TPU v7x, 512 devices: a whole 4x4x16 slice. The times are simulated.
512 devices in a mesh: outer: 8 (over y_hi, x), dp: 64 (over y_lo, z, core).
Axes of the slice: x: 4, y: 4 (y_hi: 2, y_lo: 2; y = y_hi * 2 + y_lo), z: 16, core: 2. Of those that a mesh axis runs over, the one named last changes fastest.
Arguments:
- grads: bfloat16 [8, 64, 1, 256, 6144], P('outer', 'dp'), may hold values from -0.4375 to 0.4375
- basis: bfloat16 [256, 6144], P(None, 'dp'), may hold values from -6 to 6
- weights: float32 [1, 256, 6144], P(None, 'dp'), may hold values from -10 to 10
- moment: float32 [1, 256, 6144], P(None, 'dp'), may hold values from -4 to 4
- second: float32 [1, 256, 6144], P(None, 'dp'), may hold values from 0.0001 to 0.01
Outputs:
- weight_new: float32 [1, 256, 6144], P(None, 'dp')
- moment_new: float32 [1, 256, 6144], P(None, 'dp')
- second_new: float32 [1, 256, 6144], P(None, 'dp')
- gathered: bfloat16 [1, 256, 6144], replicated
All inputs are finite; a program needn't handle non-finite values.
Results may differ from a plain program's by a relative error of at most 0.006.
Values may be sent and summed in bfloat16 or wider, within the bound.
No kernel may reach another device: no remote copies, remote signals or barrier semaphores. Data moves between devices by JAX's collectives and lax.ppermute only.
A program may use at most 64 MiB of HBM per device.

v0:
```python
import jax
import jax.numpy as jnp
from jax import lax
from jax.sharding import PartitionSpec as P

beta_one = 0.9
beta_two = 0.999
bias_one = 1.0 - 0.9**10
bias_two = 1.0 - 0.999**10
adam_eps = 1e-06
norm_eps = 1e-06
decay = 0.01
rate = 0.1


def on_device(grads, basis, weights, moment, second):
    local_grad = grads[0, 0]
    layer_count, total_rows, model_width = local_grad.shape
    own_rows = weights.shape[1]
    sketch_rank = basis.shape[0]
    grad_rows = local_grad.reshape(layer_count * total_rows, model_width)
    whole_basis = lax.all_gather(basis, "dp", axis=1, tiled=True)
    sketch = lax.dot_general(
        grad_rows, whole_basis, (((1,), (1,)), ((), ())), preferred_element_type=jnp.float32
    )
    sketch = sketch.reshape(layer_count, total_rows, sketch_rank)
    summed = lax.psum(sketch, ("outer", "dp"))
    owned = lax.dynamic_slice_in_dim(summed, lax.axis_index("dp") * own_rows, own_rows, 1)
    owned_rows = owned.reshape(layer_count * own_rows, sketch_rank)
    estimate = jnp.dot(owned_rows, whole_basis.astype(jnp.float32), precision=lax.Precision.HIGHEST)
    estimate = (estimate / sketch_rank).reshape(layer_count, own_rows, model_width)
    moment_new = beta_one * moment + (1.0 - beta_one) * estimate
    second_new = beta_two * second + (1.0 - beta_two) * estimate * estimate
    update = moment_new / bias_one / (jnp.sqrt(second_new / bias_two) + adam_eps) + decay * weights
    update_local = jnp.sum(update * update, axis=(1, 2))
    weight_total, update_total = lax.psum(
        (jnp.sum(weights * weights, axis=(1, 2)), update_local), "dp"
    )
    trust_ratio = jnp.sqrt(weight_total) / (jnp.sqrt(update_total) + norm_eps)
    weight_new = weights - rate * trust_ratio[:, None, None] * update
    gathered = lax.all_gather(weight_new.astype(jnp.bfloat16), "dp", axis=1, tiled=True)
    return (weight_new, moment_new, second_new, gathered)


def solution(mesh):
    placed = (
        P("outer", "dp", None, None, None),
        P(None, "dp"),
        P(None, "dp", None),
        P(None, "dp", None),
        P(None, "dp", None),
    )
    return jax.shard_map(
        on_device,
        mesh=mesh,
        in_specs=placed,
        out_specs=(P(None, "dp", None), P(None, "dp", None), P(None, "dp", None), P()),
        check_vma=False,
    )
```

profile of v0, /device:TPU:1, one launch (start us, length us, event | category | flops | bytes accessed | tf_op | source)
XLA Modules:
  0.0 844.8 jit_solution(8537265217605419289)
XLA Ops:
  7.2 0.0 copy-start
  7.2 0.0 all-gather.3.cloned.1.call-start
  7.2 0.7 all-gather.3.cloned.1.call-update
  7.9 0.0 copy-start.1
  7.9 0.0 copy-start.2
  7.9 0.0 copy-start.3
  7.9 0.0 all-reduce.3.cloned.1.call-start
  8.0 131.4 %all-gather.3.cloned.1.call-done = bf16[256,6144]{0,1:T(8,128)(2,1)} async-done(((bf16[256,96]{0,1:T(8,128)(2,1)}), bf16[256,6144]{0,1:T(8,128)(2,1)}) %all-gather.3.cloned.1.call-update) | async-done | bytes 3145744 | tf_op jit(solution)/shard_map/all_gather | solution.py:22
  139.4 0.0 copy-done
  139.4 3.6 fusion.2
  143.0 0.0 all-reduce.3.cloned.1.call-update
  143.0 0.0 all-gather.5.cloned.1.call-start
  143.0 454.3 %all-reduce.3.cloned.1.call-done = f32[1,256,256]{2,1,0:T(8,128)} async-done(((f32[1,256,256]{2,1,0:T(8,128)}), f32[1,256,256]{2,1,0:T(8,128)}) %all-reduce.3.cloned.1.call-update) | async-done | bytes 262160 | tf_op jit(solution)/shard_map/psum | solution.py:27
  597.3 0.0 copy-done.1
  597.3 0.0 copy-done.2
  597.3 0.0 copy-done.3
  597.3 5.7 multiply_reduce_fusion
  603.0 106.6 %all-reduce = (f32[1]{0:T(128)}, f32[1]{0:T(128)}) all-reduce(f32[1]{0:T(128)} %bitcast, f32[1]{0:T(128)} %bitcast.6), channel_id=1, replica_groups=mesh['outer'=8,'dp'=64] {'dp'}, use_global_device_ids=true, to_apply=%region_1.0 | all-reduce | flops 2 | bytes 16 | tf_op jit(solution)/shard_map/psum | solution.py:36
  711.1 0.7 fusion.9
  711.7 0.7 copy.9
  712.4 0.0 all-gather.5.cloned.1.call-update
  712.5 119.6 %all-gather.5.cloned.1.call-done = bf16[1,256,6144]{2,0,1:T(2,128)(2,1)} async-done(((bf16[1,4,6144]{2,0,1:T(2,128)(2,1)}), bf16[1,256,6144]{2,0,1:T(2,128)(2,1)}) %all-gather.5.cloned.1.call-update) | async-done | bytes 3145744 | tf_op jit(solution)/shard_map/all_gather | solution.py:41
  832.0 6.2 copy.10
Async XLA Ops:
  7.2 132.2 %copy-start = (bf16[1,1,1,256,6144]{4,3,2,1,0:T(8,128)(2,1)S(1)}, bf16[1,1,1,256,6144]{4,3,2,1,0:T(8,128)(2,1)}, u32[]{:S(2)}) copy-start(bf16[1,1,1,256,6144]{4,3,2,1,0:T(8,128)(2,1)} %param.5) | copy-start | bytes 9437188
  7.2 132.2 %all-gather.3.cloned.1.call-start = ((), (), s32[]{:S(2)}) async-start(), calls=%async_computation | async-start | bytes 3194880 | tf_op jit(solution)/shard_map/all_gather | solution.py:22
  7.9 589.4 %copy-start.1 = (f32[1,4,6144]{2,1,0:T(4,128)S(1)}, f32[1,4,6144]{2,1,0:T(4,128)}, u32[]{:S(2)}) copy-start(f32[1,4,6144]{2,1,0:T(4,128)} %param.7) | copy-start | bytes 294916
  7.9 589.4 %copy-start.2 = (f32[1,4,6144]{2,1,0:T(4,128)S(1)}, f32[1,4,6144]{2,1,0:T(4,128)}, u32[]{:S(2)}) copy-start(f32[1,4,6144]{2,1,0:T(4,128)} %param.8) | copy-start | bytes 294916
  7.9 589.4 %copy-start.3 = (f32[1,4,6144]{2,1,0:T(4,128)S(1)}, f32[1,4,6144]{2,1,0:T(4,128)}, u32[]{:S(2)}) copy-start(f32[1,4,6144]{2,1,0:T(4,128)} %param.9) | copy-start | bytes 294916
  7.9 589.4 %all-reduce.3.cloned.1.call-start = ((), (), s32[]{:S(2)}) async-start(), calls=%async_computation.1 | async-start | bytes 524288 | tf_op jit(solution)/shard_map/psum | solution.py:27
  143.0 689.0 %all-gather.5.cloned.1.call-start = ((), (), s32[]{:S(2)}) async-start(), calls=%async_computation.2 | async-start | bytes 6389760 | tf_op jit(solution)/shard_map/all_gather | solution.py:41
Sparse Core Ops, SparseCore 0:
  10.2 129.1 all-gather.2
  145.4 451.8 all-reduce.2
  712.6 119.3 all-gather.4
where the time goes:
time: 845 us
  waiting for transfers between devices  706 us (84%)
  blocking collectives  107 us (13%)
  between operations  15.2 us (2%)
  matrix products  9.29 us (1%)
    psum x1, waiting for transfers between devices, on_device(): summed = lax.psum(sketch, ('outer', 'dp'))  454 us
    all_gather x1, waiting for transfers between devices, on_device(): whole_basis = lax.all_gather(basis, 'dp', axis=1, tiled=True)  131 us
    all_gather x1, waiting for transfers between devices, on_device(): lax.all_gather(weight_new.astype(jnp.bfloat16), 'dp', axis=1, tiled=True)  120 us
    psum x1, blocking collectives, on_device(): lax.psum((jnp.sum(weights * weights, axis=(1, 2)), update_local), 'dp')  107 us
  transfers between devices with their start and end apart: 3, of which 3 were waited for; matrix products, arithmetic and copies ran while one was open for 0% of the time, Pallas kernels for 0%

commit v1 on v0

v1 whole, which is shorter than its diff:
```python
import jax
import jax.numpy as jnp
from jax import lax
from jax.sharding import Mesh
from jax.sharding import PartitionSpec as P

beta_one = 0.9
beta_two = 0.999
bias_one = 1.0 - 0.9**10
bias_two = 1.0 - 0.999**10
adam_eps = 1e-06
norm_eps = 1e-06
decay = 0.01
rate = 0.1

FINE = {"yh": 2, "x": 4, "yl": 2, "z": 16, "c": 2}
OUTER = ("yh", "x")
DP = ("yl", "z", "c")
PLANE = ("yl", "yh", "x")
SWAP = [(0, 1), (1, 0)]


def exchange(blocks, axes):
    return lax.all_to_all(blocks, axes, 0, 0, tiled=True)


def share(block, axes, count):
    return exchange(jnp.broadcast_to(block[None], (count,) + block.shape), axes)


def swap(block):
    return lax.ppermute(block, "c", SWAP)


def in_core_order(core, mine, other, axis):
    first = jnp.where(core == 0, mine, other)
    second = jnp.where(core == 0, other, mine)
    return first, second


def pieces(values, count):
    parts = []
    rest = values
    for _ in range(count):
        part = lax.reduce_precision(rest, 8, 7)
        parts.append(part.astype(jnp.bfloat16))
        rest = rest - part
    return jnp.concatenate(parts, axis=0)


def estimate_rows(halves, core, own_basis, other_basis, count):
    rows = halves.shape[1]
    total = 0.0
    for half, basis in ((core, own_basis), (1 - core, other_basis)):
        left = pieces(lax.dynamic_index_in_dim(halves, half, 0, keepdims=False), count)
        total = total + lax.dot_general(
            left, basis, (((1,), (1,)), ((), ())), preferred_element_type=jnp.float32
        )
    total = total.reshape(count, rows, -1)
    return jnp.sum(total, axis=0) / 256


def moments(estimate, weights, moment, second):
    moment_new = beta_one * moment + (1.0 - beta_one) * estimate
    second_new = beta_two * second + (1.0 - beta_two) * estimate * estimate
    update = moment_new / bias_one / (jnp.sqrt(second_new / bias_two) + adam_eps) + decay * weights
    return moment_new, second_new, update


def on_device(grads, basis, weights, moment, second):
    grad = grads[0, 0, 0]
    width = grad.shape[1]
    core = lax.axis_index("c")
    deep = lax.axis_index("z")
    low = lax.axis_index("yl")
    outer = lax.axis_index("yh") * 4 + lax.axis_index("x")

    state = jnp.concatenate([moment, second, weights], axis=0).astype(jnp.bfloat16)
    state_z = lax.all_gather(state, "z")
    other_grad = swap(grad)

    turned = basis.T
    half = turned.shape[1] // 2
    mine = lax.dynamic_slice_in_dim(turned, half * core, half, 1)
    theirs = swap(lax.dynamic_slice_in_dim(turned, half * (1 - core), half, 1))
    chip = jnp.concatenate(in_core_order(core, mine, theirs, 0), axis=0)
    part = chip.shape[0] // 8
    piece = lax.dynamic_slice_in_dim(chip, part * outer, part, 0)
    along_z = share(piece, "z", 16)
    blocks = share(along_z, PLANE, 16).reshape(2, 8, 16, part, half)
    own_basis = blocks.transpose(0, 2, 1, 3, 4).reshape(width, half)
    other_basis = swap(own_basis)

    contract = (((1,), (0,)), ((), ()))
    sketch = lax.dot_general(grad, own_basis, contract, preferred_element_type=jnp.float32)
    sketch = sketch + lax.dot_general(
        other_grad, own_basis, contract, preferred_element_type=jnp.float32
    )
    plane_sum = jnp.sum(exchange(sketch.reshape(16, 16, half), PLANE), axis=0)
    spread = jnp.broadcast_to(plane_sum.reshape(1, 2, 8, half), (16, 2, 8, half))
    halves = jnp.sum(
        exchange(spread.reshape(32, 8, half), ("z", "c")).reshape(16, 2, 8, half), axis=0
    )

    picked = lax.dynamic_index_in_dim(state_z, 2 * outer + core, 0, keepdims=False)
    passed = swap(lax.dynamic_index_in_dim(state_z, 2 * outer + 1 - core, 0, keepdims=False))
    m8, v8, w8 = jnp.concatenate(in_core_order(core, picked, passed, 1), axis=1).astype(jnp.float32)
    estimate8 = estimate_rows(halves, core, own_basis, other_basis, 2)
    _, _, update8 = moments(estimate8, w8, m8, v8)
    squares = jnp.stack([jnp.sum(w8 * w8), jnp.sum(update8 * update8)])
    notes = jnp.zeros((8, half), jnp.float32).at[0, :2].set(squares)
    for_core = halves.reshape(2, 2, 4, half).transpose(1, 0, 2, 3).reshape(2, 8, half)
    message = jnp.concatenate([for_core, jnp.broadcast_to(notes[None], (2, 8, half))], axis=1)
    inbox = exchange(
        jnp.broadcast_to(message[None], (16, 2, 16, half)).reshape(32, 16, half), PLANE + ("c",)
    )
    totals = jnp.sum(inbox[:, 8, :2], axis=0)
    trust_ratio = jnp.sqrt(totals[0]) / (jnp.sqrt(totals[1]) + norm_eps)
    rows8 = (w8 - rate * trust_ratio * update8).astype(jnp.bfloat16)
    rows_mine = share(rows8, PLANE, 16)
    rows_other = swap(rows_mine)
    gathered = jnp.stack(in_core_order(core, rows_mine, rows_other, 1), axis=1)
    gathered = gathered.reshape(1, 256, width)

    own = lax.dynamic_index_in_dim(inbox, low * 16 + deep, 0, keepdims=False)[:8]
    estimate = estimate_rows(own.reshape(2, 4, half), core, own_basis, other_basis, 3)[None]
    moment_new, second_new, update = moments(estimate, weights, moment, second)
    weight_new = weights - rate * trust_ratio * update
    return (weight_new, moment_new, second_new, gathered)


def solution(mesh):
    fine = Mesh(mesh.devices.reshape(tuple(FINE.values())), tuple(FINE))
    rows = P(None, DP, None)
    return jax.shard_map(
        on_device,
        mesh=fine,
        in_specs=(P(OUTER, DP, None, None, None), P(None, DP), rows, rows, rows),
        out_specs=(rows, rows, rows, P()),
        check_vma=False,
    )
```

time: 845 us -> 192 us (0.23)
  waiting for transfers between devices: 706 us -> 45.1 us
  blocking collectives: 107 us -> 59.2 us
  starting transfers between devices: 0.12 us -> 44.4 us
  other arithmetic: 0.68 us -> 12.7 us
    psum x1 -> x0, waiting for transfers between devices: 454 us -> none  [on_device(): summed = lax.psum(sketch, ('outer', 'dp'))]
    all_gather x2 -> x1, waiting for transfers between devices: 251 us -> 0.01 us  [on_device(): state_z = lax.all_gather(state, 'z')]
    psum x1 -> x0, blocking collectives: 107 us -> none  [on_device(): lax.psum((jnp.sum(weights * weights, axis=(1, 2)), update_local), 'dp')]
    all_to_all x0 -> x3, blocking collectives: none -> 59.2 us  [exchange(): return lax.all_to_all(blocks, axes, 0, 0, tiled=True)]
    all_to_all x0 -> x3, waiting for transfers between devices: none -> 42 us  [exchange(): return lax.all_to_all(blocks, axes, 0, 0, tiled=True)]
    ppermute x0 -> x5, starting transfers between devices: none -> 23.8 us  [swap(): return lax.ppermute(block, 'c', SWAP)]
    all_to_all x0 -> x3, starting transfers between devices: none -> 20.5 us  [exchange(): return lax.all_to_all(blocks, axes, 0, 0, tiled=True)]
  transfers between devices with their start and end apart: 3 -> 9, of which waited for: 3 -> 5; matrix products, arithmetic and copies ran while one was open for 0% -> 8% of each run, Pallas kernels for 0% -> 0%
where the time goes in v1:
time: 192 us; the launch traced here: 191 us
  blocking collectives  59.2 us (31%)
  waiting for transfers between devices  45.1 us (23%)
  starting transfers between devices  44.4 us (23%)
  between operations  15.7 us (8%)
  other arithmetic  12.7 us (7%)
  local copies, waits for them, and re-layouts  7.63 us (4%)
  matrix products  6.32 us (3%)
    all_to_all x3, blocking collectives, exchange(): return lax.all_to_all(blocks, axes, 0, 0, tiled=True)  59.2 us
    all_to_all x3, waiting for transfers between devices, exchange(): return lax.all_to_all(blocks, axes, 0, 0, tiled=True)  42 us
    ppermute x5, starting transfers between devices, swap(): return lax.ppermute(block, 'c', SWAP)  23.8 us
    all_to_all x3, starting transfers between devices, exchange(): return lax.all_to_all(blocks, axes, 0, 0, tiled=True)  20.5 us
    another operation x2, other arithmetic, on_device(): gathered = jnp.stack(in_core_order(core, rows_mine, rows_other, 1), axis=1)  4.04 us
  transfers between devices with their start and end apart: 9, of which 5 were waited for; matrix products, arithmetic and copies ran while one was open for 8% of the time, Pallas kernels for 0%

profile of v1, /device:TPU:1, one launch (start us, length us, event | category | flops | bytes accessed | tf_op | source)
XLA Modules:
  0.0 191.0 jit_solution(13020249074276840813)
XLA Ops:
  7.2 0.0 all-gather.2.cloned.1.call-start
  7.2 8.8 %collective-permute-start.1 = (bf16[256,6144]{1,0:T(8,128)(2,1)}, bf16[256,6144]{1,0:T(8,128)(2,1)}, u32[]{:S(2)}, u32[]{:S(2)}) collective-permute-start(bf16[256,6144]{1,0:T(8,128)(2,1)} %bitcast.148), channel_id=1, source_target_pairs={{0,1},{1,0},{2,3},{3,2},{4,5},{5,4},{6,7},{7,6},{8,9},{9,8},{10,11... | collective-permute-start | bytes 9437192 | tf_op jit(solution)/shard_map/ppermute | solution.py:32
  16.0 0.9 convert_bitcast_fusion.2
  16.9 1.0 convert_bitcast_fusion
  17.9 0.8 pad_maximum_fusion.1
  18.7 0.0 all-gather.2.cloned.1.call-update
  18.7 0.7 dynamic-slice_bitcast_fusion.1
  19.5 1.9 collective-permute-start
  21.4 1.1 collective-permute-done
  22.5 0.8 bitcast_select_fusion.2
  23.4 21.3 %all_to_all.30 = bf16[16,24,128]{2,1,0:T(8,128)(2,1)S(1)} all-to-all(bf16[16,24,128]{2,1,0:T(8,128)(2,1)S(1)} %broadcast_in_dim.18), channel_id=1, replica_groups=mesh['yh'=2,'x'=4,'yl'=2,'z'=16,'c'=2] {'z'}, dimensions={0} | all-to-all | bytes 196608 | tf_op jit(solution)/shard_map/all_to_all | solution.py:24
  44.7 0.3 broadcast_in_dim.19
  45.0 25.4 %all_to_all.31 = bf16[16,16,24,128]{3,2,1,0:T(8,128)(2,1)S(1)} all-to-all(bf16[16,16,24,128]{3,2,1,0:T(8,128)(2,1)S(1)} %broadcast_in_dim.19), channel_id=1, replica_groups=mesh['yh'=2,'x'=4,'yl'=2,'z'=16,'c'=2] {'yl','yh','x'}, dimensions={0} | all-to-all | bytes 3145728 | tf_op jit(solution)/shard_map/all_to_all | solution.py:24
  70.4 0.0 copy-start
  70.4 0.4 copy.25
  70.8 1.5 copy-done
  72.3 1.2 fusion.53
  73.5 0.0 collective-permute-done.1
  73.5 3.1 %fusion.2 = f32[256,128]{0,1:T(8,128)S(1)} fusion(f32[128,256]{1,0:T(8,128)S(1)} %fusion.53, bf16[6144,128]{1,0:T(8,128)(2,1)S(1)} %bitcast.143, bf16[256,6144]{1,0:T(8,128)(2,1)} %collective-permute-done.1), kind=kOutput, calls=%fused_computation.8 | convolution fusion | flops 402685952 | bytes 4980736 | tf_op jit(solution)/shard_map/dot_general | solution.py:96
  76.6 0.7 copy.26
  77.3 3.5 %all-to-all-start.2 = ((f32[16,16,128]{2,1,0:T(8,128)}), f32[16,16,128]{2,1,0:T(8,128)S(1)}, u32[]{:S(2)}, u32[]{:S(2)}) async-start(f32[16,16,128]{2,1,0:T(8,128)} %bitcast.7), calls=%async_computation.2 | async-start | bytes 262144 | tf_op jit(solution)/shard_map/all_to_all | solution.py:24
  80.8 6.9 %collective-permute-start.3 = (bf16[6144,128]{1,0:T(8,128)(2,1)S(1)}, bf16[6144,128]{1,0:T(8,128)(2,1)S(1)}, u32[]{:S(2)}, u32[]{:S(2)}) collective-permute-start(bf16[6144,128]{1,0:T(8,128)(2,1)S(1)} %bitcast.144), channel_id=1, source_target_pairs={{0,1},{1,0},{2,3},{3,2},{4,5},{5,4},{6,7},{7,6},{8,9},{9,8},{10,11... | collective-permute-start | bytes 4718600 | tf_op jit(solution)/shard_map/ppermute | solution.py:32
  87.7 0.0 all-to-all-done.2
  87.7 0.7 broadcast_in_dim.21
  88.4 12.6 %all-to-all-start.3 = ((f32[32,8,128]{2,1,0:T(8,128)}), f32[32,8,128]{2,1,0:T(8,128)S(1)}, u32[]{:S(2)}, u32[]{:S(2)}) async-start(f32[32,8,128]{2,1,0:T(8,128)} %bitcast.9), calls=%async_computation.3 | async-start | bytes 262144 | tf_op jit(solution)/shard_map/all_to_all | solution.py:24
  101.0 15.8 %all-to-all-done.3 = f32[32,8,128]{2,1,0:T(8,128)S(1)} async-done(((f32[32,8,128]{2,1,0:T(8,128)}), f32[32,8,128]{2,1,0:T(8,128)S(1)}, u32[]{:S(2)}, u32[]{:S(2)}) %all-to-all-start.3) | async-done | bytes 131104 | tf_op jit(solution)/shard_map/all_to_all | solution.py:24
  116.9 0.5 fusion.25
  117.4 0.0 all-gather.2.cloned.1.call-done
  117.4 1.0 dynamic-slice_bitcast_fusion
  118.4 3.5 %collective-permute-start.2 = (bf16[3,4,6144]{2,1,0:T(4,128)(2,1)S(1)}, bf16[3,4,6144]{2,1,0:T(4,128)(2,1)S(1)}, u32[]{:S(2)}, u32[]{:S(2)}) collective-permute-start(bf16[3,4,6144]{2,1,0:T(4,128)(2,1)S(1)} %dynamic-slice_bitcast_fusion), channel_id=1, source_target_pairs={{0,1},{1,0},{2,3},{3,2},{4,5},{5,4},{6,7},{7,6},{8,9},{9,8},{10,11... | collective-permute-start | bytes 442376 | tf_op jit(solution)/shard_map/ppermute | solution.py:32
  121.9 0.0 collective-permute-done.3
  121.9 0.5 fusion.1
  122.4 0.5 collective-permute-done.2
  122.9 1.0 bitcast_select_fusion.1
  123.9 0.1 maximum_convert_fusion
  124.0 0.6 multiply_reduce_fusion
  124.7 0.8 fusion.12
  125.5 1.4 maximum_bitcast_fusion
  126.9 12.5 %all_to_all.32 = f32[32,16,128]{2,1,0:T(8,128)S(1)} all-to-all(f32[32,16,128]{2,1,0:T(8,128)S(1)} %bitcast.150), channel_id=1, replica_groups=mesh['yh'=2,'x'=4,'yl'=2,'z'=16,'c'=2] {'yl','yh','x','c'}, dimensions={0} | all-to-all | bytes 524288 | tf_op jit(solution)/shard_map/all_to_all | solution.py:24
  139.3 0.1 slice_reduce_fusion
  139.4 0.6 fusion.55
  141.4 0.2 fusion.19
  141.6 1.3 broadcast_in_dim.51
  142.9 4.4 %all-to-all-start.5 = ((bf16[16,8,6144]{2,1,0:T(8,128)(2,1)}), bf16[16,8,6144]{2,1,0:T(8,128)(2,1)}, u32[]{:S(2)}, u32[]{:S(2)}) async-start(bf16[16,8,6144]{2,1,0:T(8,128)(2,1)} %broadcast_in_dim.51), calls=%async_computation.5 | async-start | bytes 3145728 | tf_op jit(solution)/shard_map/all_to_all | solution.py:24
  147.3 0.5 fusion.32
  147.8 26.1 %all-to-all-done.5 = bf16[16,8,6144]{2,1,0:T(8,128)(2,1)} async-done(((bf16[16,8,6144]{2,1,0:T(8,128)(2,1)}), bf16[16,8,6144]{2,1,0:T(8,128)(2,1)}, u32[]{:S(2)}, u32[]{:S(2)}) %all-to-all-start.5) | async-done | bytes 1572896 | tf_op jit(solution)/shard_map/all_to_all | solution.py:24
  174.0 2.8 %collective-permute-start.4 = (bf16[16,8,6144]{2,1,0:T(8,128)(2,1)}, bf16[16,8,6144]{2,1,0:T(8,128)(2,1)}, u32[]{:S(2)}, u32[]{:S(2)}) collective-permute-start(bf16[16,8,6144]{2,1,0:T(8,128)(2,1)} %all-to-all-done.5), channel_id=1, source_target_pairs={{0,1},{1,0},{2,3},{3,2},{4,5},{5,4},{6,7},{7,6},{8,9},{9,8},{10,11... | collective-permute-start | bytes 4718600 | tf_op jit(solution)/shard_map/ppermute | solution.py:32
  176.8 0.0 copy-start.1
  176.8 0.0 copy-start.2
  176.8 0.0 copy-start.3
  176.8 0.5 convolution_add_fusion
  177.3 0.1 reshape.210
  177.4 0.1 reduce_sum.69
  177.5 0.2 copy-done.1
  177.7 0.0 copy-done.2
  177.7 0.0 copy-done.3
  177.8 0.8 multiply_subtract_fusion
  178.6 1.5 collective-permute-done.4
  180.1 2.1 %select_bitcast_fusion.1 = (bf16[16,1,8,6144]{3,2,1,0:T(8,128)(2,1)S(1)}, bf16[16,1,8,6144]{3,2,1,0:T(8,128)(2,1)S(1)}) fusion(bf16[16,8,6144]{2,1,0:T(8,128)(2,1)} %all-to-all-done.5, bf16[16,8,6144]{2,1,0:T(8,128)(2,1)} %collective-permute-done.4, pred[]{:T(512)S(6)} %eq.2), kind=kLoop, calls=%fused_computation.5 | loop fusion | flops 1572864 | bytes 6291457 | tf_op jit(solution)/shard_map/stack | solution.py:122
  182.2 2.0 %pad_maximum_fusion = bf16[16,2,8,6144]{3,2,1,0:T(8,128)(2,1)} fusion(bf16[16,1,8,6144]{3,2,1,0:T(8,128)(2,1)S(1)} %get-tuple-element.20, bf16[16,1,8,6144]{3,2,1,0:T(8,128)(2,1)S(1)} %get-tuple-element.19), kind=kLoop, calls=%fused_computation.3 | loop fusion | flops 1572864 | bytes 6291456 | tf_op jit(solution)/shard_map/stack | solution.py:122
  (12 shorter events, 0.2 us)
Async XLA Ops:
  7.2 110.2 %all-gather.2.cloned.1.call-start = ((), (), s32[]{:S(2)}) async-start(), calls=%async_computation.6 | async-start | bytes 2506752 | tf_op jit(solution)/shard_map/all_gather | solution.py:79
  7.2 66.3 %collective-permute-start.1 = (bf16[256,6144]{1,0:T(8,128)(2,1)}, bf16[256,6144]{1,0:T(8,128)(2,1)}, u32[]{:S(2)}, u32[]{:S(2)}) collective-permute-start(bf16[256,6144]{1,0:T(8,128)(2,1)} %bitcast.148), channel_id=1, source_target_pairs={{0,1},{1,0},{2,3},{3,2},{4,5},{5,4},{6,7},{7,6},{8,9},{9,8},{10,11... | collective-permute-start | bytes 9437192 | tf_op jit(solution)/shard_map/ppermute | solution.py:32
  19.5 3.1 %collective-permute-start = (bf16[96,128]{1,0:T(8,128)(2,1)S(1)}, bf16[96,128]{1,0:T(8,128)(2,1)S(1)}, u32[]{:S(2)}, u32[]{:S(2)}) collective-permute-start(bf16[96,128]{1,0:T(8,128)(2,1)S(1)} %dynamic-slice_bitcast_fusion.1), channel_id=1, source_target_pairs={{0,1},{1,0},{2,3},{3,2},{4,5},{5,4},{6,7},{7,6},{8,9},{9,8},{10,11... | collective-permute-start | bytes 73736 | tf_op jit(solution)/shard_map/ppermute | solution.py:32
  70.4 1.9 copy-start
  77.3 10.4 %all-to-all-start.2 = ((f32[16,16,128]{2,1,0:T(8,128)}), f32[16,16,128]{2,1,0:T(8,128)S(1)}, u32[]{:S(2)}, u32[]{:S(2)}) async-start(f32[16,16,128]{2,1,0:T(8,128)} %bitcast.7), calls=%async_computation.2 | async-start | bytes 262144 | tf_op jit(solution)/shard_map/all_to_all | solution.py:24
  80.8 41.1 %collective-permute-start.3 = (bf16[6144,128]{1,0:T(8,128)(2,1)S(1)}, bf16[6144,128]{1,0:T(8,128)(2,1)S(1)}, u32[]{:S(2)}, u32[]{:S(2)}) collective-permute-start(bf16[6144,128]{1,0:T(8,128)(2,1)S(1)} %bitcast.144), channel_id=1, source_target_pairs={{0,1},{1,0},{2,3},{3,2},{4,5},{5,4},{6,7},{7,6},{8,9},{9,8},{10,11... | collective-permute-start | bytes 4718600 | tf_op jit(solution)/shard_map/ppermute | solution.py:32
  88.4 28.4 %all-to-all-start.3 = ((f32[32,8,128]{2,1,0:T(8,128)}), f32[32,8,128]{2,1,0:T(8,128)S(1)}, u32[]{:S(2)}, u32[]{:S(2)}) async-start(f32[32,8,128]{2,1,0:T(8,128)} %bitcast.9), calls=%async_computation.3 | async-start | bytes 262144 | tf_op jit(solution)/shard_map/all_to_all | solution.py:24
  118.4 4.5 %collective-permute-start.2 = (bf16[3,4,6144]{2,1,0:T(4,128)(2,1)S(1)}, bf16[3,4,6144]{2,1,0:T(4,128)(2,1)S(1)}, u32[]{:S(2)}, u32[]{:S(2)}) collective-permute-start(bf16[3,4,6144]{2,1,0:T(4,128)(2,1)S(1)} %dynamic-slice_bitcast_fusion), channel_id=1, source_target_pairs={{0,1},{1,0},{2,3},{3,2},{4,5},{5,4},{6,7},{7,6},{8,9},{9,8},{10,11... | collective-permute-start | bytes 442376 | tf_op jit(solution)/shard_map/ppermute | solution.py:32
  142.9 31.1 %all-to-all-start.5 = ((bf16[16,8,6144]{2,1,0:T(8,128)(2,1)}), bf16[16,8,6144]{2,1,0:T(8,128)(2,1)}, u32[]{:S(2)}, u32[]{:S(2)}) async-start(bf16[16,8,6144]{2,1,0:T(8,128)(2,1)} %broadcast_in_dim.51), calls=%async_computation.5 | async-start | bytes 3145728 | tf_op jit(solution)/shard_map/all_to_all | solution.py:24
  174.0 6.1 %collective-permute-start.4 = (bf16[16,8,6144]{2,1,0:T(8,128)(2,1)}, bf16[16,8,6144]{2,1,0:T(8,128)(2,1)}, u32[]{:S(2)}, u32[]{:S(2)}) collective-permute-start(bf16[16,8,6144]{2,1,0:T(8,128)(2,1)} %all-to-all-done.5), channel_id=1, source_target_pairs={{0,1},{1,0},{2,3},{3,2},{4,5},{5,4},{6,7},{7,6},{8,9},{9,8},{10,11... | collective-permute-start | bytes 4718600 | tf_op jit(solution)/shard_map/ppermute | solution.py:32
  176.8 0.9 copy-start.1
  176.8 0.9 copy-start.2
  176.8 1.0 copy-start.3
Sparse Core Ops, SparseCore 0:
  18.8 67.3 all-gather.1

commit v2 on v1

v2 whole, which is shorter than its diff:
```python
import jax
import jax.numpy as jnp
from jax import lax
from jax.experimental import pallas as pl
from jax.experimental.pallas import tpu as pltpu
from jax.sharding import Mesh
from jax.sharding import PartitionSpec as P

beta_one = 0.9
beta_two = 0.999
bias_one = 1.0 - 0.9**10
bias_two = 1.0 - 0.999**10
adam_eps = 1e-06
norm_eps = 1e-06
decay = 0.01
rate = 0.1

FINE = {"yh": 2, "x": 4, "yl": 2, "z": 16, "c": 2}
OUTER = ("yh", "x")
DP = ("yl", "z", "c")
PLANE = ("yl", "yh", "x")
SWAP = [(0, 1), (1, 0)]


def exchange(blocks, axes):
    return lax.all_to_all(blocks, axes, 0, 0, tiled=True)


def share(block, axes, count):
    return exchange(jnp.broadcast_to(block[None], (count,) + block.shape), axes)


def swap(block):
    return lax.ppermute(block, "c", SWAP)


def in_order(position, mine, other, axis):
    shape = [1] * (mine.ndim + 1)
    shape[axis] = 2
    here = (jnp.arange(2) == position).reshape(shape)
    return jnp.where(here, jnp.expand_dims(mine, axis), jnp.expand_dims(other, axis))


def pieces(values, count):
    parts = []
    rest = values
    for _ in range(count):
        part = lax.reduce_precision(rest, 8, 7)
        parts.append(part.astype(jnp.bfloat16))
        rest = rest - part
    return jnp.concatenate(parts, axis=0)


def estimate_rows(halves, core, own_basis, other_basis, count):
    rows = halves.shape[1]
    total = 0.0
    for half, basis in ((core, own_basis), (1 - core, other_basis)):
        left = pieces(lax.dynamic_index_in_dim(halves, half, 0, keepdims=False), count)
        total = total + lax.dot_general(
            left, basis, (((1,), (1,)), ((), ())), preferred_element_type=jnp.float32
        )
    total = total.reshape(count, rows, -1)
    return jnp.sum(total, axis=0) / 256


def moments(estimate, weights, moment, second):
    moment_new = beta_one * moment + (1.0 - beta_one) * estimate
    second_new = beta_two * second + (1.0 - beta_two) * estimate * estimate
    update = moment_new / bias_one / (jnp.sqrt(second_new / bias_two) + adam_eps) + decay * weights
    return moment_new, second_new, update


VMEM = pl.BlockSpec(memory_space=pltpu.VMEM)
SMEM = pl.BlockSpec(memory_space=pltpu.SMEM)
LIMIT = pltpu.CompilerParams(vmem_limit_bytes=40 << 20)
CHUNK = 512


def update_kernel(core_ref, terms_ref, own_ref, other_ref, state_ref, update_ref, message_ref):
    first, second = terms_ref[0], terms_ref[16]
    for step in range(1, 16):
        first = first + terms_ref[step]
        second = second + terms_ref[16 + step]
    at_first = core_ref[0] == 0

    def left_of(half):
        high = half.astype(jnp.bfloat16).astype(jnp.float32)
        return jnp.concatenate([high, half - high], axis=0).astype(jnp.bfloat16)

    left_own = left_of(jnp.where(at_first, first, second))
    left_other = left_of(jnp.where(at_first, second, first))
    contract = (((1,), (1,)), ((), ()))
    weight_sq = jnp.zeros((8, CHUNK), jnp.float32)
    update_sq = jnp.zeros((8, CHUNK), jnp.float32)
    for start in range(0, own_ref.shape[0], CHUNK):
        part = pl.ds(start, CHUNK)
        both = lax.dot_general(
            left_own, own_ref[part, :], contract, preferred_element_type=jnp.float32
        ) + lax.dot_general(
            left_other, other_ref[part, :], contract, preferred_element_type=jnp.float32
        )
        weights = state_ref[2, :, part]
        _, _, update = moments(
            (both[:8] + both[8:]) / 256, weights, state_ref[0, :, part], state_ref[1, :, part]
        )
        update_ref[:, part] = update
        weight_sq = weight_sq + weights * weights
        update_sq = update_sq + update * update
    row = lax.broadcasted_iota(jnp.int32, (8, 128), 0)
    lane = lax.broadcasted_iota(jnp.int32, (8, 128), 1)
    notes = jnp.where(
        (row == 0) & (lane == 0),
        jnp.sum(weight_sq),
        jnp.where((row == 0) & (lane == 1), jnp.sum(update_sq), 0.0),
    )
    for core in range(2):
        rows = slice(4 * core, 4 * core + 4)
        sent = jnp.concatenate([first[rows], second[rows]], axis=0)
        for place in range(16):
            message_ref[16 * core + place, 0:8, :] = sent
            message_ref[16 * core + place, 8:16, :] = notes


def rows_kernel(inbox_ref, update_ref, state_ref, rows_ref, ratio_ref):
    notes = inbox_ref[0, 8:16, :]
    for source in range(1, 32):
        notes = notes + inbox_ref[source, 8:16, :]
    lane = lax.broadcasted_iota(jnp.int32, (8, 128), 1)
    weight_sq = jnp.sum(jnp.where(lane == 0, notes, 0.0), keepdims=True)
    update_sq = jnp.sum(jnp.where(lane == 1, notes, 0.0), keepdims=True)
    ratio = jnp.sqrt(weight_sq) / (jnp.sqrt(update_sq) + norm_eps)
    ratio_ref[...] = jnp.broadcast_to(ratio, (8, 128))
    for start in range(0, update_ref.shape[1], CHUNK):
        part = pl.ds(start, CHUNK)
        rows = (state_ref[2, :, part] - rate * ratio * update_ref[:, part]).astype(jnp.bfloat16)
        for place in range(16):
            rows_ref[place, :, part] = rows


def order_kernel(core_ref, mine_ref, other_ref, out_ref):
    mine = mine_ref[0].astype(jnp.float32)
    other = other_ref[0].astype(jnp.float32)
    at_first = core_ref[0] == 0
    both = [jnp.where(at_first, mine, other), jnp.where(at_first, other, mine)]
    out_ref[...] = jnp.concatenate(both, axis=0).astype(jnp.bfloat16)


def on_device(grads, basis, weights, moment, second):
    grad = grads[0, 0, 0]
    width = grad.shape[1]
    core = lax.axis_index("c")
    deep = lax.axis_index("z")
    low = lax.axis_index("yl")
    outer = lax.axis_index("yh") * 4 + lax.axis_index("x")
    core_at = core.astype(jnp.int32).reshape(1)

    turned = basis.T
    half = turned.shape[1] // 2
    mine = lax.dynamic_slice_in_dim(turned, half * core, half, 1)
    theirs = swap(lax.dynamic_slice_in_dim(turned, half * (1 - core), half, 1))
    chip = in_order(core, mine, theirs, 0).reshape(-1, half)
    part = chip.shape[0] // 8
    piece = lax.dynamic_slice_in_dim(chip, part * outer, part, 0)
    state = jnp.concatenate([moment, second, weights], axis=0).astype(jnp.bfloat16)
    state_z = lax.all_gather(state, "z")
    along_z = share(piece, "z", 16)
    other_grad = swap(grad)
    blocks = share(along_z, PLANE, 16).reshape(2, 8, 16, part, half)
    own_basis = blocks.transpose(0, 2, 1, 3, 4).reshape(width, half)
    other_basis = swap(own_basis)

    contract = (((1,), (0,)), ((), ()))
    sketch = lax.dot_general(grad, own_basis, contract, preferred_element_type=jnp.float32)
    sketch = sketch + lax.dot_general(
        other_grad, own_basis, contract, preferred_element_type=jnp.float32
    )
    plane_terms = exchange(sketch.reshape(16, 16, half), PLANE)
    plane_terms, state_z = lax.optimization_barrier((plane_terms, state_z))
    plane_sum = jnp.sum(plane_terms, axis=0)
    spread = jnp.broadcast_to(plane_sum.reshape(2, 1, 8, half), (2, 16, 8, half))
    terms = exchange(spread.reshape(32, 8, half), ("c", "z"))

    picked = lax.dynamic_index_in_dim(state_z, 2 * outer + core, 0, keepdims=False)
    passed = swap(lax.dynamic_index_in_dim(state_z, 2 * outer + 1 - core, 0, keepdims=False))
    state8 = in_order(core, picked, passed, 1).reshape(3, 8, width).astype(jnp.float32)
    update8, message = pl.pallas_call(
        update_kernel,
        out_shape=(
            jax.ShapeDtypeStruct((8, width), jnp.float32),
            jax.ShapeDtypeStruct((32, 16, half), jnp.float32),
        ),
        in_specs=[SMEM, VMEM, VMEM, VMEM, VMEM],
        out_specs=(VMEM, VMEM),
        compiler_params=LIMIT,
        name="update",
    )(core_at, terms, own_basis, other_basis, state8)
    inbox = exchange(message, ("c",) + PLANE)
    rows_out, ratio = pl.pallas_call(
        rows_kernel,
        out_shape=(
            jax.ShapeDtypeStruct((16, 8, width), jnp.bfloat16),
            jax.ShapeDtypeStruct((8, 128), jnp.float32),
        ),
        in_specs=[VMEM, VMEM, VMEM],
        out_specs=(VMEM, VMEM),
        compiler_params=LIMIT,
        name="rows",
    )(inbox, update8, state8)
    rows_mine = exchange(rows_out, PLANE)
    rows_other = swap(rows_mine)
    gathered = pl.pallas_call(
        order_kernel,
        grid=(16,),
        out_shape=jax.ShapeDtypeStruct((256, width), jnp.bfloat16),
        in_specs=[
            SMEM,
            pl.BlockSpec((1, 8, width), lambda i: (i, 0, 0)),
            pl.BlockSpec((1, 8, width), lambda i: (i, 0, 0)),
        ],
        out_specs=pl.BlockSpec((16, width), lambda i: (i, 0)),
        name="order",
    )(core_at, rows_mine, rows_other)[None]

    trust_ratio = ratio[0, 0]
    source = (deep % 2) * 16 + low * 8 + deep // 2
    own = lax.dynamic_index_in_dim(inbox, source, 0, keepdims=False)[:8]
    estimate = estimate_rows(own.reshape(2, 4, half), core, own_basis, other_basis, 3)[None]
    moment_new, second_new, update = moments(estimate, weights, moment, second)
    weight_new = weights - rate * trust_ratio * update
    return (weight_new, moment_new, second_new, gathered)


def solution(mesh):
    fine = Mesh(mesh.devices.reshape(tuple(FINE.values())), tuple(FINE))
    rows = P(None, DP, None)
    return jax.shard_map(
        on_device,
        mesh=fine,
        in_specs=(P(OUTER, DP, None, None, None), P(None, DP), rows, rows, rows),
        out_specs=(rows, rows, rows, P()),
        check_vma=False,
    )
```

time: 192 us -> 194 us (1.010)
  Pallas kernels: 0 us -> 11.5 us
  waiting for transfers between devices: 45.1 us -> 35 us
  local copies, waits for them, and re-layouts: 7.63 us -> 15.4 us
  other arithmetic: 12.7 us -> 5.68 us
  blocking collectives: 59.2 us -> 63.6 us
  starting transfers between devices: 44.4 us -> 41.5 us
    pallas_call x0 -> x3, Pallas kernels: none -> 11.5 us  [the longest x1 10.1 us: on_device(): pl.pallas_call(order_kernel, grid=(16,), out_shape=jax.ShapeDtypeStruct((...]
    all_to_all x3, waiting for transfers between devices: 42 us -> 31.5 us  [exchange(): return lax.all_to_all(blocks, axes, 0, 0, tiled=True)]
    broadcast_in_dim x3 -> x11, local copies, waits for them, and re-layouts: 0.68 us -> 6.99 us  [the longest x10 6.32 us: in_order(): jnp.where(here, jnp.expand_dims(mine, axis), jnp.expand_dims(other, axis))]
    all_to_all x3, starting transfers between devices: 20.5 us -> 14.3 us  [exchange(): return lax.all_to_all(blocks, axes, 0, 0, tiled=True)]
    all_to_all x3, blocking collectives: 59.2 us -> 63.6 us  [exchange(): return lax.all_to_all(blocks, axes, 0, 0, tiled=True)]
    another operation x2 -> x0, other arithmetic: 4.04 us -> none  [on_device(): gathered = jnp.stack(in_core_order(core, rows_mine, rows_other, 1), axis=1)]
    ppermute x5, starting transfers between devices: 23.8 us -> 27.2 us  [swap(): return lax.ppermute(block, 'c', SWAP)]
    unnamed x8 -> x14, local copies, waits for them, and re-layouts: 1.76 us -> 3.71 us
  transfers between devices with their start and end apart: 9 -> 9, of which waited for: 5 -> 5; matrix products, arithmetic and copies ran while one was open for 8% -> 10% of each run, Pallas kernels for 0% -> 0%
where the time goes in v2:
time: 194 us; the launch traced here: 193 us
  blocking collectives  63.6 us (33%)
  starting transfers between devices  41.5 us (21%)
  waiting for transfers between devices  35 us (18%)
  local copies, waits for them, and re-layouts  15.4 us (8%)
  between operations  15 us (8%)
  Pallas kernels  11.5 us (6%)
  other arithmetic  5.68 us (3%)
  matrix products  5.3 us (3%)
    all_to_all x3, blocking collectives, exchange(): return lax.all_to_all(blocks, axes, 0, 0, tiled=True)  63.6 us
    all_to_all x3, waiting for transfers between devices, exchange(): return lax.all_to_all(blocks, axes, 0, 0, tiled=True)  31.5 us
    ppermute x5, starting transfers between devices, swap(): return lax.ppermute(block, 'c', SWAP)  27.2 us
    all_to_all x3, starting transfers between devices, exchange(): return lax.all_to_all(blocks, axes, 0, 0, tiled=True)  14.3 us
    pallas_call x1, Pallas kernels, on_device(): pl.pallas_call(order_kernel, grid=(16,), out_shape=jax.ShapeDtypeStruct((...  10.1 us
    broadcast_in_dim x10, local copies, waits for them, and re-layouts, in_order(): jnp.where(here, jnp.expand_dims(mine, axis), jnp.expand_dims(other, axis))  6.32 us
  transfers between devices with their start and end apart: 9, of which 5 were waited for; matrix products, arithmetic and copies ran while one was open for 10% of the time, Pallas kernels for 0%

profile of v2, /device:TPU:1, one launch (start us, length us, event | category | flops | bytes accessed | tf_op | source)
XLA Modules:
  0.0 192.9 jit_solution(5199145000780265147)
XLA Ops:
  7.2 0.0 all-gather.2.cloned.1.call-start
  7.2 0.9 convert_bitcast_fusion.2
  8.1 1.0 convert_bitcast_fusion
  9.1 0.8 pad_maximum_fusion
  9.9 0.0 all-gather.2.cloned.1.call-update
  9.9 8.8 %collective-permute-start.1 = (bf16[256,6144]{1,0:T(8,128)(2,1)}, bf16[256,6144]{1,0:T(8,128)(2,1)}, u32[]{:S(2)}, u32[]{:S(2)}) collective-permute-start(bf16[256,6144]{1,0:T(8,128)(2,1)} %bitcast.65), channel_id=1, source_target_pairs={{0,1},{1,0},{2,3},{3,2},{4,5},{5,4},{6,7},{7,6},{8,9},{9,8},{10,11... | collective-permute-start | bytes 9437192 | tf_op jit(solution)/shard_map/ppermute | solution.py:34
  18.7 0.8 dynamic-slice_bitcast_fusion.3
  19.5 1.9 collective-permute-start
  21.4 0.1 broadcast_in_dim.93
  21.5 0.1 broadcast_in_dim.94
  21.6 0.1 dynamic-slice.8
  21.7 2.3 %collective-permute-done = bf16[96,128]{1,0:T(8,128)(2,1)S(1)} collective-permute-done((bf16[96,128]{1,0:T(8,128)(2,1)S(1)}, bf16[96,128]{1,0:T(8,128)(2,1)S(1)}, u32[]{:S(2)}, u32[]{:S(2)}) %collective-permute-start) | collective-permute-done | bytes 24608 | tf_op jit(solution)/shard_map/ppermute | solution.py:34
  24.0 0.1 dynamic-slice_select_fusion
  24.1 21.3 %all_to_all.30 = bf16[16,24,128]{2,1,0:T(8,128)(2,1)S(1)} all-to-all(bf16[16,24,128]{2,1,0:T(8,128)(2,1)S(1)} %broadcast_in_dim.100), channel_id=1, replica_groups=mesh['yh'=2,'x'=4,'yl'=2,'z'=16,'c'=2] {'z'}, dimensions={0} | all-to-all | bytes 196608 | tf_op jit(solution)/shard_map/all_to_all | solution.py:26
  45.4 0.3 broadcast_in_dim.101
  45.7 26.9 %all_to_all.31 = bf16[16,16,24,128]{3,2,1,0:T(8,128)(2,1)S(1)} all-to-all(bf16[16,16,24,128]{3,2,1,0:T(8,128)(2,1)S(1)} %broadcast_in_dim.101), channel_id=1, replica_groups=mesh['yh'=2,'x'=4,'yl'=2,'z'=16,'c'=2] {'yl','yh','x'}, dimensions={0} | all-to-all | bytes 3145728 | tf_op jit(solution)/shard_map/all_to_all | solution.py:26
  72.7 0.0 copy-start.3
  72.7 0.4 copy.11
  73.1 1.5 copy-done.3
  74.6 1.2 fusion.20
  75.8 0.0 collective-permute-done.1
  75.8 3.1 %fusion = f32[256,128]{0,1:T(8,128)S(1)} fusion(f32[128,256]{1,0:T(8,128)S(1)} %fusion.20, bf16[6144,128]{1,0:T(8,128)(2,1)S(1)} %bitcast.60, bf16[256,6144]{1,0:T(8,128)(2,1)} %collective-permute-done.1), kind=kOutput, calls=%fused_computation.2 | convolution fusion | flops 402685952 | bytes 4980736 | tf_op jit(solution)/shard_map/dot_general | solution.py:174
  78.9 0.8 copy.12
  79.6 3.5 %all-to-all-start.2 = ((f32[16,16,128]{2,1,0:T(8,128)}), f32[16,16,128]{2,1,0:T(8,128)S(1)}, u32[]{:S(2)}, u32[]{:S(2)}) async-start(f32[16,16,128]{2,1,0:T(8,128)} %bitcast.10), calls=%async_computation.2 | async-start | bytes 262144 | tf_op jit(solution)/shard_map/all_to_all | solution.py:26
  83.2 5.4 %collective-permute-start.2 = (bf16[6144,128]{1,0:T(8,128)(2,1)S(1)}, bf16[6144,128]{1,0:T(8,128)(2,1)S(1)}, u32[]{:S(2)}, u32[]{:S(2)}) collective-permute-start(bf16[6144,128]{1,0:T(8,128)(2,1)S(1)} %bitcast.61), channel_id=1, source_target_pairs={{0,1},{1,0},{2,3},{3,2},{4,5},{5,4},{6,7},{7,6},{8,9},{9,8},{10,11... | collective-permute-start | bytes 4718600 | tf_op jit(solution)/shard_map/ppermute | solution.py:34
  88.6 1.4 all-to-all-done.2
  90.0 1.7 dynamic-slice_bitcast_fusion
  91.7 6.5 %collective-permute-start.3 = (bf16[3,4,6144]{2,1,0:T(4,128)(2,1)}, bf16[3,4,6144]{2,1,0:T(4,128)(2,1)}, u32[]{:S(2)}, u32[]{:S(2)}) collective-permute-start(bf16[3,4,6144]{2,1,0:T(4,128)(2,1)} %get-tuple-element.19), channel_id=1, source_target_pairs={{0,1},{1,0},{2,3},{3,2},{4,5},{5,4},{6,7},{7,6},{8,9},{9,8},{10,11... | collective-permute-start | bytes 442376 | tf_op jit(solution)/shard_map/ppermute | solution.py:34
  98.2 0.1 broadcast_in_dim.104
  98.3 0.1 broadcast_in_dim.105
  98.4 0.7 broadcast_in_dim.103
  99.1 6.4 %all-to-all-start.3 = ((f32[32,8,128]{2,1,0:T(8,128)}), f32[32,8,128]{2,1,0:T(8,128)S(1)}, u32[]{:S(2)}, u32[]{:S(2)}) async-start(f32[32,8,128]{2,1,0:T(8,128)} %bitcast.15), calls=%async_computation.3 | async-start | bytes 262144 | tf_op jit(solution)/shard_map/all_to_all | solution.py:26
  105.5 0.8 broadcast_in_dim.108
  106.3 1.8 broadcast_in_dim.109
  108.0 0.0 collective-permute-done.3
  108.0 1.7 broadcast_in_dim.110
  109.7 1.7 broadcast_in_dim.111
  111.5 2.0 %select_convert_fusion.state_ref = f32[3,8,6144]{2,1,0:T(8,128)} fusion(bf16[3,8,6144]{2,1,0:T(8,128)(2,1)} %broadcast_in_dim.109, bf16[3,8,6144]{2,1,0:T(8,128)(2,1)} %broadcast_in_dim.111, pred[8]{0:T(512)(128)(4,1)S(1)} %broadcast_in_dim.105), kind=kLoop, calls=%fused_computation.3 | loop fusion | flops 294912 | bytes 1179656 | tf_op jit(solution)/shard_map/convert_element_type | solution.py:185
  113.5 0.0 collective-permute-done.2.other_ref
  113.5 8.4 %all-to-all-done.3.terms_ref = f32[32,8,128]{2,1,0:T(8,128)S(1)} async-done(((f32[32,8,128]{2,1,0:T(8,128)}), f32[32,8,128]{2,1,0:T(8,128)S(1)}, u32[]{:S(2)}, u32[]{:S(2)}) %all-to-all-start.3) | async-done | bytes 131104 | tf_op jit(solution)/shard_map/all_to_all | solution.py:26
  121.9 1.1 copy-done
  122.9 1.1 update.1
  124.0 15.3 %all_to_all.32.inbox_ref = f32[32,16,128]{2,1,0:T(8,128)S(1)} all-to-all(f32[32,16,128]{2,1,0:T(8,128)S(1)} %get-tuple-element.12), channel_id=1, replica_groups=mesh['yh'=2,'x'=4,'yl'=2,'z'=16,'c'=2] {'c','yl','yh','x'}, dimensions={0} | all-to-all | bytes 524288 | tf_op jit(solution)/shard_map/all_to_all | solution.py:26
  139.4 0.0 copy-done.1
  139.4 0.3 rows.1
  139.7 0.0 copy-start.2
  139.7 1.1 copy-done.2
  140.8 4.4 %all-to-all-start.5 = ((bf16[16,8,6144]{2,1,0:T(8,128)(2,1)}), bf16[16,8,6144]{2,1,0:T(8,128)(2,1)}, u32[]{:S(2)}, u32[]{:S(2)}) async-start(bf16[16,8,6144]{2,1,0:T(8,128)(2,1)} %copy-done.2), calls=%async_computation.5 | async-start | bytes 3145728 | tf_op jit(solution)/shard_map/all_to_all | solution.py:26
  145.3 0.5 slice.7
  145.8 0.5 fusion.1
  146.3 21.7 %all-to-all-done.5.mine_ref = bf16[16,8,6144]{2,1,0:T(8,128)(2,1)} async-done(((bf16[16,8,6144]{2,1,0:T(8,128)(2,1)}), bf16[16,8,6144]{2,1,0:T(8,128)(2,1)}, u32[]{:S(2)}, u32[]{:S(2)}) %all-to-all-start.5) | async-done | bytes 1572896 | tf_op jit(solution)/shard_map/all_to_all | solution.py:26
  168.0 4.6 %collective-permute-start.4 = (bf16[16,8,6144]{2,1,0:T(8,128)(2,1)}, bf16[16,8,6144]{2,1,0:T(8,128)(2,1)}, u32[]{:S(2)}, u32[]{:S(2)}) collective-permute-start(bf16[16,8,6144]{2,1,0:T(8,128)(2,1)} %all-to-all-done.5.mine_ref), channel_id=1, source_target_pairs={{0,1},{1,0},{2,3},{3,2},{4,5},{5,4},{6,7},{7,6},{8,9},{9,8},{10,11... | collective-permute-start | bytes 4718600 | tf_op jit(solution)/shard_map/ppermute | solution.py:34
  172.6 0.0 copy-start.4
  172.6 0.0 copy-start.5
  172.6 0.0 copy-start.6
  172.7 0.5 convolution_add_fusion
  173.2 0.1 reshape.141
  173.3 0.1 reduce_sum.19
  174.0 0.0 copy-done.4
  174.0 0.0 copy-done.5
  174.0 0.0 copy-done.6
  174.0 0.8 multiply_subtract_fusion
  174.9 1.1 collective-permute-done.4.other_ref
  176.0 10.1 %order.1 = bf16[256,6144]{1,0:T(8,128)(2,1)} custom-call(s32[1]{0:T(128)} %bitcast.core_ref, bf16[16,8,6144]{2,1,0:T(8,128)(2,1)} %all-to-all-done.5.mine_ref, bf16[16,8,6144]{2,1,0:T(8,128)(2,1)} %collective-permute-done.4.other_ref), custom_call_target="tpu_custom_call" | custom-call | tf_op jit(solution)/shard_map/order/pallas_call | solution.py:211
  (10 shorter events, 0.1 us)
Async XLA Ops:
  7.2 82.8 %all-gather.2.cloned.1.call-start = ((), (), s32[]{:S(2)}) async-start(), calls=%async_computation.6 | async-start | bytes 2506752 | tf_op jit(solution)/shard_map/all_gather | solution.py:165
  9.9 65.9 %collective-permute-start.1 = (bf16[256,6144]{1,0:T(8,128)(2,1)}, bf16[256,6144]{1,0:T(8,128)(2,1)}, u32[]{:S(2)}, u32[]{:S(2)}) collective-permute-start(bf16[256,6144]{1,0:T(8,128)(2,1)} %bitcast.65), channel_id=1, source_target_pairs={{0,1},{1,0},{2,3},{3,2},{4,5},{5,4},{6,7},{7,6},{8,9},{9,8},{10,11... | collective-permute-start | bytes 9437192 | tf_op jit(solution)/shard_map/ppermute | solution.py:34
  19.5 4.5 %collective-permute-start = (bf16[96,128]{1,0:T(8,128)(2,1)S(1)}, bf16[96,128]{1,0:T(8,128)(2,1)S(1)}, u32[]{:S(2)}, u32[]{:S(2)}) collective-permute-start(bf16[96,128]{1,0:T(8,128)(2,1)S(1)} %get-tuple-element.22), channel_id=1, source_target_pairs={{0,1},{1,0},{2,3},{3,2},{4,5},{5,4},{6,7},{7,6},{8,9},{9,8},{10,11... | collective-permute-start | bytes 73736 | tf_op jit(solution)/shard_map/ppermute | solution.py:34
  72.7 1.9 copy-start.3
  79.6 10.3 %all-to-all-start.2 = ((f32[16,16,128]{2,1,0:T(8,128)}), f32[16,16,128]{2,1,0:T(8,128)S(1)}, u32[]{:S(2)}, u32[]{:S(2)}) async-start(f32[16,16,128]{2,1,0:T(8,128)} %bitcast.10), calls=%async_computation.2 | async-start | bytes 262144 | tf_op jit(solution)/shard_map/all_to_all | solution.py:26
  83.2 30.3 %collective-permute-start.2 = (bf16[6144,128]{1,0:T(8,128)(2,1)S(1)}, bf16[6144,128]{1,0:T(8,128)(2,1)S(1)}, u32[]{:S(2)}, u32[]{:S(2)}) collective-permute-start(bf16[6144,128]{1,0:T(8,128)(2,1)S(1)} %bitcast.61), channel_id=1, source_target_pairs={{0,1},{1,0},{2,3},{3,2},{4,5},{5,4},{6,7},{7,6},{8,9},{9,8},{10,11... | collective-permute-start | bytes 4718600 | tf_op jit(solution)/shard_map/ppermute | solution.py:34
  91.7 16.3 %collective-permute-start.3 = (bf16[3,4,6144]{2,1,0:T(4,128)(2,1)}, bf16[3,4,6144]{2,1,0:T(4,128)(2,1)}, u32[]{:S(2)}, u32[]{:S(2)}) collective-permute-start(bf16[3,4,6144]{2,1,0:T(4,128)(2,1)} %get-tuple-element.19), channel_id=1, source_target_pairs={{0,1},{1,0},{2,3},{3,2},{4,5},{5,4},{6,7},{7,6},{8,9},{9,8},{10,11... | collective-permute-start | bytes 442376 | tf_op jit(solution)/shard_map/ppermute | solution.py:34
  99.1 22.8 %all-to-all-start.3 = ((f32[32,8,128]{2,1,0:T(8,128)}), f32[32,8,128]{2,1,0:T(8,128)S(1)}, u32[]{:S(2)}, u32[]{:S(2)}) async-start(f32[32,8,128]{2,1,0:T(8,128)} %bitcast.15), calls=%async_computation.3 | async-start | bytes 262144 | tf_op jit(solution)/shard_map/all_to_all | solution.py:26
  121.9 1.1 copy-start
  122.9 16.4 %copy-start.1 = (f32[3,8,6144]{2,1,0:T(8,128)S(1)}, f32[3,8,6144]{2,1,0:T(8,128)}, u32[]{:S(2)}) copy-start(f32[3,8,6144]{2,1,0:T(8,128)} %select_convert_fusion.state_ref) | copy-start | bytes 1769476
  139.7 1.1 copy-start.2
  140.8 27.2 %all-to-all-start.5 = ((bf16[16,8,6144]{2,1,0:T(8,128)(2,1)}), bf16[16,8,6144]{2,1,0:T(8,128)(2,1)}, u32[]{:S(2)}, u32[]{:S(2)}) async-start(bf16[16,8,6144]{2,1,0:T(8,128)(2,1)} %copy-done.2), calls=%async_computation.5 | async-start | bytes 3145728 | tf_op jit(solution)/shard_map/all_to_all | solution.py:26
  168.0 8.0 %collective-permute-start.4 = (bf16[16,8,6144]{2,1,0:T(8,128)(2,1)}, bf16[16,8,6144]{2,1,0:T(8,128)(2,1)}, u32[]{:S(2)}, u32[]{:S(2)}) collective-permute-start(bf16[16,8,6144]{2,1,0:T(8,128)(2,1)} %all-to-all-done.5.mine_ref), channel_id=1, source_target_pairs={{0,1},{1,0},{2,3},{3,2},{4,5},{5,4},{6,7},{7,6},{8,9},{9,8},{10,11... | collective-permute-start | bytes 4718600 | tf_op jit(solution)/shard_map/ppermute | solution.py:34
  172.6 1.4 copy-start.4
  172.6 1.4 copy-start.5
  172.6 1.4 copy-start.6
Sparse Core Ops, SparseCore 0:
  10.7 73.4 all-gather.1

commit v3 on v2

--- a/solution.py
+++ b/solution.py
@@ -20,6 +20,21 @@
 DP = ("yl", "z", "c")
 PLANE = ("yl", "yh", "x")
 SWAP = [(0, 1), (1, 0)]
+ALL = tuple(FINE)
+
+
+def flat(outer, low, deep, core):
+    return ((outer * 2 + low) * 16 + deep) * 2 + core
+
+
+def state_moves(other):
+    return [
+        (flat(o, low, z, c), flat(z // 2, low, 2 * o + (1 - c if other else c), z % 2))
+        for o in range(8)
+        for low in range(2)
+        for z in range(16)
+        for c in range(2)
+    ]
 
 
 def exchange(blocks, axes):
@@ -117,8 +132,8 @@
         rows = slice(4 * core, 4 * core + 4)
         sent = jnp.concatenate([first[rows], second[rows]], axis=0)
         for place in range(16):
-            message_ref[16 * core + place, 0:8, :] = sent
-            message_ref[16 * core + place, 8:16, :] = notes
+            message_ref[2 * place + core, 0:8, :] = sent
+            message_ref[2 * place + core, 8:16, :] = notes
 
 
 def rows_kernel(inbox_ref, update_ref, state_ref, rows_ref, ratio_ref):
@@ -137,12 +152,29 @@
             rows_ref[place, :, part] = rows
 
 
-def order_kernel(core_ref, mine_ref, other_ref, out_ref):
-    mine = mine_ref[0].astype(jnp.float32)
-    other = other_ref[0].astype(jnp.float32)
-    at_first = core_ref[0] == 0
-    both = [jnp.where(at_first, mine, other), jnp.where(at_first, other, mine)]
-    out_ref[...] = jnp.concatenate(both, axis=0).astype(jnp.bfloat16)
+def place_kernel(at_ref, rows_ref, *refs):
+    out_ref, sems = refs[-2:]
+    copies = [
+        pltpu.make_async_copy(rows_ref.at[i], out_ref.at[i, at_ref[0]], sems.at[i])
+        for i in range(16)
+    ]
+    for copy in copies:
+        copy.start()
+    for copy in copies:
+        copy.wait()
+
+
+def place(at, rows, *partly):
+    shape = (16, 2) + rows.shape[1:]
+    return pl.pallas_call(
+        place_kernel,
+        out_shape=jax.ShapeDtypeStruct(shape, rows.dtype),
+        in_specs=[SMEM, VMEM] + [pl.BlockSpec(memory_space=pl.ANY)] * len(partly),
+        out_specs=pl.BlockSpec(memory_space=pl.ANY),
+        scratch_shapes=[pltpu.SemaphoreType.DMA((16,))],
+        input_output_aliases={2: 0} if partly else {},
+        name="place",
+    )(at, rows, *partly)
 
 
 def on_device(grads, basis, weights, moment, second):
@@ -161,8 +193,6 @@
     chip = in_order(core, mine, theirs, 0).reshape(-1, half)
     part = chip.shape[0] // 8
     piece = lax.dynamic_slice_in_dim(chip, part * outer, part, 0)
-    state = jnp.concatenate([moment, second, weights], axis=0).astype(jnp.bfloat16)
-    state_z = lax.all_gather(state, "z")
     along_z = share(piece, "z", 16)
     other_grad = swap(grad)
     blocks = share(along_z, PLANE, 16).reshape(2, 8, 16, part, half)
@@ -174,15 +204,16 @@
     sketch = sketch + lax.dot_general(
         other_grad, own_basis, contract, preferred_element_type=jnp.float32
     )
+    sketch, m_in, v_in, w_in = lax.optimization_barrier((sketch, moment, second, weights))
     plane_terms = exchange(sketch.reshape(16, 16, half), PLANE)
-    plane_terms, state_z = lax.optimization_barrier((plane_terms, state_z))
     plane_sum = jnp.sum(plane_terms, axis=0)
     spread = jnp.broadcast_to(plane_sum.reshape(2, 1, 8, half), (2, 16, 8, half))
     terms = exchange(spread.reshape(32, 8, half), ("c", "z"))
 
-    picked = lax.dynamic_index_in_dim(state_z, 2 * outer + core, 0, keepdims=False)
-    passed = swap(lax.dynamic_index_in_dim(state_z, 2 * outer + 1 - core, 0, keepdims=False))
-    state8 = in_order(core, picked, passed, 1).reshape(3, 8, width).astype(jnp.float32)
+    state = jnp.stack([m_in[0], v_in[0], w_in[0]]).astype(jnp.bfloat16)
+    state_one = lax.ppermute(state, ALL, state_moves(False))
+    state_two = lax.ppermute(state, ALL, state_moves(True))
+    state8 = in_order(deep % 2, state_one, state_two, 1).reshape(3, 8, width).astype(jnp.float32)
     update8, message = pl.pallas_call(
         update_kernel,
         out_shape=(
@@ -194,7 +225,7 @@
         compiler_params=LIMIT,
         name="update",
     )(core_at, terms, own_basis, other_basis, state8)
-    inbox = exchange(message, ("c",) + PLANE)
+    inbox = exchange(message, PLANE + ("c",))
     rows_out, ratio = pl.pallas_call(
         rows_kernel,
         out_shape=(
@@ -208,22 +239,11 @@
     )(inbox, update8, state8)
     rows_mine = exchange(rows_out, PLANE)
     rows_other = swap(rows_mine)
-    gathered = pl.pallas_call(
-        order_kernel,
-        grid=(16,),
-        out_shape=jax.ShapeDtypeStruct((256, width), jnp.bfloat16),
-        in_specs=[
-            SMEM,
-            pl.BlockSpec((1, 8, width), lambda i: (i, 0, 0)),
-            pl.BlockSpec((1, 8, width), lambda i: (i, 0, 0)),
-        ],
-        out_specs=pl.BlockSpec((16, width), lambda i: (i, 0)),
-        name="order",
-    )(core_at, rows_mine, rows_other)[None]
+    gathered = place(1 - core_at, rows_other, place(core_at, rows_mine))
+    gathered = gathered.reshape(1, 256, width)
 
     trust_ratio = ratio[0, 0]
-    source = (deep % 2) * 16 + low * 8 + deep // 2
-    own = lax.dynamic_index_in_dim(inbox, source, 0, keepdims=False)[:8]
+    own = lax.dynamic_index_in_dim(inbox, low * 16 + deep, 0, keepdims=False)[:8]
     estimate = estimate_rows(own.reshape(2, 4, half), core, own_basis, other_basis, 3)[None]
     moment_new, second_new, update = moments(estimate, weights, moment, second)
     weight_new = weights - rate * trust_ratio * update

time: 194 us -> 197 us (1.015)
  between operations: 15 us -> 1.67 us
  waiting for transfers between devices: 35 us -> 48.2 us
  starting transfers between devices: 41.5 us -> 51.3 us
  Pallas kernels: 11.5 us -> 6.74 us
  blocking collectives: 63.6 us -> 66.9 us
  local copies, waits for them, and re-layouts: 15.4 us -> 12.2 us
    all_to_all x3, waiting for transfers between devices: 31.5 us -> 45.9 us  [exchange(): return lax.all_to_all(blocks, axes, 0, 0, tiled=True)]
    all_to_all x3, starting transfers between devices: 14.3 us -> 26 us  [exchange(): return lax.all_to_all(blocks, axes, 0, 0, tiled=True)]
    ppermute x5 -> x4, starting transfers between devices: 27.2 us -> 19.7 us  [swap(): return lax.ppermute(block, 'c', SWAP)]
    ppermute x0 -> x2, starting transfers between devices: none -> 5.54 us  [the longest x1 3.63 us: on_device(): state_one = lax.ppermute(state, ALL, state_moves(False))]
    pallas_call x1 -> x2, Pallas kernels: 10.1 us -> 5.35 us  [place(): pl.pallas_call(place_kernel, out_shape=jax.ShapeDtypeStruct(shape, rows.d...]
    all_to_all x3, blocking collectives: 63.6 us -> 66.9 us  [exchange(): return lax.all_to_all(blocks, axes, 0, 0, tiled=True)]
    concatenate x3 -> x0, other arithmetic: 2.67 us -> none  [on_device(): jnp.concatenate([moment, second, weights], axis=0).astype(jnp.bfloat16)]
  transfers between devices with their start and end apart: 9 -> 9, of which waited for: 5 -> 4; matrix products, arithmetic and copies ran while one was open for 10% -> 10% of each run, Pallas kernels for 0% -> 1%
where the time goes in v3:
time: 197 us; the launch traced here: 196 us
  blocking collectives  66.9 us (34%)
  starting transfers between devices  51.3 us (26%)
  waiting for transfers between devices  48.2 us (24%)
  local copies, waits for them, and re-layouts  12.2 us (6%)
  Pallas kernels  6.74 us (3%)
  matrix products  5.34 us (3%)
  other arithmetic  3.85 us (2%)
    all_to_all x3, blocking collectives, exchange(): return lax.all_to_all(blocks, axes, 0, 0, tiled=True)  66.9 us
    all_to_all x3, waiting for transfers between devices, exchange(): return lax.all_to_all(blocks, axes, 0, 0, tiled=True)  45.9 us
    all_to_all x3, starting transfers between devices, exchange(): return lax.all_to_all(blocks, axes, 0, 0, tiled=True)  26 us
    ppermute x4, starting transfers between devices, swap(): return lax.ppermute(block, 'c', SWAP)  19.7 us
    broadcast_in_dim x10, local copies, waits for them, and re-layouts, in_order(): jnp.where(here, jnp.expand_dims(mine, axis), jnp.expand_dims(other, axis))  6.32 us
    pallas_call x2, Pallas kernels, place(): pl.pallas_call(place_kernel, out_shape=jax.ShapeDtypeStruct(shape, rows.d...  5.35 us
  transfers between devices with their start and end apart: 9, of which 4 were waited for; matrix products, arithmetic and copies ran while one was open for 10% of the time, Pallas kernels for 1%

profile of v3, /device:TPU:1, one launch (start us, length us, event | category | flops | bytes accessed | tf_op | source)
XLA Modules:
  0.0 196.2 jit_solution(11417731442081952126)
XLA Ops:
  0.6 8.8 %collective-permute-start.1 = (bf16[256,6144]{1,0:T(8,128)(2,1)}, bf16[256,6144]{1,0:T(8,128)(2,1)}, u32[]{:S(2)}, u32[]{:S(2)}) collective-permute-start(bf16[256,6144]{1,0:T(8,128)(2,1)} %bitcast.54), channel_id=1, source_target_pairs={{0,1},{1,0},{2,3},{3,2},{4,5},{5,4},{6,7},{7,6},{8,9},{9,8},{10,11... | collective-permute-start | bytes 9437192 | tf_op jit(solution)/shard_map/ppermute | solution.py:49
  9.4 0.8 dynamic-slice_bitcast_fusion.1
  10.2 1.9 collective-permute-start
  12.1 0.1 broadcast_in_dim.88
  12.2 0.1 broadcast_in_dim.89
  12.3 0.1 dynamic-slice.8
  12.4 2.3 %collective-permute-done = bf16[96,128]{1,0:T(8,128)(2,1)S(1)} collective-permute-done((bf16[96,128]{1,0:T(8,128)(2,1)S(1)}, bf16[96,128]{1,0:T(8,128)(2,1)S(1)}, u32[]{:S(2)}, u32[]{:S(2)}) %collective-permute-start) | collective-permute-done | bytes 24608 | tf_op jit(solution)/shard_map/ppermute | solution.py:49
  14.7 0.1 dynamic-slice_select_fusion
  14.8 21.2 %all_to_all.30 = bf16[16,24,128]{2,1,0:T(8,128)(2,1)S(1)} all-to-all(bf16[16,24,128]{2,1,0:T(8,128)(2,1)S(1)} %broadcast_in_dim.95), channel_id=1, replica_groups=mesh['yh'=2,'x'=4,'yl'=2,'z'=16,'c'=2] {'z'}, dimensions={0} | all-to-all | bytes 196608 | tf_op jit(solution)/shard_map/all_to_all | solution.py:41
  36.1 0.3 broadcast_in_dim.96
  36.4 26.2 %all_to_all.31 = bf16[16,16,24,128]{3,2,1,0:T(8,128)(2,1)S(1)} all-to-all(bf16[16,16,24,128]{3,2,1,0:T(8,128)(2,1)S(1)} %broadcast_in_dim.96), channel_id=1, replica_groups=mesh['yh'=2,'x'=4,'yl'=2,'z'=16,'c'=2] {'yl','yh','x'}, dimensions={0} | all-to-all | bytes 3145728 | tf_op jit(solution)/shard_map/all_to_all | solution.py:41
  62.6 0.4 copy.10
  63.0 6.3 %collective-permute-start.2 = (bf16[6144,128]{1,0:T(8,128)(2,1)S(1)}, bf16[6144,128]{1,0:T(8,128)(2,1)S(1)}, u32[]{:S(2)}, u32[]{:S(2)}) collective-permute-start(bf16[6144,128]{1,0:T(8,128)(2,1)S(1)} %bitcast.47), channel_id=1, source_target_pairs={{0,1},{1,0},{2,3},{3,2},{4,5},{5,4},{6,7},{7,6},{8,9},{9,8},{10,11... | collective-permute-start | bytes 4718600 | tf_op jit(solution)/shard_map/ppermute | solution.py:49
  69.3 0.0 copy-done.3
  69.3 1.2 fusion.18
  70.5 0.0 copy-start.8
  70.5 0.0 copy-start.6
  70.5 0.0 copy-start.4
  70.5 0.0 collective-permute-done.1
  70.5 3.1 %fusion = f32[256,128]{0,1:T(8,128)S(1)} fusion(f32[128,256]{1,0:T(8,128)S(1)} %fusion.18, bf16[6144,128]{1,0:T(8,128)(2,1)S(1)} %bitcast.49, bf16[256,6144]{1,0:T(8,128)(2,1)} %collective-permute-done.1), kind=kOutput, calls=%fused_computation.2 | convolution fusion | flops 402685952 | bytes 4980736 | tf_op jit(solution)/shard_map/dot_general | solution.py:204
  73.7 0.0 copy-done.8
  73.8 0.8 pad_maximum_fusion
  74.5 1.9 collective-permute-start.4
  76.5 3.6 %collective-permute-start.3 = (bf16[3,4,6144]{2,1,0:T(4,128)(2,1)}, bf16[3,4,6144]{2,1,0:T(4,128)(2,1)S(1)}, u32[]{:S(2)}, u32[]{:S(2)}) collective-permute-start(bf16[3,4,6144]{2,1,0:T(4,128)(2,1)} %pad_maximum_fusion), channel_id=1, source_target_pairs={{0,0},{1,2},{2,1},{3,3},{4,64},{5,66},{6,65},{7,67},{8,128},{9,130... | collective-permute-start | bytes 442376 | tf_op jit(solution)/shard_map/ppermute | solution.py:214
  80.1 0.8 copy.11
  80.9 13.9 %all-to-all-start.2 = ((f32[16,16,128]{2,1,0:T(8,128)}), f32[16,16,128]{2,1,0:T(8,128)S(1)}, u32[]{:S(2)}, u32[]{:S(2)}) async-start(f32[16,16,128]{2,1,0:T(8,128)} %bitcast.10), calls=%async_computation.2 | async-start | bytes 262144 | tf_op jit(solution)/shard_map/all_to_all | solution.py:41
  94.7 0.1 broadcast_in_dim.99
  94.8 0.1 broadcast_in_dim.100
  94.9 6.7 %all-to-all-done.2 = f32[16,16,128]{2,1,0:T(8,128)S(1)} async-done(((f32[16,16,128]{2,1,0:T(8,128)}), f32[16,16,128]{2,1,0:T(8,128)S(1)}, u32[]{:S(2)}, u32[]{:S(2)}) %all-to-all-start.2) | async-done | bytes 131104 | tf_op jit(solution)/shard_map/all_to_all | solution.py:41
  101.6 0.7 broadcast_in_dim.98
  102.2 7.8 %all-to-all-start.3 = ((f32[32,8,128]{2,1,0:T(8,128)}), f32[32,8,128]{2,1,0:T(8,128)S(1)}, u32[]{:S(2)}, u32[]{:S(2)}) async-start(f32[32,8,128]{2,1,0:T(8,128)} %bitcast.12), calls=%async_computation.3 | async-start | bytes 262144 | tf_op jit(solution)/shard_map/all_to_all | solution.py:41
  110.0 0.0 collective-permute-done.4
  110.0 1.7 broadcast_in_dim.104
  111.8 1.7 broadcast_in_dim.105
  113.5 0.0 collective-permute-done.3
  113.5 0.8 broadcast_in_dim.102
  114.3 1.7 broadcast_in_dim.103
  116.0 2.0 %select_convert_fusion.state_ref = f32[3,8,6144]{2,1,0:T(8,128)} fusion(bf16[3,8,6144]{2,1,0:T(8,128)(2,1)} %broadcast_in_dim.103, bf16[3,8,6144]{2,1,0:T(8,128)(2,1)} %broadcast_in_dim.105, pred[8]{0:T(512)(128)(4,1)S(1)} %broadcast_in_dim.100), kind=kLoop, calls=%fused_computation.3 | loop fusion | flops 294912 | bytes 1179656 | tf_op jit(solution)/shard_map/convert_element_type | solution.py:216
  118.0 0.0 collective-permute-done.2.other_ref
  118.0 13.1 %all-to-all-done.3.terms_ref = f32[32,8,128]{2,1,0:T(8,128)S(1)} async-done(((f32[32,8,128]{2,1,0:T(8,128)}), f32[32,8,128]{2,1,0:T(8,128)S(1)}, u32[]{:S(2)}, u32[]{:S(2)}) %all-to-all-start.3) | async-done | bytes 131104 | tf_op jit(solution)/shard_map/all_to_all | solution.py:41
  131.1 1.1 copy-done
  132.2 1.1 update.1
  133.3 19.4 %all_to_all.32.inbox_ref = f32[32,16,128]{2,1,0:T(8,128)S(1)} all-to-all(f32[32,16,128]{2,1,0:T(8,128)S(1)} %get-tuple-element.16), channel_id=1, replica_groups=mesh['yh'=2,'x'=4,'yl'=2,'z'=16,'c'=2] {'yl','yh','x','c'}, dimensions={0} | all-to-all | bytes 524288 | tf_op jit(solution)/shard_map/all_to_all | solution.py:41
  152.7 0.3 rows.1
  153.0 0.0 copy-start.2
  153.0 1.1 copy-done.2
  154.2 4.4 %all-to-all-start.5 = ((bf16[16,8,6144]{2,1,0:T(8,128)(2,1)}), bf16[16,8,6144]{2,1,0:T(8,128)(2,1)}, u32[]{:S(2)}, u32[]{:S(2)}) async-start(bf16[16,8,6144]{2,1,0:T(8,128)(2,1)} %copy-done.2), calls=%async_computation.5 | async-start | bytes 3145728 | tf_op jit(solution)/shard_map/all_to_all | solution.py:41
  158.6 0.5 fusion.1
  159.2 26.1 %all-to-all-done.5.rows_ref = bf16[16,8,6144]{2,1,0:T(8,128)(2,1)} async-done(((bf16[16,8,6144]{2,1,0:T(8,128)(2,1)}), bf16[16,8,6144]{2,1,0:T(8,128)(2,1)}, u32[]{:S(2)}, u32[]{:S(2)}) %all-to-all-start.5) | async-done | bytes 1572896 | tf_op jit(solution)/shard_map/all_to_all | solution.py:41
  185.3 2.8 %collective-permute-start.5 = (bf16[16,8,6144]{2,1,0:T(8,128)(2,1)}, bf16[16,8,6144]{2,1,0:T(8,128)(2,1)}, u32[]{:S(2)}, u32[]{:S(2)}) collective-permute-start(bf16[16,8,6144]{2,1,0:T(8,128)(2,1)} %all-to-all-done.5.rows_ref), channel_id=1, source_target_pairs={{0,1},{1,0},{2,3},{3,2},{4,5},{5,4},{6,7},{7,6},{8,9},{9,8},{10,11... | collective-permute-start | bytes 4718600 | tf_op jit(solution)/shard_map/ppermute | solution.py:49
  188.1 0.0 copy-start.5
  188.1 0.0 copy-start.7
  188.1 0.0 copy-start.9
  188.1 0.5 convolution_add_fusion
  188.6 0.1 reshape.98
  188.7 0.1 reduce_sum.19
  188.8 0.5 slice.7
  190.0 0.0 copy-done.5
  190.0 0.0 copy-done.7
  190.0 0.0 copy-done.9
  190.0 0.8 multiply_subtract_fusion
  190.8 2.7 %place.2.refs_0_ = bf16[16,2,8,6144]{3,2,1,0:T(8,128)(2,1)} custom-call(s32[1]{0:T(128)} %bitcast.core_ref.at_ref, bf16[16,8,6144]{2,1,0:T(8,128)(2,1)} %all-to-all-done.5.rows_ref), custom_call_target="tpu_custom_call" | custom-call | tf_op jit(solution)/shard_map/place/pallas_call | solution.py:169
  193.5 0.0 collective-permute-done.5.rows_ref
  193.5 2.7 %place.3 = bf16[16,2,8,6144]{3,2,1,0:T(8,128)(2,1)} custom-call(s32[1]{0:T(128)S(6)} %sub.28.at_ref, bf16[16,8,6144]{2,1,0:T(8,128)(2,1)} %collective-permute-done.5.rows_ref, bf16[16,2,8,6144]{3,2,1,0:T(8,128)(2,1)} %place.2.refs_0_), custom_call_target="tpu_custom_call", output_to_operand_aliasing={{}: (2, {})} | custom-call | tf_op jit(solution)/shard_map/place/pallas_call | solution.py:169
  (17 shorter events, 0.2 us)
Async XLA Ops:
  0.6 69.9 %collective-permute-start.1 = (bf16[256,6144]{1,0:T(8,128)(2,1)}, bf16[256,6144]{1,0:T(8,128)(2,1)}, u32[]{:S(2)}, u32[]{:S(2)}) collective-permute-start(bf16[256,6144]{1,0:T(8,128)(2,1)} %bitcast.54), channel_id=1, source_target_pairs={{0,1},{1,0},{2,3},{3,2},{4,5},{5,4},{6,7},{7,6},{8,9},{9,8},{10,11... | collective-permute-start | bytes 9437192 | tf_op jit(solution)/shard_map/ppermute | solution.py:49
  10.2 4.5 %collective-permute-start = (bf16[96,128]{1,0:T(8,128)(2,1)S(1)}, bf16[96,128]{1,0:T(8,128)(2,1)S(1)}, u32[]{:S(2)}, u32[]{:S(2)}) collective-permute-start(bf16[96,128]{1,0:T(8,128)(2,1)S(1)} %get-tuple-element.24), channel_id=1, source_target_pairs={{0,1},{1,0},{2,3},{3,2},{4,5},{5,4},{6,7},{7,6},{8,9},{9,8},{10,11... | collective-permute-start | bytes 73736 | tf_op jit(solution)/shard_map/ppermute | solution.py:49
  62.6 6.7 %copy-start.3 = (bf16[1,1,1,256,6144]{4,3,2,1,0:T(8,128)(2,1)S(1)}, bf16[1,1,1,256,6144]{4,3,2,1,0:T(8,128)(2,1)}, u32[]{:S(2)}) copy-start(bf16[1,1,1,256,6144]{4,3,2,1,0:T(8,128)(2,1)} %param.5) | copy-start | bytes 9437188
  63.0 55.0 %collective-permute-start.2 = (bf16[6144,128]{1,0:T(8,128)(2,1)S(1)}, bf16[6144,128]{1,0:T(8,128)(2,1)S(1)}, u32[]{:S(2)}, u32[]{:S(2)}) collective-permute-start(bf16[6144,128]{1,0:T(8,128)(2,1)S(1)} %bitcast.47), channel_id=1, source_target_pairs={{0,1},{1,0},{2,3},{3,2},{4,5},{5,4},{6,7},{7,6},{8,9},{9,8},{10,11... | collective-permute-start | bytes 4718600 | tf_op jit(solution)/shard_map/ppermute | solution.py:49
  70.5 3.2 %copy-start.8 = (f32[1,4,6144]{2,1,0:T(4,128)S(1)}, f32[1,4,6144]{2,1,0:T(4,128)}, u32[]{:S(2)}) copy-start(f32[1,4,6144]{2,1,0:T(4,128)} %param.8) | copy-start | bytes 294916
  70.5 3.2 %copy-start.6 = (f32[1,4,6144]{2,1,0:T(4,128)S(1)}, f32[1,4,6144]{2,1,0:T(4,128)}, u32[]{:S(2)}) copy-start(f32[1,4,6144]{2,1,0:T(4,128)} %param.9) | copy-start | bytes 294916
  70.5 3.2 %copy-start.4 = (f32[1,4,6144]{2,1,0:T(4,128)S(1)}, f32[1,4,6144]{2,1,0:T(4,128)}, u32[]{:S(2)}) copy-start(f32[1,4,6144]{2,1,0:T(4,128)} %param.7) | copy-start | bytes 294916
  74.5 35.5 %collective-permute-start.4 = (bf16[3,4,6144]{2,1,0:T(4,128)(2,1)}, bf16[3,4,6144]{2,1,0:T(4,128)(2,1)}, u32[]{:S(2)}, u32[]{:S(2)}) collective-permute-start(bf16[3,4,6144]{2,1,0:T(4,128)(2,1)} %pad_maximum_fusion), channel_id=1, source_target_pairs={{0,2},{1,0},{2,3},{3,1},{4,66},{5,64},{6,67},{7,65},{8,130},{9,128... | collective-permute-start | bytes 442376 | tf_op jit(solution)/shard_map/ppermute | solution.py:215
  76.5 37.0 %collective-permute-start.3 = (bf16[3,4,6144]{2,1,0:T(4,128)(2,1)}, bf16[3,4,6144]{2,1,0:T(4,128)(2,1)S(1)}, u32[]{:S(2)}, u32[]{:S(2)}) collective-permute-start(bf16[3,4,6144]{2,1,0:T(4,128)(2,1)} %pad_maximum_fusion), channel_id=1, source_target_pairs={{0,0},{1,2},{2,1},{3,3},{4,64},{5,66},{6,65},{7,67},{8,128},{9,130... | collective-permute-start | bytes 442376 | tf_op jit(solution)/shard_map/ppermute | solution.py:214
  80.9 20.7 %all-to-all-start.2 = ((f32[16,16,128]{2,1,0:T(8,128)}), f32[16,16,128]{2,1,0:T(8,128)S(1)}, u32[]{:S(2)}, u32[]{:S(2)}) async-start(f32[16,16,128]{2,1,0:T(8,128)} %bitcast.10), calls=%async_computation.2 | async-start | bytes 262144 | tf_op jit(solution)/shard_map/all_to_all | solution.py:41
  102.2 28.9 %all-to-all-start.3 = ((f32[32,8,128]{2,1,0:T(8,128)}), f32[32,8,128]{2,1,0:T(8,128)S(1)}, u32[]{:S(2)}, u32[]{:S(2)}) async-start(f32[32,8,128]{2,1,0:T(8,128)} %bitcast.12), calls=%async_computation.3 | async-start | bytes 262144 | tf_op jit(solution)/shard_map/all_to_all | solution.py:41
  131.1 1.1 copy-start
  132.2 20.6 %copy-start.1 = (f32[3,8,6144]{2,1,0:T(8,128)S(1)}, f32[3,8,6144]{2,1,0:T(8,128)}, u32[]{:S(2)}) copy-start(f32[3,8,6144]{2,1,0:T(8,128)} %select_convert_fusion.state_ref) | copy-start | bytes 1769476
  153.0 1.1 copy-start.2
  154.2 31.1 %all-to-all-start.5 = ((bf16[16,8,6144]{2,1,0:T(8,128)(2,1)}), bf16[16,8,6144]{2,1,0:T(8,128)(2,1)}, u32[]{:S(2)}, u32[]{:S(2)}) async-start(bf16[16,8,6144]{2,1,0:T(8,128)(2,1)} %copy-done.2), calls=%async_computation.5 | async-start | bytes 3145728 | tf_op jit(solution)/shard_map/all_to_all | solution.py:41
  185.3 8.2 %collective-permute-start.5 = (bf16[16,8,6144]{2,1,0:T(8,128)(2,1)}, bf16[16,8,6144]{2,1,0:T(8,128)(2,1)}, u32[]{:S(2)}, u32[]{:S(2)}) collective-permute-start(bf16[16,8,6144]{2,1,0:T(8,128)(2,1)} %all-to-all-done.5.rows_ref), channel_id=1, source_target_pairs={{0,1},{1,0},{2,3},{3,2},{4,5},{5,4},{6,7},{7,6},{8,9},{9,8},{10,11... | collective-permute-start | bytes 4718600 | tf_op jit(solution)/shard_map/ppermute | solution.py:49
  188.1 1.9 copy-start.5
  188.1 1.9 copy-start.7
  188.1 1.9 copy-start.9

commit v4 on v3

--- a/solution.py
+++ b/solution.py
@@ -87,16 +87,30 @@
 
 VMEM = pl.BlockSpec(memory_space=pltpu.VMEM)
 SMEM = pl.BlockSpec(memory_space=pltpu.SMEM)
-LIMIT = pltpu.CompilerParams(vmem_limit_bytes=40 << 20)
+LIMIT = pltpu.CompilerParams(vmem_limit_bytes=12 << 20)
 CHUNK = 512
 
 
-def update_kernel(core_ref, terms_ref, own_ref, other_ref, state_ref, update_ref, message_ref):
+def pack_kernel(moment_ref, second_ref, weights_ref, out_ref):
+    rows = [moment_ref[0], second_ref[0], weights_ref[0]]
+    out_ref[...] = jnp.concatenate(rows, axis=0).astype(jnp.bfloat16)
+
+
+def product_kernel(grad_ref, other_ref, basis_ref, out_ref):
+    basis = basis_ref[...]
+    total = jnp.dot(grad_ref[...], basis, preferred_element_type=jnp.float32)
+    out_ref[...] = total + jnp.dot(other_ref[...], basis, preferred_element_type=jnp.float32)
+
+
+def update_kernel(
+    at_ref, terms_ref, own_ref, other_ref, one_ref, two_ref, update_ref, kept_ref, message_ref
+):
     first, second = terms_ref[0], terms_ref[16]
     for step in range(1, 16):
         first = first + terms_ref[step]
         second = second + terms_ref[16 + step]
-    at_first = core_ref[0] == 0
+    at_first = at_ref[0] == 0
+    one_first = at_ref[1] == 0
 
     def left_of(half):
         high = half.astype(jnp.bfloat16).astype(jnp.float32)
@@ -114,11 +128,16 @@
         ) + lax.dot_general(
             left_other, other_ref[part, :], contract, preferred_element_type=jnp.float32
         )
-        weights = state_ref[2, :, part]
-        _, _, update = moments(
-            (both[:8] + both[8:]) / 256, weights, state_ref[0, :, part], state_ref[1, :, part]
-        )
+        one = one_ref[:, part].astype(jnp.float32)
+        two = two_ref[:, part].astype(jnp.float32)
+        upper = jnp.where(one_first, one, two)
+        lower = jnp.where(one_first, two, one)
+        moment, before, weights = [
+            jnp.concatenate([upper[r : r + 4], lower[r : r + 4]], axis=0) for r in (0, 4, 8)
+        ]
+        _, _, update = moments((both[:8] + both[8:]) / 256, weights, moment, before)
         update_ref[:, part] = update
+        kept_ref[:, part] = weights
         weight_sq = weight_sq + weights * weights
         update_sq = update_sq + update * update
     row = lax.broadcasted_iota(jnp.int32, (8, 128), 0)
@@ -136,7 +155,7 @@
             message_ref[2 * place + core, 8:16, :] = notes
 
 
-def rows_kernel(inbox_ref, update_ref, state_ref, rows_ref, ratio_ref):
+def rows_kernel(inbox_ref, update_ref, kept_ref, rows_ref, ratio_ref):
     notes = inbox_ref[0, 8:16, :]
     for source in range(1, 32):
         notes = notes + inbox_ref[source, 8:16, :]
@@ -147,7 +166,7 @@
     ratio_ref[...] = jnp.broadcast_to(ratio, (8, 128))
     for start in range(0, update_ref.shape[1], CHUNK):
         part = pl.ds(start, CHUNK)
-        rows = (state_ref[2, :, part] - rate * ratio * update_ref[:, part]).astype(jnp.bfloat16)
+        rows = (kept_ref[:, part] - rate * ratio * update_ref[:, part]).astype(jnp.bfloat16)
         for place in range(16):
             rows_ref[place, :, part] = rows
 
@@ -169,10 +188,11 @@
     return pl.pallas_call(
         place_kernel,
         out_shape=jax.ShapeDtypeStruct(shape, rows.dtype),
-        in_specs=[SMEM, VMEM] + [pl.BlockSpec(memory_space=pl.ANY)] * len(partly),
+        in_specs=[SMEM] + [pl.BlockSpec(memory_space=pl.ANY)] * (1 + len(partly)),
         out_specs=pl.BlockSpec(memory_space=pl.ANY),
         scratch_shapes=[pltpu.SemaphoreType.DMA((16,))],
         input_output_aliases={2: 0} if partly else {},
+        cost_estimate=pl.CostEstimate(flops=0, bytes_accessed=2 * rows.nbytes, transcendentals=0),
         name="place",
     )(at, rows, *partly)
 
@@ -194,37 +214,53 @@
     part = chip.shape[0] // 8
     piece = lax.dynamic_slice_in_dim(chip, part * outer, part, 0)
     along_z = share(piece, "z", 16)
+    along_z, m_in, v_in, w_in = lax.optimization_barrier((along_z, moment, second, weights))
+    state = pl.pallas_call(
+        pack_kernel,
+        out_shape=jax.ShapeDtypeStruct((12, width), jnp.bfloat16),
+        in_specs=[VMEM, VMEM, VMEM],
+        out_specs=VMEM,
+        name="pack",
+    )(m_in, v_in, w_in)
+    state_one = lax.ppermute(state, ALL, state_moves(False))
+    state_two = lax.ppermute(state, ALL, state_moves(True))
     other_grad = swap(grad)
-    blocks = share(along_z, PLANE, 16).reshape(2, 8, 16, part, half)
+    blocks = share(along_z, PLANE, 16)
+    blocks, state_one, state_two = lax.optimization_barrier((blocks, state_one, state_two))
+    blocks = blocks.reshape(2, 8, 16, part, half)
     own_basis = blocks.transpose(0, 2, 1, 3, 4).reshape(width, half)
-    other_basis = swap(own_basis)
-
-    contract = (((1,), (0,)), ((), ()))
-    sketch = lax.dot_general(grad, own_basis, contract, preferred_element_type=jnp.float32)
-    sketch = sketch + lax.dot_general(
-        other_grad, own_basis, contract, preferred_element_type=jnp.float32
-    )
-    sketch, m_in, v_in, w_in = lax.optimization_barrier((sketch, moment, second, weights))
+
+    sketch = pl.pallas_call(
+        product_kernel,
+        out_shape=jax.ShapeDtypeStruct((grad.shape[0], half), jnp.float32),
+        in_specs=[VMEM, VMEM, VMEM],
+        out_specs=VMEM,
+        compiler_params=LIMIT,
+        name="product",
+    )(grad, other_grad, own_basis)
+    sketch, basis_sent = lax.optimization_barrier((sketch, own_basis))
+    other_basis = swap(basis_sent)
     plane_terms = exchange(sketch.reshape(16, 16, half), PLANE)
     plane_sum = jnp.sum(plane_terms, axis=0)
     spread = jnp.broadcast_to(plane_sum.reshape(2, 1, 8, half), (2, 16, 8, half))
     terms = exchange(spread.reshape(32, 8, half), ("c", "z"))
 
-    state = jnp.stack([m_in[0], v_in[0], w_in[0]]).astype(jnp.bfloat16)
-    state_one = lax.ppermute(state, ALL, state_moves(False))
-    state_two = lax.ppermute(state, ALL, state_moves(True))
-    state8 = in_order(deep % 2, state_one, state_two, 1).reshape(3, 8, width).astype(jnp.float32)
-    update8, message = pl.pallas_call(
+    wide = jax.ShapeDtypeStruct((8, width), jnp.float32)
+    update8, kept8, message = pl.pallas_call(
         update_kernel,
-        out_shape=(
-            jax.ShapeDtypeStruct((8, width), jnp.float32),
-            jax.ShapeDtypeStruct((32, 16, half), jnp.float32),
-        ),
-        in_specs=[SMEM, VMEM, VMEM, VMEM, VMEM],
-        out_specs=(VMEM, VMEM),
+        out_shape=(wide, wide, jax.ShapeDtypeStruct((32, 16, half), jnp.float32)),
+        in_specs=[SMEM, VMEM, VMEM, VMEM, VMEM, VMEM],
+        out_specs=(VMEM, VMEM, VMEM),
         compiler_params=LIMIT,
         name="update",
-    )(core_at, terms, own_basis, other_basis, state8)
+    )(
+        jnp.stack([core, deep % 2]).astype(jnp.int32),
+        terms,
+        own_basis,
+        other_basis,
+        state_one,
+        state_two,
+    )
     inbox = exchange(message, PLANE + ("c",))
     rows_out, ratio = pl.pallas_call(
         rows_kernel,
@@ -236,10 +272,12 @@
         out_specs=(VMEM, VMEM),
         compiler_params=LIMIT,
         name="rows",
-    )(inbox, update8, state8)
+    )(inbox, update8, kept8)
     rows_mine = exchange(rows_out, PLANE)
     rows_other = swap(rows_mine)
-    gathered = place(1 - core_at, rows_other, place(core_at, rows_mine))
+    partly = place(core_at, rows_mine)
+    partly, inbox, ratio = lax.optimization_barrier((partly, inbox, ratio))
+    gathered = place(1 - core_at, rows_other, partly)
     gathered = gathered.reshape(1, 256, width)
 
     trust_ratio = ratio[0, 0]

time: 197 us -> 314 us (1.59)
  Pallas kernels: 6.74 us -> 105 us
  blocking collectives: 66.9 us -> 94.3 us
  waiting for transfers between devices: 48.2 us -> 55.5 us
  starting transfers between devices: 51.3 us -> 44.3 us
  matrix products: 5.34 us -> 1.02 us
    pallas_call x2, Pallas kernels: 5.35 us -> 97.8 us  [place(): pl.pallas_call(place_kernel, out_shape=jax.ShapeDtypeStruct(shape, rows.d...]
    all_to_all x3, blocking collectives: 66.9 us -> 94.3 us  [exchange(): return lax.all_to_all(blocks, axes, 0, 0, tiled=True)]
    all_to_all x3, starting transfers between devices: 26 us -> 16.6 us  [exchange(): return lax.all_to_all(blocks, axes, 0, 0, tiled=True)]
    broadcast_in_dim x10 -> x4, local copies, waits for them, and re-layouts: 6.32 us -> 0.17 us  [in_order(): jnp.where(here, jnp.expand_dims(mine, axis), jnp.expand_dims(other, axis))]
    pallas_call x1 -> x3, Pallas kernels: 1.09 us -> 7.01 us  [the longest x1 3.68 us: on_device(): pl.pallas_call(product_kernel, out_shape=jax.ShapeDtypeStruct((grad.shape...]
    dot_general x2 -> x0, matrix products: 4.32 us -> none  [the longest x1 3.12 us: on_device(): lax.dot_general(other_grad, own_basis, contract, preferred_element_type=j...]
    ppermute x1, waiting for transfers between devices: 0.01 us -> 3.41 us  [on_device(): state_one = lax.ppermute(state, ALL, state_moves(False))]
    ppermute x1, waiting for transfers between devices: 0.01 us -> 3.36 us  [on_device(): state_two = lax.ppermute(state, ALL, state_moves(True))]
  transfers between devices with their start and end apart: 9 -> 9, of which waited for: 4 -> 6; matrix products, arithmetic and copies ran while one was open for 10% -> 2% of each run, Pallas kernels for 1% -> 1%
where the time goes in v4:
time: 314 us; the launch traced here: 313 us
  Pallas kernels  105 us (33%)
  blocking collectives  94.3 us (30%)
  waiting for transfers between devices  55.5 us (18%)
  starting transfers between devices  44.3 us (14%)
  local copies, waits for them, and re-layouts  9.56 us (3%)
    pallas_call x2, Pallas kernels, place(): pl.pallas_call(place_kernel, out_shape=jax.ShapeDtypeStruct(shape, rows.d...  97.8 us
    all_to_all x3, blocking collectives, exchange(): return lax.all_to_all(blocks, axes, 0, 0, tiled=True)  94.3 us
    all_to_all x3, waiting for transfers between devices, exchange(): return lax.all_to_all(blocks, axes, 0, 0, tiled=True)  46.3 us
    ppermute x4, starting transfers between devices, swap(): return lax.ppermute(block, 'c', SWAP)  20.1 us
    all_to_all x3, starting transfers between devices, exchange(): return lax.all_to_all(blocks, axes, 0, 0, tiled=True)  16.6 us
  transfers between devices with their start and end apart: 9, of which 6 were waited for; matrix products, arithmetic and copies ran while one was open for 2% of the time, Pallas kernels for 1%

profile of v4, /device:TPU:1, one launch (start us, length us, event | category | flops | bytes accessed | tf_op | source)
XLA Modules:
  0.0 313.3 jit_solution(15286029941718232567)
XLA Ops:
  0.6 8.8 %collective-permute-start = (bf16[256,6144]{1,0:T(8,128)(2,1)}, bf16[256,6144]{1,0:T(8,128)(2,1)}, u32[]{:S(2)}, u32[]{:S(2)}) collective-permute-start(bf16[256,6144]{1,0:T(8,128)(2,1)} %bitcast.45), channel_id=1, source_target_pairs={{0,1},{1,0},{2,3},{3,2},{4,5},{5,4},{6,7},{7,6},{8,9},{9,8},{10,11... | collective-permute-start | bytes 9437192 | tf_op jit(solution)/shard_map/ppermute | solution.py:49
  9.4 0.8 dynamic-slice_bitcast_fusion.1
  10.2 1.9 collective-permute-start.1
  12.1 0.1 broadcast_in_dim.54
  12.2 0.1 broadcast_in_dim.55
  12.3 0.1 dynamic-slice.8
  12.4 2.3 collective-permute-done.1
  14.7 0.1 dynamic-slice_select_fusion
  14.8 21.2 %all_to_all.30 = bf16[16,24,128]{2,1,0:T(8,128)(2,1)S(1)} all-to-all(bf16[16,24,128]{2,1,0:T(8,128)(2,1)S(1)} %broadcast_in_dim.61), channel_id=1, replica_groups=mesh['yh'=2,'x'=4,'yl'=2,'z'=16,'c'=2] {'z'}, dimensions={0} | all-to-all | bytes 196608 | tf_op jit(solution)/shard_map/all_to_all | solution.py:41
  36.1 1.4 broadcast_in_dim.62
  37.5 6.8 %all-to-all-start.1 = ((bf16[16,16,24,128]{3,2,1,0:T(8,128)(2,1)}), bf16[16,16,24,128]{3,2,1,0:T(8,128)(2,1)S(1)}, u32[]{:S(2)}, u32[]{:S(2)}) async-start(bf16[16,16,24,128]{3,2,1,0:T(8,128)(2,1)} %broadcast_in_dim.62), calls=%async_computation.1 | async-start | bytes 3145728 | tf_op jit(solution)/shard_map/all_to_all | solution.py:41
  44.3 1.7 pack.1
  46.0 5.7 %collective-permute-start.2 = (bf16[12,6144]{1,0:T(8,128)(2,1)}, bf16[12,6144]{1,0:T(8,128)(2,1)S(1)}, u32[]{:S(2)}, u32[]{:S(2)}) collective-permute-start(bf16[12,6144]{1,0:T(8,128)(2,1)} %pack.1), channel_id=1, source_target_pairs={{0,0},{1,2},{2,1},{3,3},{4,64},{5,66},{6,65},{7,67},{8,128},{9,130... | collective-permute-start | bytes 442376 | tf_op jit(solution)/shard_map/ppermute | solution.py:225
  51.7 1.9 collective-permute-start.3
  53.6 3.4 %collective-permute-done.2.one_ref = bf16[12,6144]{1,0:T(8,128)(2,1)S(1)} collective-permute-done((bf16[12,6144]{1,0:T(8,128)(2,1)}, bf16[12,6144]{1,0:T(8,128)(2,1)S(1)}, u32[]{:S(2)}, u32[]{:S(2)}) %collective-permute-start.2) | collective-permute-done | bytes 147488 | tf_op jit(solution)/shard_map/ppermute | solution.py:225
  57.0 3.4 %collective-permute-done.3.two_ref = bf16[12,6144]{1,0:T(8,128)(2,1)S(1)} collective-permute-done((bf16[12,6144]{1,0:T(8,128)(2,1)}, bf16[12,6144]{1,0:T(8,128)(2,1)S(1)}, u32[]{:S(2)}, u32[]{:S(2)}) %collective-permute-start.3) | collective-permute-done | bytes 147488 | tf_op jit(solution)/shard_map/ppermute | solution.py:226
  60.4 0.0 copy-start.2
  60.4 0.7 copy-done.2
  61.1 3.3 %all-to-all-done.1 = bf16[16,16,24,128]{3,2,1,0:T(8,128)(2,1)S(1)} async-done(((bf16[16,16,24,128]{3,2,1,0:T(8,128)(2,1)}), bf16[16,16,24,128]{3,2,1,0:T(8,128)(2,1)S(1)}, u32[]{:S(2)}, u32[]{:S(2)}) %all-to-all-start.1) | async-done | bytes 1572896 | tf_op jit(solution)/shard_map/all_to_all | solution.py:41
  64.4 0.0 copy-start
  64.4 0.4 copy.10
  64.8 0.0 collective-permute-done.other_ref
  64.8 1.5 copy-done
  66.3 3.7 %product.1 = f32[256,128]{1,0:T(8,128)S(1)} custom-call(bf16[256,6144]{1,0:T(8,128)(2,1)S(1)} %bitcast.46, bf16[256,6144]{1,0:T(8,128)(2,1)} %collective-permute-done.other_ref, bf16[6144,128]{1,0:T(8,128)(2,1)S(1)} %bitcast.41), custom_call_target="tpu_custom_call" | custom-call | tf_op jit(solution)/shard_map/product/pallas_call | solution.py:233
  69.9 6.6 %collective-permute-start.4 = (bf16[6144,128]{1,0:T(8,128)(2,1)S(1)}, bf16[6144,128]{1,0:T(8,128)(2,1)S(1)}, u32[]{:S(2)}, u32[]{:S(2)}) collective-permute-start(bf16[6144,128]{1,0:T(8,128)(2,1)S(1)} %bitcast.42), channel_id=1, source_target_pairs={{0,1},{1,0},{2,3},{3,2},{4,5},{5,4},{6,7},{7,6},{8,9},{9,8},{10,11... | collective-permute-start | bytes 4718600 | tf_op jit(solution)/shard_map/ppermute | solution.py:49
  76.5 60.5 %all_to_all.31 = f32[16,16,128]{2,1,0:T(8,128)S(1)} all-to-all(f32[16,16,128]{2,1,0:T(8,128)S(1)} %bitcast.47), channel_id=1, replica_groups=mesh['yh'=2,'x'=4,'yl'=2,'z'=16,'c'=2] {'yl','yh','x'}, dimensions={0} | all-to-all | bytes 262144 | tf_op jit(solution)/shard_map/all_to_all | solution.py:41
  137.1 0.7 broadcast_in_dim.64
  137.8 5.5 %all-to-all-start.3 = ((f32[32,8,128]{2,1,0:T(8,128)}), f32[32,8,128]{2,1,0:T(8,128)S(1)}, u32[]{:S(2)}, u32[]{:S(2)}) async-start(f32[32,8,128]{2,1,0:T(8,128)} %bitcast.50), calls=%async_computation.3 | async-start | bytes 262144 | tf_op jit(solution)/shard_map/all_to_all | solution.py:41
  143.2 0.1 pad_add_fusion.at_ref
  143.3 16.3 %all-to-all-done.3.terms_ref = f32[32,8,128]{2,1,0:T(8,128)S(1)} async-done(((f32[32,8,128]{2,1,0:T(8,128)}), f32[32,8,128]{2,1,0:T(8,128)S(1)}, u32[]{:S(2)}, u32[]{:S(2)}) %all-to-all-start.3) | async-done | bytes 131104 | tf_op jit(solution)/shard_map/all_to_all | solution.py:41
  159.7 0.0 collective-permute-done.4.other_ref
  159.7 0.0 copy-start.3
  159.7 0.9 copy-done.3
  160.6 1.6 update.1
  162.2 12.5 %all_to_all.32.inbox_ref = f32[32,16,128]{2,1,0:T(8,128)S(1)} all-to-all(f32[32,16,128]{2,1,0:T(8,128)S(1)} %get-tuple-element.30), channel_id=1, replica_groups=mesh['yh'=2,'x'=4,'yl'=2,'z'=16,'c'=2] {'yl','yh','x','c'}, dimensions={0} | all-to-all | bytes 524288 | tf_op jit(solution)/shard_map/all_to_all | solution.py:41
  174.7 0.3 rows.1
  175.0 0.0 copy-start.1
  175.0 1.1 copy-done.1
  176.2 4.4 %all-to-all-start.5 = ((bf16[16,8,6144]{2,1,0:T(8,128)(2,1)}), bf16[16,8,6144]{2,1,0:T(8,128)(2,1)}, u32[]{:S(2)}, u32[]{:S(2)}) async-start(bf16[16,8,6144]{2,1,0:T(8,128)(2,1)} %copy-done.1), calls=%async_computation.5 | async-start | bytes 3145728 | tf_op jit(solution)/shard_map/all_to_all | solution.py:41
  180.6 26.7 %all-to-all-done.5.rows_ref = bf16[16,8,6144]{2,1,0:T(8,128)(2,1)} async-done(((bf16[16,8,6144]{2,1,0:T(8,128)(2,1)}), bf16[16,8,6144]{2,1,0:T(8,128)(2,1)}, u32[]{:S(2)}, u32[]{:S(2)}) %all-to-all-start.5) | async-done | bytes 1572896 | tf_op jit(solution)/shard_map/all_to_all | solution.py:41
  207.3 48.9 %place.2.refs_0_ = bf16[16,2,8,6144]{3,2,1,0:T(8,128)(2,1)} custom-call(s32[1]{0:T(128)} %bitcast.at_ref, bf16[16,8,6144]{2,1,0:T(8,128)(2,1)} %all-to-all-done.5.rows_ref), custom_call_target="tpu_custom_call" | custom-call | bytes 3145728 | tf_op jit(solution)/shard_map/place/pallas_call | solution.py:188
  256.2 0.5 slice.7
  256.7 0.5 fusion
  257.2 2.8 collective-permute-start.5
  260.0 0.5 convolution_add_fusion
  260.5 0.1 reshape.87
  260.6 0.1 reduce_sum.19
  261.3 1.8 multiply_subtract_fusion
  263.2 0.0 collective-permute-done.5.rows_ref
  263.2 0.0 copy-start.4
  263.2 1.2 copy-done.4
  264.4 48.9 %place.3 = bf16[16,2,8,6144]{3,2,1,0:T(8,128)(2,1)} custom-call(s32[1]{0:T(128)S(6)} %sub.28.at_ref, bf16[16,8,6144]{2,1,0:T(8,128)(2,1)} %copy-done.4, bf16[16,2,8,6144]{3,2,1,0:T(8,128)(2,1)} %place.2.refs_0_), custom_call_target="tpu_custom_call", output_to_operand_aliasing={{}: (2, {})} | custom-call | bytes 3145728 | tf_op jit(solution)/shard_map/place/pallas_call | solution.py:188
  (7 shorter events, 0.1 us)
Async XLA Ops:
  0.6 64.2 %collective-permute-start = (bf16[256,6144]{1,0:T(8,128)(2,1)}, bf16[256,6144]{1,0:T(8,128)(2,1)}, u32[]{:S(2)}, u32[]{:S(2)}) collective-permute-start(bf16[256,6144]{1,0:T(8,128)(2,1)} %bitcast.45), channel_id=1, source_target_pairs={{0,1},{1,0},{2,3},{3,2},{4,5},{5,4},{6,7},{7,6},{8,9},{9,8},{10,11... | collective-permute-start | bytes 9437192 | tf_op jit(solution)/shard_map/ppermute | solution.py:49
  10.2 4.5 %collective-permute-start.1 = (bf16[96,128]{1,0:T(8,128)(2,1)S(1)}, bf16[96,128]{1,0:T(8,128)(2,1)S(1)}, u32[]{:S(2)}, u32[]{:S(2)}) collective-permute-start(bf16[96,128]{1,0:T(8,128)(2,1)S(1)} %get-tuple-element.42), channel_id=1, source_target_pairs={{0,1},{1,0},{2,3},{3,2},{4,5},{5,4},{6,7},{7,6},{8,9},{9,8},{10,11... | collective-permute-start | bytes 73736 | tf_op jit(solution)/shard_map/ppermute | solution.py:49
  37.5 26.8 %all-to-all-start.1 = ((bf16[16,16,24,128]{3,2,1,0:T(8,128)(2,1)}), bf16[16,16,24,128]{3,2,1,0:T(8,128)(2,1)S(1)}, u32[]{:S(2)}, u32[]{:S(2)}) async-start(bf16[16,16,24,128]{3,2,1,0:T(8,128)(2,1)} %broadcast_in_dim.62), calls=%async_computation.1 | async-start | bytes 3145728 | tf_op jit(solution)/shard_map/all_to_all | solution.py:41
  46.0 11.0 %collective-permute-start.2 = (bf16[12,6144]{1,0:T(8,128)(2,1)}, bf16[12,6144]{1,0:T(8,128)(2,1)S(1)}, u32[]{:S(2)}, u32[]{:S(2)}) collective-permute-start(bf16[12,6144]{1,0:T(8,128)(2,1)} %pack.1), channel_id=1, source_target_pairs={{0,0},{1,2},{2,1},{3,3},{4,64},{5,66},{6,65},{7,67},{8,128},{9,130... | collective-permute-start | bytes 442376 | tf_op jit(solution)/shard_map/ppermute | solution.py:225
  51.7 8.7 %collective-permute-start.3 = (bf16[12,6144]{1,0:T(8,128)(2,1)}, bf16[12,6144]{1,0:T(8,128)(2,1)S(1)}, u32[]{:S(2)}, u32[]{:S(2)}) collective-permute-start(bf16[12,6144]{1,0:T(8,128)(2,1)} %pack.1), channel_id=1, source_target_pairs={{0,2},{1,0},{2,3},{3,1},{4,66},{5,64},{6,67},{7,65},{8,130},{9,128... | collective-permute-start | bytes 442376 | tf_op jit(solution)/shard_map/ppermute | solution.py:226
  60.4 0.7 copy-start.2
  64.4 1.9 copy-start
  69.9 89.7 %collective-permute-start.4 = (bf16[6144,128]{1,0:T(8,128)(2,1)S(1)}, bf16[6144,128]{1,0:T(8,128)(2,1)S(1)}, u32[]{:S(2)}, u32[]{:S(2)}) collective-permute-start(bf16[6144,128]{1,0:T(8,128)(2,1)S(1)} %bitcast.42), channel_id=1, source_target_pairs={{0,1},{1,0},{2,3},{3,2},{4,5},{5,4},{6,7},{7,6},{8,9},{9,8},{10,11... | collective-permute-start | bytes 4718600 | tf_op jit(solution)/shard_map/ppermute | solution.py:49
  137.8 21.9 %all-to-all-start.3 = ((f32[32,8,128]{2,1,0:T(8,128)}), f32[32,8,128]{2,1,0:T(8,128)S(1)}, u32[]{:S(2)}, u32[]{:S(2)}) async-start(f32[32,8,128]{2,1,0:T(8,128)} %bitcast.50), calls=%async_computation.3 | async-start | bytes 262144 | tf_op jit(solution)/shard_map/all_to_all | solution.py:41
  159.7 0.9 copy-start.3
  175.0 1.1 copy-start.1
  176.2 31.1 %all-to-all-start.5 = ((bf16[16,8,6144]{2,1,0:T(8,128)(2,1)}), bf16[16,8,6144]{2,1,0:T(8,128)(2,1)}, u32[]{:S(2)}, u32[]{:S(2)}) async-start(bf16[16,8,6144]{2,1,0:T(8,128)(2,1)} %copy-done.1), calls=%async_computation.5 | async-start | bytes 3145728 | tf_op jit(solution)/shard_map/all_to_all | solution.py:41
  257.2 6.0 %collective-permute-start.5 = (bf16[16,8,6144]{2,1,0:T(8,128)(2,1)}, bf16[16,8,6144]{2,1,0:T(8,128)(2,1)S(1)}, u32[]{:S(2)}, u32[]{:S(2)}) collective-permute-start(bf16[16,8,6144]{2,1,0:T(8,128)(2,1)} %all-to-all-done.5.rows_ref), channel_id=1, source_target_pairs={{0,1},{1,0},{2,3},{3,2},{4,5},{5,4},{6,7},{7,6},{8,9},{9,8},{10,11... | collective-permute-start | bytes 4718600 | tf_op jit(solution)/shard_map/ppermute | solution.py:49
  263.2 1.2 copy-start.4

commit v5 on v4

--- a/solution.py
+++ b/solution.py
@@ -20,21 +20,6 @@
 DP = ("yl", "z", "c")
 PLANE = ("yl", "yh", "x")
 SWAP = [(0, 1), (1, 0)]
-ALL = tuple(FINE)
-
-
-def flat(outer, low, deep, core):
-    return ((outer * 2 + low) * 16 + deep) * 2 + core
-
-
-def state_moves(other):
-    return [
-        (flat(o, low, z, c), flat(z // 2, low, 2 * o + (1 - c if other else c), z % 2))
-        for o in range(8)
-        for low in range(2)
-        for z in range(16)
-        for c in range(2)
-    ]
 
 
 def exchange(blocks, axes):
@@ -172,15 +157,19 @@
 
 
 def place_kernel(at_ref, rows_ref, *refs):
-    out_ref, sems = refs[-2:]
-    copies = [
-        pltpu.make_async_copy(rows_ref.at[i], out_ref.at[i, at_ref[0]], sems.at[i])
+    out_ref, held, in_sems, out_sems = refs[-4:]
+    reads = [pltpu.make_async_copy(rows_ref.at[i], held.at[i], in_sems.at[i]) for i in range(16)]
+    writes = [
+        pltpu.make_async_copy(held.at[i], out_ref.at[i, at_ref[0]], out_sems.at[i])
         for i in range(16)
     ]
-    for copy in copies:
-        copy.start()
-    for copy in copies:
-        copy.wait()
+    for read in reads:
+        read.start()
+    for read, write in zip(reads, writes):
+        read.wait()
+        write.start()
+    for write in writes:
+        write.wait()
 
 
 def place(at, rows, *partly):
@@ -190,9 +179,14 @@
         out_shape=jax.ShapeDtypeStruct(shape, rows.dtype),
         in_specs=[SMEM] + [pl.BlockSpec(memory_space=pl.ANY)] * (1 + len(partly)),
         out_specs=pl.BlockSpec(memory_space=pl.ANY),
-        scratch_shapes=[pltpu.SemaphoreType.DMA((16,))],
+        scratch_shapes=[
+            pltpu.VMEM(rows.shape, rows.dtype),
+            pltpu.SemaphoreType.DMA((16,)),
+            pltpu.SemaphoreType.DMA((16,)),
+        ],
         input_output_aliases={2: 0} if partly else {},
         cost_estimate=pl.CostEstimate(flops=0, bytes_accessed=2 * rows.nbytes, transcendentals=0),
+        compiler_params=LIMIT,
         name="place",
     )(at, rows, *partly)
 
@@ -210,23 +204,20 @@
     half = turned.shape[1] // 2
     mine = lax.dynamic_slice_in_dim(turned, half * core, half, 1)
     theirs = swap(lax.dynamic_slice_in_dim(turned, half * (1 - core), half, 1))
-    chip = in_order(core, mine, theirs, 0).reshape(-1, half)
-    part = chip.shape[0] // 8
-    piece = lax.dynamic_slice_in_dim(chip, part * outer, part, 0)
-    along_z = share(piece, "z", 16)
-    along_z, m_in, v_in, w_in = lax.optimization_barrier((along_z, moment, second, weights))
     state = pl.pallas_call(
         pack_kernel,
         out_shape=jax.ShapeDtypeStruct((12, width), jnp.bfloat16),
         in_specs=[VMEM, VMEM, VMEM],
         out_specs=VMEM,
         name="pack",
-    )(m_in, v_in, w_in)
-    state_one = lax.ppermute(state, ALL, state_moves(False))
-    state_two = lax.ppermute(state, ALL, state_moves(True))
+    )(moment, second, weights)
+    state_z = lax.all_gather(state, "z")
+    chip = in_order(core, mine, theirs, 0).reshape(-1, half)
+    part = chip.shape[0] // 8
+    piece = lax.dynamic_slice_in_dim(chip, part * outer, part, 0)
+    along_z = share(piece, "z", 16)
     other_grad = swap(grad)
     blocks = share(along_z, PLANE, 16)
-    blocks, state_one, state_two = lax.optimization_barrier((blocks, state_one, state_two))
     blocks = blocks.reshape(2, 8, 16, part, half)
     own_basis = blocks.transpose(0, 2, 1, 3, 4).reshape(width, half)
 
@@ -241,10 +232,13 @@
     sketch, basis_sent = lax.optimization_barrier((sketch, own_basis))
     other_basis = swap(basis_sent)
     plane_terms = exchange(sketch.reshape(16, 16, half), PLANE)
+    plane_terms, state_z = lax.optimization_barrier((plane_terms, state_z))
     plane_sum = jnp.sum(plane_terms, axis=0)
     spread = jnp.broadcast_to(plane_sum.reshape(2, 1, 8, half), (2, 16, 8, half))
     terms = exchange(spread.reshape(32, 8, half), ("c", "z"))
 
+    state_one = lax.dynamic_index_in_dim(state_z, 2 * outer + core, 0, keepdims=False)
+    state_two = swap(lax.dynamic_index_in_dim(state_z, 2 * outer + 1 - core, 0, keepdims=False))
     wide = jax.ShapeDtypeStruct((8, width), jnp.float32)
     update8, kept8, message = pl.pallas_call(
         update_kernel,
@@ -254,7 +248,7 @@
         compiler_params=LIMIT,
         name="update",
     )(
-        jnp.stack([core, deep % 2]).astype(jnp.int32),
+        jnp.stack([core, core]).astype(jnp.int32),
         terms,
         own_basis,
         other_basis,
@@ -276,7 +270,6 @@
     rows_mine = exchange(rows_out, PLANE)
     rows_other = swap(rows_mine)
     partly = place(core_at, rows_mine)
-    partly, inbox, ratio = lax.optimization_barrier((partly, inbox, ratio))
     gathered = place(1 - core_at, rows_other, partly)
     gathered = gathered.reshape(1, 256, width)
 

time: 314 us -> 196 us (0.62)
  Pallas kernels: 105 us -> 14.8 us
  blocking collectives: 94.3 us -> 64.4 us
  between operations: 1.49 us -> 14.9 us
  waiting for transfers between devices: 55.5 us -> 48.3 us
  starting transfers between devices: 44.3 us -> 38.4 us
    pallas_call x2, Pallas kernels: 97.8 us -> 6.85 us  [place(): pl.pallas_call(place_kernel, out_shape=jax.ShapeDtypeStruct(shape, rows.d...]
    all_to_all x3, blocking collectives: 94.3 us -> 64.4 us  [exchange(): return lax.all_to_all(blocks, axes, 0, 0, tiled=True)]
    ppermute x2 -> x0, starting transfers between devices: 7.62 us -> none  [the longest x1 5.7 us: on_device(): state_one = lax.ppermute(state, ALL, state_moves(False))]
    ppermute x2 -> x0, waiting for transfers between devices: 6.78 us -> none  [the longest x1 3.41 us: on_device(): state_one = lax.ppermute(state, ALL, state_moves(False))]
    ppermute x4 -> x5, starting transfers between devices: 20.1 us -> 21.8 us  [swap(): return lax.ppermute(block, 'c', SWAP)]
  transfers between devices with their start and end apart: 9 -> 9, of which waited for: 6 -> 5; matrix products, arithmetic and copies ran while one was open for 2% -> 5% of each run, Pallas kernels for 1% -> 4%
where the time goes in v5:
time: 196 us; the launch traced here: 195 us
  blocking collectives  64.4 us (33%)
  waiting for transfers between devices  48.3 us (25%)
  starting transfers between devices  38.4 us (20%)
  between operations  14.9 us (8%)
  Pallas kernels  14.8 us (8%)
  local copies, waits for them, and re-layouts  9.31 us (5%)
  matrix products  3.19 us (2%)
  other arithmetic  2.1 us (1%)
    all_to_all x3, blocking collectives, exchange(): return lax.all_to_all(blocks, axes, 0, 0, tiled=True)  64.4 us
    all_to_all x3, waiting for transfers between devices, exchange(): return lax.all_to_all(blocks, axes, 0, 0, tiled=True)  44.8 us
    ppermute x5, starting transfers between devices, swap(): return lax.ppermute(block, 'c', SWAP)  21.8 us
    all_to_all x3, starting transfers between devices, exchange(): return lax.all_to_all(blocks, axes, 0, 0, tiled=True)  16.6 us
    pallas_call x2, Pallas kernels, place(): pl.pallas_call(place_kernel, out_shape=jax.ShapeDtypeStruct(shape, rows.d...  6.85 us
    pallas_call x1, Pallas kernels, on_device(): pl.pallas_call(product_kernel, out_shape=jax.ShapeDtypeStruct((grad.shape...  4.36 us
    unnamed x10, local copies, waits for them, and re-layouts  4.25 us
  transfers between devices with their start and end apart: 9, of which 5 were waited for; matrix products, arithmetic and copies ran while one was open for 5% of the time, Pallas kernels for 4%

profile of v5, /device:TPU:1, one launch (start us, length us, event | category | flops | bytes accessed | tf_op | source)
XLA Modules:
  0.0 195.4 jit_solution(17528799646364998620)
XLA Ops:
  7.2 0.0 all-gather.4.cloned.1.call-start
  7.2 1.7 pack.1
  8.9 0.0 all-gather.4.cloned.1.call-update
  8.9 8.8 %collective-permute-start = (bf16[256,6144]{1,0:T(8,128)(2,1)}, bf16[256,6144]{1,0:T(8,128)(2,1)}, u32[]{:S(2)}, u32[]{:S(2)}) collective-permute-start(bf16[256,6144]{1,0:T(8,128)(2,1)} %bitcast.51), channel_id=1, source_target_pairs={{0,1},{1,0},{2,3},{3,2},{4,5},{5,4},{6,7},{7,6},{8,9},{9,8},{10,11... | collective-permute-start | bytes 9437192 | tf_op jit(solution)/shard_map/ppermute | solution.py:34
  17.7 0.8 dynamic-slice_bitcast_fusion.3
  18.5 1.9 collective-permute-start.1
  20.4 0.1 broadcast_in_dim.54
  20.5 0.1 broadcast_in_dim.55
  20.6 0.1 dynamic-slice.8
  20.7 2.3 %collective-permute-done.1 = bf16[96,128]{1,0:T(8,128)(2,1)S(1)} collective-permute-done((bf16[96,128]{1,0:T(8,128)(2,1)S(1)}, bf16[96,128]{1,0:T(8,128)(2,1)S(1)}, u32[]{:S(2)}, u32[]{:S(2)}) %collective-permute-start.1) | collective-permute-done | bytes 24608 | tf_op jit(solution)/shard_map/ppermute | solution.py:34
  23.0 0.1 dynamic-slice_select_fusion
  23.1 21.5 %all_to_all.30 = bf16[16,24,128]{2,1,0:T(8,128)(2,1)S(1)} all-to-all(bf16[16,24,128]{2,1,0:T(8,128)(2,1)S(1)} %broadcast_in_dim.61), channel_id=1, replica_groups=mesh['yh'=2,'x'=4,'yl'=2,'z'=16,'c'=2] {'z'}, dimensions={0} | all-to-all | bytes 196608 | tf_op jit(solution)/shard_map/all_to_all | solution.py:26
  44.6 0.3 broadcast_in_dim.62
  44.9 26.3 %all_to_all.31 = bf16[16,16,24,128]{3,2,1,0:T(8,128)(2,1)S(1)} all-to-all(bf16[16,16,24,128]{3,2,1,0:T(8,128)(2,1)S(1)} %broadcast_in_dim.62), channel_id=1, replica_groups=mesh['yh'=2,'x'=4,'yl'=2,'z'=16,'c'=2] {'yl','yh','x'}, dimensions={0} | all-to-all | bytes 3145728 | tf_op jit(solution)/shard_map/all_to_all | solution.py:26
  71.2 0.0 copy-start.1
  71.2 0.4 copy.11
  71.7 0.0 collective-permute-done.other_ref
  71.7 1.5 copy-done.1
  73.1 4.4 %product.1 = f32[256,128]{1,0:T(8,128)} custom-call(bf16[256,6144]{1,0:T(8,128)(2,1)S(1)} %bitcast.52, bf16[256,6144]{1,0:T(8,128)(2,1)} %collective-permute-done.other_ref, bf16[6144,128]{1,0:T(8,128)(2,1)S(1)} %bitcast.47), custom_call_target="tpu_custom_call" | custom-call | tf_op jit(solution)/shard_map/product/pallas_call | solution.py:224
  77.5 6.2 %collective-permute-start.2 = (bf16[6144,128]{1,0:T(8,128)(2,1)S(1)}, bf16[6144,128]{1,0:T(8,128)(2,1)S(1)}, u32[]{:S(2)}, u32[]{:S(2)}) collective-permute-start(bf16[6144,128]{1,0:T(8,128)(2,1)S(1)} %bitcast.48), channel_id=1, source_target_pairs={{0,1},{1,0},{2,3},{3,2},{4,5},{5,4},{6,7},{7,6},{8,9},{9,8},{10,11... | collective-permute-start | bytes 4718600 | tf_op jit(solution)/shard_map/ppermute | solution.py:34
  83.7 3.5 %all-to-all-start.2 = ((f32[16,16,128]{2,1,0:T(8,128)}), f32[16,16,128]{2,1,0:T(8,128)S(1)}, u32[]{:S(2)}, u32[]{:S(2)}) async-start(f32[16,16,128]{2,1,0:T(8,128)} %bitcast.9), calls=%async_computation.2 | async-start | bytes 262144 | tf_op jit(solution)/shard_map/all_to_all | solution.py:26
  87.3 7.4 %all-to-all-done.2 = f32[16,16,128]{2,1,0:T(8,128)S(1)} async-done(((f32[16,16,128]{2,1,0:T(8,128)}), f32[16,16,128]{2,1,0:T(8,128)S(1)}, u32[]{:S(2)}, u32[]{:S(2)}) %all-to-all-start.2) | async-done | bytes 131104 | tf_op jit(solution)/shard_map/all_to_all | solution.py:26
  94.6 0.0 all-gather.4.cloned.1.call-done
  94.7 0.7 broadcast_in_dim.64
  95.3 9.3 %all-to-all-start.3 = ((f32[32,8,128]{2,1,0:T(8,128)}), f32[32,8,128]{2,1,0:T(8,128)S(1)}, u32[]{:S(2)}, u32[]{:S(2)}) async-start(f32[32,8,128]{2,1,0:T(8,128)} %bitcast.12), calls=%async_computation.3 | async-start | bytes 262144 | tf_op jit(solution)/shard_map/all_to_all | solution.py:26
  104.7 1.1 dynamic-slice_bitcast_fusion
  105.7 2.1 %collective-permute-start.3 = (bf16[12,6144]{1,0:T(8,128)(2,1)S(1)}, bf16[12,6144]{1,0:T(8,128)(2,1)S(1)}, u32[]{:S(2)}, u32[]{:S(2)}) collective-permute-start(bf16[12,6144]{1,0:T(8,128)(2,1)S(1)} %get-tuple-element.25), channel_id=1, source_target_pairs={{0,1},{1,0},{2,3},{3,2},{4,5},{5,4},{6,7},{7,6},{8,9},{9,8},{10,11... | collective-permute-start | bytes 442376 | tf_op jit(solution)/shard_map/ppermute | solution.py:34
  107.9 0.1 pad_add_fusion.at_ref
  107.9 1.1 collective-permute-done.3.two_ref
  109.1 0.0 copy-start.3
  109.1 0.7 copy-done.3
  109.7 0.0 collective-permute-done.2.other_ref
  109.7 0.0 copy-start
  109.7 11.3 %all-to-all-done.3.terms_ref = f32[32,8,128]{2,1,0:T(8,128)S(1)} async-done(((f32[32,8,128]{2,1,0:T(8,128)}), f32[32,8,128]{2,1,0:T(8,128)S(1)}, u32[]{:S(2)}, u32[]{:S(2)}) %all-to-all-start.3) | async-done | bytes 131104 | tf_op jit(solution)/shard_map/all_to_all | solution.py:26
  121.0 0.0 copy-start.4
  121.0 0.9 copy-done.4
  122.0 1.6 update.1
  123.6 0.0 copy-done
  123.6 16.6 %all_to_all.32.inbox_ref = f32[32,16,128]{2,1,0:T(8,128)S(1)} all-to-all(f32[32,16,128]{2,1,0:T(8,128)S(1)} %get-tuple-element.17), channel_id=1, replica_groups=mesh['yh'=2,'x'=4,'yl'=2,'z'=16,'c'=2] {'yl','yh','x','c'}, dimensions={0} | all-to-all | bytes 524288 | tf_op jit(solution)/shard_map/all_to_all | solution.py:26
  140.2 0.3 rows.1
  140.5 0.0 copy-start.2
  140.5 1.2 copy-done.2
  141.7 3.7 %all-to-all-start.5 = ((bf16[16,8,6144]{2,1,0:T(8,128)(2,1)}), bf16[16,8,6144]{2,1,0:T(8,128)(2,1)S(1)}, u32[]{:S(2)}, u32[]{:S(2)}) async-start(bf16[16,8,6144]{2,1,0:T(8,128)(2,1)} %copy-done.2), calls=%async_computation.5 | async-start | bytes 3145728 | tf_op jit(solution)/shard_map/all_to_all | solution.py:26
  145.5 0.5 fusion
  146.0 26.1 %all-to-all-done.5.rows_ref = bf16[16,8,6144]{2,1,0:T(8,128)(2,1)S(1)} async-done(((bf16[16,8,6144]{2,1,0:T(8,128)(2,1)}), bf16[16,8,6144]{2,1,0:T(8,128)(2,1)S(1)}, u32[]{:S(2)}, u32[]{:S(2)}) %all-to-all-start.5) | async-done | bytes 1572896 | tf_op jit(solution)/shard_map/all_to_all | solution.py:26
  172.0 2.8 %collective-permute-start.4 = (bf16[16,8,6144]{2,1,0:T(8,128)(2,1)S(1)}, bf16[16,8,6144]{2,1,0:T(8,128)(2,1)S(1)}, u32[]{:S(2)}, u32[]{:S(2)}) collective-permute-start(bf16[16,8,6144]{2,1,0:T(8,128)(2,1)S(1)} %all-to-all-done.5.rows_ref), channel_id=1, source_target_pairs={{0,1},{1,0},{2,3},{3,2},{4,5},{5,4},{6,7},{7,6},{8,9},{9,8},{10,11... | collective-permute-start | bytes 4718600 | tf_op jit(solution)/shard_map/ppermute | solution.py:34
  174.8 2.7 %convolution_add_fusion = f32[12,6144]{1,0:T(8,128)} fusion(f32[12,6144]{1,0:T(8,128)S(1)} %fusion, bf16[6144,128]{1,0:T(8,128)(2,1)} %copy-done, bf16[4,128]{1,0:T(4,128)(2,1)S(1)} %get-tuple-element.33, bf16[4,128]{1,0:T(4,128)(2,1)S(1)} %get-tuple-element.32, bf16[4,128]{1,0:T(4,128)(2,1)S(1)} %get-tuple-element.29), kind=kOutput, calls=%fused_computation | convolution fusion | flops 18957312 | bytes 2165760 | tf_op jit(solution)/shard_map/dot_general | solution.py:59
  177.5 1.1 reshape.84
  178.6 0.1 reduce_sum.19
  178.7 0.5 slice.7
  179.8 1.8 multiply_subtract_fusion
  181.7 3.4 %place.2.refs_0_ = bf16[16,2,8,6144]{3,2,1,0:T(8,128)(2,1)} custom-call(s32[1]{0:T(128)} %bitcast.at_ref, bf16[16,8,6144]{2,1,0:T(8,128)(2,1)S(1)} %all-to-all-done.5.rows_ref), custom_call_target="tpu_custom_call" | custom-call | bytes 3145728 | tf_op jit(solution)/shard_map/place/pallas_call | solution.py:177
  185.1 0.0 collective-permute-done.4.rows_ref
  185.1 3.4 %place.3 = bf16[16,2,8,6144]{3,2,1,0:T(8,128)(2,1)} custom-call(s32[1]{0:T(128)S(6)} %sub.32.at_ref, bf16[16,8,6144]{2,1,0:T(8,128)(2,1)S(1)} %collective-permute-done.4.rows_ref, bf16[16,2,8,6144]{3,2,1,0:T(8,128)(2,1)} %place.2.refs_0_), custom_call_target="tpu_custom_call", output_to_operand_aliasing={{}: (2, {})} | custom-call | bytes 3145728 | tf_op jit(solution)/shard_map/place/pallas_call | solution.py:177
  (7 shorter events, 0.1 us)
Async XLA Ops:
  7.2 87.5 %all-gather.4.cloned.1.call-start = ((), (), s32[]{:S(2)}) async-start(), calls=%async_computation.6 | async-start | bytes 3342336 | tf_op jit(solution)/shard_map/all_gather | solution.py:214
  8.9 62.7 %collective-permute-start = (bf16[256,6144]{1,0:T(8,128)(2,1)}, bf16[256,6144]{1,0:T(8,128)(2,1)}, u32[]{:S(2)}, u32[]{:S(2)}) collective-permute-start(bf16[256,6144]{1,0:T(8,128)(2,1)} %bitcast.51), channel_id=1, source_target_pairs={{0,1},{1,0},{2,3},{3,2},{4,5},{5,4},{6,7},{7,6},{8,9},{9,8},{10,11... | collective-permute-start | bytes 9437192 | tf_op jit(solution)/shard_map/ppermute | solution.py:34
  18.5 4.5 %collective-permute-start.1 = (bf16[96,128]{1,0:T(8,128)(2,1)S(1)}, bf16[96,128]{1,0:T(8,128)(2,1)S(1)}, u32[]{:S(2)}, u32[]{:S(2)}) collective-permute-start(bf16[96,128]{1,0:T(8,128)(2,1)S(1)} %get-tuple-element.28), channel_id=1, source_target_pairs={{0,1},{1,0},{2,3},{3,2},{4,5},{5,4},{6,7},{7,6},{8,9},{9,8},{10,11... | collective-permute-start | bytes 73736 | tf_op jit(solution)/shard_map/ppermute | solution.py:34
  71.2 1.9 copy-start.1
  77.5 32.2 %collective-permute-start.2 = (bf16[6144,128]{1,0:T(8,128)(2,1)S(1)}, bf16[6144,128]{1,0:T(8,128)(2,1)S(1)}, u32[]{:S(2)}, u32[]{:S(2)}) collective-permute-start(bf16[6144,128]{1,0:T(8,128)(2,1)S(1)} %bitcast.48), channel_id=1, source_target_pairs={{0,1},{1,0},{2,3},{3,2},{4,5},{5,4},{6,7},{7,6},{8,9},{9,8},{10,11... | collective-permute-start | bytes 4718600 | tf_op jit(solution)/shard_map/ppermute | solution.py:34
  83.7 10.9 %all-to-all-start.2 = ((f32[16,16,128]{2,1,0:T(8,128)}), f32[16,16,128]{2,1,0:T(8,128)S(1)}, u32[]{:S(2)}, u32[]{:S(2)}) async-start(f32[16,16,128]{2,1,0:T(8,128)} %bitcast.9), calls=%async_computation.2 | async-start | bytes 262144 | tf_op jit(solution)/shard_map/all_to_all | solution.py:26
  95.3 25.7 %all-to-all-start.3 = ((f32[32,8,128]{2,1,0:T(8,128)}), f32[32,8,128]{2,1,0:T(8,128)S(1)}, u32[]{:S(2)}, u32[]{:S(2)}) async-start(f32[32,8,128]{2,1,0:T(8,128)} %bitcast.12), calls=%async_computation.3 | async-start | bytes 262144 | tf_op jit(solution)/shard_map/all_to_all | solution.py:26
  105.7 3.3 %collective-permute-start.3 = (bf16[12,6144]{1,0:T(8,128)(2,1)S(1)}, bf16[12,6144]{1,0:T(8,128)(2,1)S(1)}, u32[]{:S(2)}, u32[]{:S(2)}) collective-permute-start(bf16[12,6144]{1,0:T(8,128)(2,1)S(1)} %get-tuple-element.25), channel_id=1, source_target_pairs={{0,1},{1,0},{2,3},{3,2},{4,5},{5,4},{6,7},{7,6},{8,9},{9,8},{10,11... | collective-permute-start | bytes 442376 | tf_op jit(solution)/shard_map/ppermute | solution.py:34
  109.1 0.7 copy-start.3
  109.7 13.9 %copy-start = (bf16[6144,128]{1,0:T(8,128)(2,1)}, bf16[6144,128]{1,0:T(8,128)(2,1)S(1)}, u32[]{:S(2)}) copy-start(bf16[6144,128]{1,0:T(8,128)(2,1)S(1)} %collective-permute-done.2.other_ref) | copy-start | bytes 4718596
  121.0 0.9 copy-start.4
  140.5 1.2 copy-start.2
  141.7 30.4 %all-to-all-start.5 = ((bf16[16,8,6144]{2,1,0:T(8,128)(2,1)}), bf16[16,8,6144]{2,1,0:T(8,128)(2,1)S(1)}, u32[]{:S(2)}, u32[]{:S(2)}) async-start(bf16[16,8,6144]{2,1,0:T(8,128)(2,1)} %copy-done.2), calls=%async_computation.5 | async-start | bytes 3145728 | tf_op jit(solution)/shard_map/all_to_all | solution.py:26
  172.0 13.0 %collective-permute-start.4 = (bf16[16,8,6144]{2,1,0:T(8,128)(2,1)S(1)}, bf16[16,8,6144]{2,1,0:T(8,128)(2,1)S(1)}, u32[]{:S(2)}, u32[]{:S(2)}) collective-permute-start(bf16[16,8,6144]{2,1,0:T(8,128)(2,1)S(1)} %all-to-all-done.5.rows_ref), channel_id=1, source_target_pairs={{0,1},{1,0},{2,3},{3,2},{4,5},{5,4},{6,7},{7,6},{8,9},{9,8},{10,11... | collective-permute-start | bytes 4718600 | tf_op jit(solution)/shard_map/ppermute | solution.py:34
Sparse Core Ops, SparseCore 0:
  10.7 77.5 all-gather.3

commit v6 on v4

--- a/solution.py
+++ b/solution.py
@@ -23,18 +23,29 @@
 ALL = tuple(FINE)
 
 
-def flat(outer, low, deep, core):
-    return ((outer * 2 + low) * 16 + deep) * 2 + core
-
-
-def state_moves(other):
-    return [
-        (flat(o, low, z, c), flat(z // 2, low, 2 * o + (1 - c if other else c), z % 2))
-        for o in range(8)
-        for low in range(2)
-        for z in range(16)
-        for c in range(2)
-    ]
+def moves(target):
+    pairs = []
+    for o in range(8):
+        for low in range(2):
+            for z in range(16):
+                for c in range(2):
+                    to_o, to_z, to_c = target(o, z, c)
+                    pairs.append(
+                        (((o * 2 + low) * 16 + z) * 2 + c, ((to_o * 2 + low) * 16 + to_z) * 2 + to_c)
+                    )
+    return pairs
+
+
+def along_z_moves(offset):
+    return moves(lambda o, z, c: (o, (o + offset - z) % 16, c))
+
+
+def in_plane_moves(first):
+    def target(o, z, c):
+        row = (o + 8 * ((c + first) % 2) - z) % 16
+        return row // 2, z, row % 2
+
+    return moves(target)
 
 
 def exchange(blocks, axes):
@@ -87,7 +98,7 @@
 
 VMEM = pl.BlockSpec(memory_space=pltpu.VMEM)
 SMEM = pl.BlockSpec(memory_space=pltpu.SMEM)
-LIMIT = pltpu.CompilerParams(vmem_limit_bytes=12 << 20)
+LIMIT = pltpu.CompilerParams(vmem_limit_bytes=6 << 20)
 CHUNK = 512
 
 
@@ -188,11 +199,12 @@
     return pl.pallas_call(
         place_kernel,
         out_shape=jax.ShapeDtypeStruct(shape, rows.dtype),
-        in_specs=[SMEM] + [pl.BlockSpec(memory_space=pl.ANY)] * (1 + len(partly)),
+        in_specs=[SMEM, VMEM] + [pl.BlockSpec(memory_space=pl.ANY)] * len(partly),
         out_specs=pl.BlockSpec(memory_space=pl.ANY),
         scratch_shapes=[pltpu.SemaphoreType.DMA((16,))],
         input_output_aliases={2: 0} if partly else {},
         cost_estimate=pl.CostEstimate(flops=0, bytes_accessed=2 * rows.nbytes, transcendentals=0),
+        compiler_params=LIMIT,
         name="place",
     )(at, rows, *partly)
 
@@ -204,7 +216,6 @@
     deep = lax.axis_index("z")
     low = lax.axis_index("yl")
     outer = lax.axis_index("yh") * 4 + lax.axis_index("x")
-    core_at = core.astype(jnp.int32).reshape(1)
 
     turned = basis.T
     half = turned.shape[1] // 2
@@ -222,11 +233,11 @@
         out_specs=VMEM,
         name="pack",
     )(m_in, v_in, w_in)
-    state_one = lax.ppermute(state, ALL, state_moves(False))
-    state_two = lax.ppermute(state, ALL, state_moves(True))
+    state_a = lax.ppermute(state, ALL, along_z_moves(0))
+    state_b = lax.ppermute(state, ALL, along_z_moves(8))
     other_grad = swap(grad)
     blocks = share(along_z, PLANE, 16)
-    blocks, state_one, state_two = lax.optimization_barrier((blocks, state_one, state_two))
+    blocks, state_a, state_b = lax.optimization_barrier((blocks, state_a, state_b))
     blocks = blocks.reshape(2, 8, 16, part, half)
     own_basis = blocks.transpose(0, 2, 1, 3, 4).reshape(width, half)
 
@@ -242,6 +253,9 @@
     other_basis = swap(basis_sent)
     plane_terms = exchange(sketch.reshape(16, 16, half), PLANE)
     plane_sum = jnp.sum(plane_terms, axis=0)
+    plane_sum, state_a, state_b = lax.optimization_barrier((plane_sum, state_a, state_b))
+    state_one = lax.ppermute(jnp.where(core == 0, state_a, state_b), ALL, in_plane_moves(0))
+    state_two = lax.ppermute(jnp.where(core == 0, state_b, state_a), ALL, in_plane_moves(1))
     spread = jnp.broadcast_to(plane_sum.reshape(2, 1, 8, half), (2, 16, 8, half))
     terms = exchange(spread.reshape(32, 8, half), ("c", "z"))
 
@@ -254,7 +268,7 @@
         compiler_params=LIMIT,
         name="update",
     )(
-        jnp.stack([core, deep % 2]).astype(jnp.int32),
+        jnp.stack([core, (2 * outer + core + deep) % 16 // 8]).astype(jnp.int32),
         terms,
         own_basis,
         other_basis,
@@ -274,17 +288,18 @@
         name="rows",
     )(inbox, update8, kept8)
     rows_mine = exchange(rows_out, PLANE)
-    rows_other = swap(rows_mine)
-    partly = place(core_at, rows_mine)
-    partly, inbox, ratio = lax.optimization_barrier((partly, inbox, ratio))
-    gathered = place(1 - core_at, rows_other, partly)
-    gathered = gathered.reshape(1, 256, width)
 
     trust_ratio = ratio[0, 0]
     own = lax.dynamic_index_in_dim(inbox, low * 16 + deep, 0, keepdims=False)[:8]
     estimate = estimate_rows(own.reshape(2, 4, half), core, own_basis, other_basis, 3)[None]
     moment_new, second_new, update = moments(estimate, weights, moment, second)
     weight_new = weights - rate * trust_ratio * update
+    rows_mine, weight_new, moment_new, second_new = lax.optimization_barrier(
+        (rows_mine, weight_new, moment_new, second_new)
+    )
+    rows_other = swap(rows_mine)
+    core_at = core.astype(jnp.int32).reshape(1)
+    gathered = place(1 - core_at, rows_other, place(core_at, rows_mine)).reshape(1, 256, width)
     return (weight_new, moment_new, second_new, gathered)
 
 

time: 314 us -> 193 us (0.61)
  Pallas kernels: 105 us -> 11.1 us
  blocking collectives: 94.3 us -> 21.2 us
  starting transfers between devices: 44.3 us -> 82.7 us
    pallas_call x2, Pallas kernels: 97.8 us -> 2.53 us  [place(): pl.pallas_call(place_kernel, out_shape=jax.ShapeDtypeStruct(shape, rows.d...]
    all_to_all x3 -> x1, blocking collectives: 94.3 us -> 21.2 us  [exchange(): return lax.all_to_all(blocks, axes, 0, 0, tiled=True)]
    all_to_all x3 -> x5, starting transfers between devices: 16.6 us -> 52 us  [exchange(): return lax.all_to_all(blocks, axes, 0, 0, tiled=True)]
    ppermute x2 -> x4, starting transfers between devices: 7.62 us -> 14.5 us  [the longest x1 5.52 us: on_device(): state_b = lax.ppermute(state, ALL, along_z_moves(8))]
    ppermute x2 -> x4, waiting for transfers between devices: 6.78 us -> 13 us  [the longest x1 7.24 us: on_device(): state_b = lax.ppermute(state, ALL, along_z_moves(8))]
    all_to_all x3 -> x5, waiting for transfers between devices: 46.3 us -> 41 us  [exchange(): return lax.all_to_all(blocks, axes, 0, 0, tiled=True)]
    ppermute x4, starting transfers between devices: 20.1 us -> 16.2 us  [swap(): return lax.ppermute(block, 'c', SWAP)]
    unnamed x10 -> x24, local copies, waits for them, and re-layouts: 5.39 us -> 7.42 us
  transfers between devices with their start and end apart: 9 -> 13, of which waited for: 6 -> 10; matrix products, arithmetic and copies ran while one was open for 2% -> 4% of each run, Pallas kernels for 1% -> 2%
where the time goes in v6:
time: 193 us; the launch traced here: 190 us
  starting transfers between devices  82.7 us (43%)
  waiting for transfers between devices  58.2 us (30%)
  blocking collectives  21.2 us (11%)
  local copies, waits for them, and re-layouts  11.6 us (6%)
  Pallas kernels  11.1 us (6%)
  other arithmetic  2.82 us (1%)
    all_to_all x5, starting transfers between devices, exchange(): return lax.all_to_all(blocks, axes, 0, 0, tiled=True)  52 us
    all_to_all x5, waiting for transfers between devices, exchange(): return lax.all_to_all(blocks, axes, 0, 0, tiled=True)  41 us
    all_to_all x1, blocking collectives, exchange(): return lax.all_to_all(blocks, axes, 0, 0, tiled=True)  21.2 us
    ppermute x4, starting transfers between devices, swap(): return lax.ppermute(block, 'c', SWAP)  16.2 us
    unnamed x24, local copies, waits for them, and re-layouts  7.42 us
    ppermute x1, waiting for transfers between devices, on_device(): state_b = lax.ppermute(state, ALL, along_z_moves(8))  7.24 us
    ppermute x1, starting transfers between devices, on_device(): state_b = lax.ppermute(state, ALL, along_z_moves(8))  5.52 us
    pallas_call x1, Pallas kernels, on_device(): pl.pallas_call(product_kernel, out_shape=jax.ShapeDtypeStruct((grad.shape...  4.34 us
  transfers between devices with their start and end apart: 13, of which 10 were waited for; matrix products, arithmetic and copies ran while one was open for 4% of the time, Pallas kernels for 2%

profile of v6, /device:TPU:1, one launch (start us, length us, event | category | flops | bytes accessed | tf_op | source)
XLA Modules:
  0.0 190.3 jit_solution(2601498013634135906)
XLA Ops:
  0.6 8.8 %collective-permute-start = (bf16[256,6144]{1,0:T(8,128)(2,1)}, bf16[256,6144]{1,0:T(8,128)(2,1)}, u32[]{:S(2)}, u32[]{:S(2)}) collective-permute-start(bf16[256,6144]{1,0:T(8,128)(2,1)} %bitcast.45), channel_id=1, source_target_pairs={{0,1},{1,0},{2,3},{3,2},{4,5},{5,4},{6,7},{7,6},{8,9},{9,8},{10,11... | collective-permute-start | bytes 9437192 | tf_op jit(solution)/shard_map/ppermute | solution.py:60
  9.4 0.8 dynamic-slice_bitcast_fusion.1
  10.2 1.9 %collective-permute-start.1 = (bf16[96,128]{1,0:T(8,128)(2,1)S(1)}, bf16[96,128]{1,0:T(8,128)(2,1)S(1)}, u32[]{:S(2)}, u32[]{:S(2)}) collective-permute-start(bf16[96,128]{1,0:T(8,128)(2,1)S(1)} %get-tuple-element.52), channel_id=1, source_target_pairs={{0,1},{1,0},{2,3},{3,2},{4,5},{5,4},{6,7},{7,6},{8,9},{9,8},{10,11... | collective-permute-start | bytes 73736 | tf_op jit(solution)/shard_map/ppermute | solution.py:60
  12.1 0.1 broadcast_in_dim.54
  12.2 0.1 broadcast_in_dim.55
  12.3 0.1 dynamic-slice.8
  12.4 2.3 %collective-permute-done.1 = bf16[96,128]{1,0:T(8,128)(2,1)S(1)} collective-permute-done((bf16[96,128]{1,0:T(8,128)(2,1)S(1)}, bf16[96,128]{1,0:T(8,128)(2,1)S(1)}, u32[]{:S(2)}, u32[]{:S(2)}) %collective-permute-start.1) | collective-permute-done | bytes 24608 | tf_op jit(solution)/shard_map/ppermute | solution.py:60
  14.7 0.1 dynamic-slice_select_fusion
  14.8 21.2 %all_to_all.30 = bf16[16,24,128]{2,1,0:T(8,128)(2,1)S(1)} all-to-all(bf16[16,24,128]{2,1,0:T(8,128)(2,1)S(1)} %broadcast_in_dim.61), channel_id=1, replica_groups=mesh['yh'=2,'x'=4,'yl'=2,'z'=16,'c'=2] {'z'}, dimensions={0} | all-to-all | bytes 196608 | tf_op jit(solution)/shard_map/all_to_all | solution.py:52
  36.1 1.4 broadcast_in_dim.62
  37.5 6.8 %all-to-all-start.1 = ((bf16[16,16,24,128]{3,2,1,0:T(8,128)(2,1)}), bf16[16,16,24,128]{3,2,1,0:T(8,128)(2,1)S(1)}, u32[]{:S(2)}, u32[]{:S(2)}) async-start(bf16[16,16,24,128]{3,2,1,0:T(8,128)(2,1)} %broadcast_in_dim.62), calls=%async_computation.1 | async-start | bytes 3145728 | tf_op jit(solution)/shard_map/all_to_all | solution.py:52
  44.3 1.7 pack.1
  46.0 5.5 %collective-permute-start.3 = (bf16[12,6144]{1,0:T(8,128)(2,1)}, bf16[12,6144]{1,0:T(8,128)(2,1)S(1)}, u32[]{:S(2)}, u32[]{:S(2)}) collective-permute-start(bf16[12,6144]{1,0:T(8,128)(2,1)} %pack.1), channel_id=1, source_target_pairs={{0,16},{1,17},{2,14},{3,15},{4,12},{5,13},{6,10},{7,11},{8,8},{9,9... | collective-permute-start | bytes 442376 | tf_op jit(solution)/shard_map/ppermute | solution.py:237
  51.5 3.0 %collective-permute-start.2 = (bf16[12,6144]{1,0:T(8,128)(2,1)}, bf16[12,6144]{1,0:T(8,128)(2,1)}, u32[]{:S(2)}, u32[]{:S(2)}) collective-permute-start(bf16[12,6144]{1,0:T(8,128)(2,1)} %pack.1), channel_id=1, source_target_pairs={{0,0},{1,1},{2,30},{3,31},{4,28},{5,29},{6,26},{7,27},{8,24},{9,25... | collective-permute-start | bytes 442376 | tf_op jit(solution)/shard_map/ppermute | solution.py:236
  54.5 7.2 %collective-permute-done.3 = bf16[12,6144]{1,0:T(8,128)(2,1)S(1)} collective-permute-done((bf16[12,6144]{1,0:T(8,128)(2,1)}, bf16[12,6144]{1,0:T(8,128)(2,1)S(1)}, u32[]{:S(2)}, u32[]{:S(2)}) %collective-permute-start.3) | collective-permute-done | bytes 147488 | tf_op jit(solution)/shard_map/ppermute | solution.py:237
  61.8 0.0 collective-permute-done.2
  61.8 2.6 %all-to-all-done.1 = bf16[16,16,24,128]{3,2,1,0:T(8,128)(2,1)S(1)} async-done(((bf16[16,16,24,128]{3,2,1,0:T(8,128)(2,1)}), bf16[16,16,24,128]{3,2,1,0:T(8,128)(2,1)S(1)}, u32[]{:S(2)}, u32[]{:S(2)}) %all-to-all-start.1) | async-done | bytes 1572896 | tf_op jit(solution)/shard_map/all_to_all | solution.py:52
  64.4 0.4 copy.10
  64.8 0.0 collective-permute-done.other_ref
  64.8 1.5 copy-done.2
  66.3 4.3 %product.1 = f32[256,128]{1,0:T(8,128)} custom-call(bf16[256,6144]{1,0:T(8,128)(2,1)S(1)} %bitcast.46, bf16[256,6144]{1,0:T(8,128)(2,1)} %collective-permute-done.other_ref, bf16[6144,128]{1,0:T(8,128)(2,1)S(1)} %bitcast.41), custom_call_target="tpu_custom_call" | custom-call | tf_op jit(solution)/shard_map/product/pallas_call | solution.py:244
  70.6 20.6 %all-to-all-start.2 = ((f32[16,16,128]{2,1,0:T(8,128)}), f32[16,16,128]{2,1,0:T(8,128)S(1)}, u32[]{:S(2)}, u32[]{:S(2)}) async-start(f32[16,16,128]{2,1,0:T(8,128)} %bitcast.10), calls=%async_computation.2 | async-start | bytes 262144 | tf_op jit(solution)/shard_map/all_to_all | solution.py:52
  91.2 2.8 %collective-permute-start.4 = (bf16[6144,128]{1,0:T(8,128)(2,1)S(1)}, bf16[6144,128]{1,0:T(8,128)(2,1)S(1)}, u32[]{:S(2)}, u32[]{:S(2)}) collective-permute-start(bf16[6144,128]{1,0:T(8,128)(2,1)S(1)} %bitcast.42), channel_id=1, source_target_pairs={{0,1},{1,0},{2,3},{3,2},{4,5},{5,4},{6,7},{7,6},{8,9},{9,8},{10,11... | collective-permute-start | bytes 4718600 | tf_op jit(solution)/shard_map/ppermute | solution.py:60
  94.0 4.2 %all-to-all-done.2 = f32[16,16,128]{2,1,0:T(8,128)S(1)} async-done(((f32[16,16,128]{2,1,0:T(8,128)}), f32[16,16,128]{2,1,0:T(8,128)S(1)}, u32[]{:S(2)}, u32[]{:S(2)}) %all-to-all-start.2) | async-done | bytes 131104 | tf_op jit(solution)/shard_map/all_to_all | solution.py:52
  98.2 0.7 broadcast_in_dim.64
  98.9 9.7 %all-to-all-start.3 = ((f32[32,8,128]{2,1,0:T(8,128)}), f32[32,8,128]{2,1,0:T(8,128)S(1)}, u32[]{:S(2)}, u32[]{:S(2)}) async-start(f32[32,8,128]{2,1,0:T(8,128)} %bitcast.12), calls=%async_computation.3 | async-start | bytes 262144 | tf_op jit(solution)/shard_map/all_to_all | solution.py:52
  108.5 1.7 broadcast_select_fusion
  110.2 2.1 %collective-permute-start.6 = (bf16[12,6144]{1,0:T(8,128)(2,1)}, bf16[12,6144]{1,0:T(8,128)(2,1)S(1)}, u32[]{:S(2)}, u32[]{:S(2)}) collective-permute-start(bf16[12,6144]{1,0:T(8,128)(2,1)} %get-tuple-element.49), channel_id=1, source_target_pairs={{0,256},{1,0},{2,195},{3,451},{4,196},{5,452},{6,135},{7,391},{8,1... | collective-permute-start | bytes 442376 | tf_op jit(solution)/shard_map/ppermute | solution.py:258
  112.4 3.9 %collective-permute-start.5 = (bf16[12,6144]{1,0:T(8,128)(2,1)}, bf16[12,6144]{1,0:T(8,128)(2,1)}, u32[]{:S(2)}, u32[]{:S(2)}) collective-permute-start(bf16[12,6144]{1,0:T(8,128)(2,1)} %get-tuple-element.50), channel_id=1, source_target_pairs={{0,0},{1,256},{2,451},{3,195},{4,452},{5,196},{6,391},{7,135},{8,3... | collective-permute-start | bytes 442376 | tf_op jit(solution)/shard_map/ppermute | solution.py:257
  116.3 0.1 pad_add_fusion.at_ref
  116.4 2.0 %collective-permute-done.6.two_ref = bf16[12,6144]{1,0:T(8,128)(2,1)S(1)} collective-permute-done((bf16[12,6144]{1,0:T(8,128)(2,1)}, bf16[12,6144]{1,0:T(8,128)(2,1)S(1)}, u32[]{:S(2)}, u32[]{:S(2)}) %collective-permute-start.6) | collective-permute-done | bytes 147488 | tf_op jit(solution)/shard_map/ppermute | solution.py:258
  118.4 3.8 %collective-permute-done.5.one_ref = bf16[12,6144]{1,0:T(8,128)(2,1)} collective-permute-done((bf16[12,6144]{1,0:T(8,128)(2,1)}, bf16[12,6144]{1,0:T(8,128)(2,1)}, u32[]{:S(2)}, u32[]{:S(2)}) %collective-permute-start.5) | collective-permute-done | bytes 147488 | tf_op jit(solution)/shard_map/ppermute | solution.py:257
  122.2 2.7 %all-to-all-done.3.terms_ref = f32[32,8,128]{2,1,0:T(8,128)S(1)} async-done(((f32[32,8,128]{2,1,0:T(8,128)}), f32[32,8,128]{2,1,0:T(8,128)S(1)}, u32[]{:S(2)}, u32[]{:S(2)}) %all-to-all-start.3) | async-done | bytes 131104 | tf_op jit(solution)/shard_map/all_to_all | solution.py:52
  124.9 0.0 collective-permute-done.4.other_ref
  124.9 2.2 %update.1 = (f32[8,6144]{1,0:T(8,128)S(1)}, f32[8,6144]{1,0:T(8,128)S(1)}, f32[32,16,128]{2,1,0:T(8,128)S(1)}) custom-call(s32[2]{0:T(128)S(1)} %pad_add_fusion.at_ref, f32[32,8,128]{2,1,0:T(8,128)S(1)} %all-to-all-done.3.terms_ref, bf16[6144,128]{1,0:T(8,128)(2,1)S(1)} %bitcast.43, bf16[6144,128]{1,0:T(8,128)(2,1)S(1)} %collective-permute-done.4.other_ref, ...), custom_call_target="tpu_custom_call" | custom-call | tf_op jit(solution)/shard_map/update/pallas_call | solution.py:263
  127.1 0.0 copy-done
  127.1 0.0 copy-start.4
  127.2 0.7 copy-done.4
  127.9 0.7 copy-done.5
  128.5 0.7 copy-done.7
  129.2 11.2 %all-to-all-start.4 = ((f32[32,16,128]{2,1,0:T(8,128)}), f32[32,16,128]{2,1,0:T(8,128)S(1)}, u32[]{:S(2)}, u32[]{:S(2)}) async-start(f32[32,16,128]{2,1,0:T(8,128)} %copy-done.4), calls=%async_computation.4 | async-start | bytes 524288 | tf_op jit(solution)/shard_map/all_to_all | solution.py:52
  140.4 9.1 %all-to-all-done.4.inbox_ref = f32[32,16,128]{2,1,0:T(8,128)S(1)} async-done(((f32[32,16,128]{2,1,0:T(8,128)}), f32[32,16,128]{2,1,0:T(8,128)S(1)}, u32[]{:S(2)}, u32[]{:S(2)}) %all-to-all-start.4) | async-done | bytes 262176 | tf_op jit(solution)/shard_map/all_to_all | solution.py:52
  149.5 0.9 copy-done.6
  150.4 0.9 copy-done.8
  151.3 0.3 rows.1
  151.6 0.0 copy-start.3
  151.6 1.2 copy-done.3
  152.8 3.7 %all-to-all-start.5 = ((bf16[16,8,6144]{2,1,0:T(8,128)(2,1)}), bf16[16,8,6144]{2,1,0:T(8,128)(2,1)S(1)}, u32[]{:S(2)}, u32[]{:S(2)}) async-start(bf16[16,8,6144]{2,1,0:T(8,128)(2,1)} %copy-done.3), calls=%async_computation.5 | async-start | bytes 3145728 | tf_op jit(solution)/shard_map/all_to_all | solution.py:52
  156.6 0.0 copy-start.1
  156.6 0.5 fusion
  157.1 0.8 copy-done.1
  158.0 0.5 convolution_add_fusion
  158.5 0.1 reshape.84
  158.6 0.1 reduce_sum.19
  158.7 0.5 slice.7
  159.8 0.0 copy-done.9
  159.8 0.0 copy-done.10
  159.8 0.0 copy-done.11
  159.9 0.8 multiply_subtract_fusion
  160.7 22.5 %all-to-all-done.5.rows_ref = bf16[16,8,6144]{2,1,0:T(8,128)(2,1)S(1)} async-done(((bf16[16,8,6144]{2,1,0:T(8,128)(2,1)}), bf16[16,8,6144]{2,1,0:T(8,128)(2,1)S(1)}, u32[]{:S(2)}, u32[]{:S(2)}) %all-to-all-start.5) | async-done | bytes 1572896 | tf_op jit(solution)/shard_map/all_to_all | solution.py:52
  183.2 2.8 %collective-permute-start.7 = (bf16[16,8,6144]{2,1,0:T(8,128)(2,1)S(1)}, bf16[16,8,6144]{2,1,0:T(8,128)(2,1)S(1)}, u32[]{:S(2)}, u32[]{:S(2)}) collective-permute-start(bf16[16,8,6144]{2,1,0:T(8,128)(2,1)S(1)} %all-to-all-done.5.rows_ref), channel_id=1, source_target_pairs={{0,1},{1,0},{2,3},{3,2},{4,5},{5,4},{6,7},{7,6},{8,9},{9,8},{10,11... | collective-permute-start | bytes 4718600 | tf_op jit(solution)/shard_map/ppermute | solution.py:60
  186.0 1.3 place.2.refs_0_
  187.2 1.7 collective-permute-done.7.rows_ref
  189.0 1.3 place.3
  (16 shorter events, 0.1 us)
Async XLA Ops:
  0.6 64.2 %collective-permute-start = (bf16[256,6144]{1,0:T(8,128)(2,1)}, bf16[256,6144]{1,0:T(8,128)(2,1)}, u32[]{:S(2)}, u32[]{:S(2)}) collective-permute-start(bf16[256,6144]{1,0:T(8,128)(2,1)} %bitcast.45), channel_id=1, source_target_pairs={{0,1},{1,0},{2,3},{3,2},{4,5},{5,4},{6,7},{7,6},{8,9},{9,8},{10,11... | collective-permute-start | bytes 9437192 | tf_op jit(solution)/shard_map/ppermute | solution.py:60
  10.2 4.5 %collective-permute-start.1 = (bf16[96,128]{1,0:T(8,128)(2,1)S(1)}, bf16[96,128]{1,0:T(8,128)(2,1)S(1)}, u32[]{:S(2)}, u32[]{:S(2)}) collective-permute-start(bf16[96,128]{1,0:T(8,128)(2,1)S(1)} %get-tuple-element.52), channel_id=1, source_target_pairs={{0,1},{1,0},{2,3},{3,2},{4,5},{5,4},{6,7},{7,6},{8,9},{9,8},{10,11... | collective-permute-start | bytes 73736 | tf_op jit(solution)/shard_map/ppermute | solution.py:60
  37.5 26.8 %all-to-all-start.1 = ((bf16[16,16,24,128]{3,2,1,0:T(8,128)(2,1)}), bf16[16,16,24,128]{3,2,1,0:T(8,128)(2,1)S(1)}, u32[]{:S(2)}, u32[]{:S(2)}) async-start(bf16[16,16,24,128]{3,2,1,0:T(8,128)(2,1)} %broadcast_in_dim.62), calls=%async_computation.1 | async-start | bytes 3145728 | tf_op jit(solution)/shard_map/all_to_all | solution.py:52
  46.0 15.8 %collective-permute-start.3 = (bf16[12,6144]{1,0:T(8,128)(2,1)}, bf16[12,6144]{1,0:T(8,128)(2,1)S(1)}, u32[]{:S(2)}, u32[]{:S(2)}) collective-permute-start(bf16[12,6144]{1,0:T(8,128)(2,1)} %pack.1), channel_id=1, source_target_pairs={{0,16},{1,17},{2,14},{3,15},{4,12},{5,13},{6,10},{7,11},{8,8},{9,9... | collective-permute-start | bytes 442376 | tf_op jit(solution)/shard_map/ppermute | solution.py:237
  51.5 10.3 %collective-permute-start.2 = (bf16[12,6144]{1,0:T(8,128)(2,1)}, bf16[12,6144]{1,0:T(8,128)(2,1)}, u32[]{:S(2)}, u32[]{:S(2)}) collective-permute-start(bf16[12,6144]{1,0:T(8,128)(2,1)} %pack.1), channel_id=1, source_target_pairs={{0,0},{1,1},{2,30},{3,31},{4,28},{5,29},{6,26},{7,27},{8,24},{9,25... | collective-permute-start | bytes 442376 | tf_op jit(solution)/shard_map/ppermute | solution.py:236
  64.4 1.9 copy-start.2
  70.6 27.6 %all-to-all-start.2 = ((f32[16,16,128]{2,1,0:T(8,128)}), f32[16,16,128]{2,1,0:T(8,128)S(1)}, u32[]{:S(2)}, u32[]{:S(2)}) async-start(f32[16,16,128]{2,1,0:T(8,128)} %bitcast.10), calls=%async_computation.2 | async-start | bytes 262144 | tf_op jit(solution)/shard_map/all_to_all | solution.py:52
  91.2 33.7 %collective-permute-start.4 = (bf16[6144,128]{1,0:T(8,128)(2,1)S(1)}, bf16[6144,128]{1,0:T(8,128)(2,1)S(1)}, u32[]{:S(2)}, u32[]{:S(2)}) collective-permute-start(bf16[6144,128]{1,0:T(8,128)(2,1)S(1)} %bitcast.42), channel_id=1, source_target_pairs={{0,1},{1,0},{2,3},{3,2},{4,5},{5,4},{6,7},{7,6},{8,9},{9,8},{10,11... | collective-permute-start | bytes 4718600 | tf_op jit(solution)/shard_map/ppermute | solution.py:60
  98.9 26.0 %all-to-all-start.3 = ((f32[32,8,128]{2,1,0:T(8,128)}), f32[32,8,128]{2,1,0:T(8,128)S(1)}, u32[]{:S(2)}, u32[]{:S(2)}) async-start(f32[32,8,128]{2,1,0:T(8,128)} %bitcast.12), calls=%async_computation.3 | async-start | bytes 262144 | tf_op jit(solution)/shard_map/all_to_all | solution.py:52
  110.2 8.2 %collective-permute-start.6 = (bf16[12,6144]{1,0:T(8,128)(2,1)}, bf16[12,6144]{1,0:T(8,128)(2,1)S(1)}, u32[]{:S(2)}, u32[]{:S(2)}) collective-permute-start(bf16[12,6144]{1,0:T(8,128)(2,1)} %get-tuple-element.49), channel_id=1, source_target_pairs={{0,256},{1,0},{2,195},{3,451},{4,196},{5,452},{6,135},{7,391},{8,1... | collective-permute-start | bytes 442376 | tf_op jit(solution)/shard_map/ppermute | solution.py:258
  112.4 9.8 %collective-permute-start.5 = (bf16[12,6144]{1,0:T(8,128)(2,1)}, bf16[12,6144]{1,0:T(8,128)(2,1)}, u32[]{:S(2)}, u32[]{:S(2)}) collective-permute-start(bf16[12,6144]{1,0:T(8,128)(2,1)} %get-tuple-element.50), channel_id=1, source_target_pairs={{0,0},{1,256},{2,451},{3,195},{4,452},{5,196},{6,391},{7,135},{8,3... | collective-permute-start | bytes 442376 | tf_op jit(solution)/shard_map/ppermute | solution.py:257
  124.9 2.2 %copy-start = (bf16[6144,128]{1,0:T(8,128)(2,1)}, bf16[6144,128]{1,0:T(8,128)(2,1)S(1)}, u32[]{:S(2)}) copy-start(bf16[6144,128]{1,0:T(8,128)(2,1)S(1)} %collective-permute-done.4.other_ref) | copy-start | bytes 4718596
  127.1 0.7 copy-start.4
  127.9 0.7 copy-start.5
  128.5 0.7 copy-start.7
  129.2 20.3 %all-to-all-start.4 = ((f32[32,16,128]{2,1,0:T(8,128)}), f32[32,16,128]{2,1,0:T(8,128)S(1)}, u32[]{:S(2)}, u32[]{:S(2)}) async-start(f32[32,16,128]{2,1,0:T(8,128)} %copy-done.4), calls=%async_computation.4 | async-start | bytes 524288 | tf_op jit(solution)/shard_map/all_to_all | solution.py:52
  149.5 0.9 copy-start.6
  150.4 0.9 copy-start.8
  151.6 1.2 copy-start.3
  152.8 30.4 %all-to-all-start.5 = ((bf16[16,8,6144]{2,1,0:T(8,128)(2,1)}), bf16[16,8,6144]{2,1,0:T(8,128)(2,1)S(1)}, u32[]{:S(2)}, u32[]{:S(2)}) async-start(bf16[16,8,6144]{2,1,0:T(8,128)(2,1)} %copy-done.3), calls=%async_computation.5 | async-start | bytes 3145728 | tf_op jit(solution)/shard_map/all_to_all | solution.py:52
  156.6 1.4 copy-start.1
  158.0 1.9 copy-start.9
  158.0 1.9 copy-start.10
  158.0 1.9 copy-start.11
  183.2 5.8 %collective-permute-start.7 = (bf16[16,8,6144]{2,1,0:T(8,128)(2,1)S(1)}, bf16[16,8,6144]{2,1,0:T(8,128)(2,1)S(1)}, u32[]{:S(2)}, u32[]{:S(2)}) collective-permute-start(bf16[16,8,6144]{2,1,0:T(8,128)(2,1)S(1)} %all-to-all-done.5.rows_ref), channel_id=1, source_target_pairs={{0,1},{1,0},{2,3},{3,2},{4,5},{5,4},{6,7},{7,6},{8,9},{9,8},{10,11... | collective-permute-start | bytes 4718600 | tf_op jit(solution)/shard_map/ppermute | solution.py:60

commit v7 on v6

--- a/solution.py
+++ b/solution.py
@@ -36,8 +36,8 @@
     return pairs
 
 
-def along_z_moves(offset):
-    return moves(lambda o, z, c: (o, (o + offset - z) % 16, c))
+def along_z_moves(first):
+    return moves(lambda o, z, c: (o, (o + 8 * ((c + first) % 2) - z) % 16, c))
 
 
 def in_plane_moves(first):
@@ -233,11 +233,10 @@
         out_specs=VMEM,
         name="pack",
     )(m_in, v_in, w_in)
-    state_a = lax.ppermute(state, ALL, along_z_moves(0))
-    state_b = lax.ppermute(state, ALL, along_z_moves(8))
+    came_one = lax.ppermute(state, ALL, along_z_moves(0))
     other_grad = swap(grad)
     blocks = share(along_z, PLANE, 16)
-    blocks, state_a, state_b = lax.optimization_barrier((blocks, state_a, state_b))
+    blocks, came_one = lax.optimization_barrier((blocks, came_one))
     blocks = blocks.reshape(2, 8, 16, part, half)
     own_basis = blocks.transpose(0, 2, 1, 3, 4).reshape(width, half)
 
@@ -249,13 +248,16 @@
         compiler_params=LIMIT,
         name="product",
     )(grad, other_grad, own_basis)
-    sketch, basis_sent = lax.optimization_barrier((sketch, own_basis))
+    sketch, basis_sent, state, came_one = lax.optimization_barrier(
+        (sketch, own_basis, state, came_one)
+    )
+    came_two = lax.ppermute(state, ALL, along_z_moves(1))
+    state_one = lax.ppermute(came_one, ALL, in_plane_moves(0))
     other_basis = swap(basis_sent)
     plane_terms = exchange(sketch.reshape(16, 16, half), PLANE)
+    plane_terms, came_two = lax.optimization_barrier((plane_terms, came_two))
     plane_sum = jnp.sum(plane_terms, axis=0)
-    plane_sum, state_a, state_b = lax.optimization_barrier((plane_sum, state_a, state_b))
-    state_one = lax.ppermute(jnp.where(core == 0, state_a, state_b), ALL, in_plane_moves(0))
-    state_two = lax.ppermute(jnp.where(core == 0, state_b, state_a), ALL, in_plane_moves(1))
+    state_two = lax.ppermute(came_two, ALL, in_plane_moves(1))
     spread = jnp.broadcast_to(plane_sum.reshape(2, 1, 8, half), (2, 16, 8, half))
     terms = exchange(spread.reshape(32, 8, half), ("c", "z"))
 

time: 193 us -> 187 us (0.969); the launches traced: 190 us -> 186 us
  starting transfers between devices: 82.7 us -> 62.5 us
  blocking collectives: 21.2 us -> 37 us
  waiting for transfers between devices: 58.2 us -> 60.9 us
    all_to_all x5 -> x4, starting transfers between devices: 52 us -> 31.8 us  [exchange(): return lax.all_to_all(blocks, axes, 0, 0, tiled=True)]
    all_to_all x1 -> x2, blocking collectives: 21.2 us -> 37 us  [exchange(): return lax.all_to_all(blocks, axes, 0, 0, tiled=True)]
    ppermute x4, waiting for transfers between devices: 13 us -> 18.2 us  [the longest x1 12.6 us: on_device(): came_one = lax.ppermute(state, ALL, along_z_moves(0))]
    ppermute x4, starting transfers between devices: 14.5 us -> 10.7 us  [the longest x1 5.52 us: on_device(): came_one = lax.ppermute(state, ALL, along_z_moves(0))]
    ppermute x4, starting transfers between devices: 16.2 us -> 20 us  [swap(): return lax.ppermute(block, 'c', SWAP)]
    all_to_all x5 -> x4, waiting for transfers between devices: 41 us -> 38.6 us  [exchange(): return lax.all_to_all(blocks, axes, 0, 0, tiled=True)]
    unnamed x24 -> x26, local copies, waits for them, and re-layouts: 7.42 us -> 7.42 us
  transfers between devices with their start and end apart: 13 -> 12, of which waited for: 10 -> 9; matrix products, arithmetic and copies ran while one was open for 4% -> 3% of each run, Pallas kernels for 2% -> 2%
where the time goes in v7:
time: 187 us; the launch traced here: 186 us
  starting transfers between devices  62.5 us (33%)
  waiting for transfers between devices  60.9 us (33%)
  blocking collectives  37 us (20%)
  local copies, waits for them, and re-layouts  11.6 us (6%)
  Pallas kernels  10.5 us (6%)
    all_to_all x4, waiting for transfers between devices, exchange(): return lax.all_to_all(blocks, axes, 0, 0, tiled=True)  38.6 us
    all_to_all x2, blocking collectives, exchange(): return lax.all_to_all(blocks, axes, 0, 0, tiled=True)  37 us
    all_to_all x4, starting transfers between devices, exchange(): return lax.all_to_all(blocks, axes, 0, 0, tiled=True)  31.8 us
    ppermute x4, starting transfers between devices, swap(): return lax.ppermute(block, 'c', SWAP)  20 us
    ppermute x1, waiting for transfers between devices, on_device(): came_one = lax.ppermute(state, ALL, along_z_moves(0))  12.6 us
    unnamed x26, local copies, waits for them, and re-layouts  7.42 us
    ppermute x1, starting transfers between devices, on_device(): came_one = lax.ppermute(state, ALL, along_z_moves(0))  5.52 us
    ppermute x1, waiting for transfers between devices, on_device(): state_one = lax.ppermute(came_one, ALL, in_plane_moves(0))  4.22 us
  transfers between devices with their start and end apart: 12, of which 9 were waited for; matrix products, arithmetic and copies ran while one was open for 3% of the time, Pallas kernels for 2%

profile of v7, /device:TPU:1, one launch (start us, length us, event | category | flops | bytes accessed | tf_op | source)
XLA Modules:
  0.0 186.3 jit_solution(6574206618252299461)
XLA Ops:
  0.6 8.8 %collective-permute-start = (bf16[256,6144]{1,0:T(8,128)(2,1)}, bf16[256,6144]{1,0:T(8,128)(2,1)}, u32[]{:S(2)}, u32[]{:S(2)}) collective-permute-start(bf16[256,6144]{1,0:T(8,128)(2,1)} %bitcast.45), channel_id=1, source_target_pairs={{0,1},{1,0},{2,3},{3,2},{4,5},{5,4},{6,7},{7,6},{8,9},{9,8},{10,11... | collective-permute-start | bytes 9437192 | tf_op jit(solution)/shard_map/ppermute | solution.py:60
  9.4 0.8 dynamic-slice_bitcast_fusion.1
  10.2 1.9 %collective-permute-start.1 = (bf16[96,128]{1,0:T(8,128)(2,1)S(1)}, bf16[96,128]{1,0:T(8,128)(2,1)S(1)}, u32[]{:S(2)}, u32[]{:S(2)}) collective-permute-start(bf16[96,128]{1,0:T(8,128)(2,1)S(1)} %get-tuple-element.50), channel_id=1, source_target_pairs={{0,1},{1,0},{2,3},{3,2},{4,5},{5,4},{6,7},{7,6},{8,9},{9,8},{10,11... | collective-permute-start | bytes 73736 | tf_op jit(solution)/shard_map/ppermute | solution.py:60
  12.1 0.1 broadcast_in_dim.54
  12.2 0.1 broadcast_in_dim.55
  12.3 0.1 dynamic-slice.8
  12.4 2.3 %collective-permute-done.1 = bf16[96,128]{1,0:T(8,128)(2,1)S(1)} collective-permute-done((bf16[96,128]{1,0:T(8,128)(2,1)S(1)}, bf16[96,128]{1,0:T(8,128)(2,1)S(1)}, u32[]{:S(2)}, u32[]{:S(2)}) %collective-permute-start.1) | collective-permute-done | bytes 24608 | tf_op jit(solution)/shard_map/ppermute | solution.py:60
  14.7 0.1 dynamic-slice_select_fusion
  14.8 21.2 %all_to_all.30 = bf16[16,24,128]{2,1,0:T(8,128)(2,1)S(1)} all-to-all(bf16[16,24,128]{2,1,0:T(8,128)(2,1)S(1)} %broadcast_in_dim.61), channel_id=1, replica_groups=mesh['yh'=2,'x'=4,'yl'=2,'z'=16,'c'=2] {'z'}, dimensions={0} | all-to-all | bytes 196608 | tf_op jit(solution)/shard_map/all_to_all | solution.py:52
  36.1 1.4 broadcast_in_dim.62
  37.5 6.8 %all-to-all-start.1 = ((bf16[16,16,24,128]{3,2,1,0:T(8,128)(2,1)}), bf16[16,16,24,128]{3,2,1,0:T(8,128)(2,1)S(1)}, u32[]{:S(2)}, u32[]{:S(2)}) async-start(bf16[16,16,24,128]{3,2,1,0:T(8,128)(2,1)} %broadcast_in_dim.62), calls=%async_computation.1 | async-start | bytes 3145728 | tf_op jit(solution)/shard_map/all_to_all | solution.py:52
  44.3 1.7 pack.1
  46.0 5.5 %collective-permute-start.2 = (bf16[12,6144]{1,0:T(8,128)(2,1)}, bf16[12,6144]{1,0:T(8,128)(2,1)}, u32[]{:S(2)}, u32[]{:S(2)}) collective-permute-start(bf16[12,6144]{1,0:T(8,128)(2,1)} %pack.1), channel_id=1, source_target_pairs={{0,0},{1,17},{2,30},{3,15},{4,28},{5,13},{6,26},{7,11},{8,24},{9,9... | collective-permute-start | bytes 442376 | tf_op jit(solution)/shard_map/ppermute | solution.py:236
  51.5 12.6 %collective-permute-done.2 = bf16[12,6144]{1,0:T(8,128)(2,1)} collective-permute-done((bf16[12,6144]{1,0:T(8,128)(2,1)}, bf16[12,6144]{1,0:T(8,128)(2,1)}, u32[]{:S(2)}, u32[]{:S(2)}) %collective-permute-start.2) | collective-permute-done | bytes 147488 | tf_op jit(solution)/shard_map/ppermute | solution.py:236
  64.1 0.3 all-to-all-done.1
  64.4 0.0 copy-start.2
  64.4 0.4 copy.10
  64.8 0.0 collective-permute-done.other_ref
  64.8 1.5 copy-done.2
  66.3 3.7 %product.1 = f32[256,128]{1,0:T(8,128)S(1)} custom-call(bf16[256,6144]{1,0:T(8,128)(2,1)S(1)} %bitcast.46, bf16[256,6144]{1,0:T(8,128)(2,1)} %collective-permute-done.other_ref, bf16[6144,128]{1,0:T(8,128)(2,1)S(1)} %bitcast.41), custom_call_target="tpu_custom_call" | custom-call | tf_op jit(solution)/shard_map/product/pallas_call | solution.py:243
  70.0 6.6 %collective-permute-start.4 = (bf16[6144,128]{1,0:T(8,128)(2,1)S(1)}, bf16[6144,128]{1,0:T(8,128)(2,1)S(1)}, u32[]{:S(2)}, u32[]{:S(2)}) collective-permute-start(bf16[6144,128]{1,0:T(8,128)(2,1)S(1)} %bitcast.42), channel_id=1, source_target_pairs={{0,1},{1,0},{2,3},{3,2},{4,5},{5,4},{6,7},{7,6},{8,9},{9,8},{10,11... | collective-permute-start | bytes 4718600 | tf_op jit(solution)/shard_map/ppermute | solution.py:60
  76.5 0.0 copy-done.12
  76.6 1.4 collective-permute-start.3
  77.9 15.8 %all_to_all.31 = f32[16,16,128]{2,1,0:T(8,128)S(1)} all-to-all(f32[16,16,128]{2,1,0:T(8,128)S(1)} %bitcast.47), channel_id=1, replica_groups=mesh['yh'=2,'x'=4,'yl'=2,'z'=16,'c'=2] {'yl','yh','x'}, dimensions={0} | all-to-all | bytes 262144 | tf_op jit(solution)/shard_map/all_to_all | solution.py:52
  93.7 0.0 collective-permute-done.3
  93.7 0.7 broadcast_in_dim.64
  94.4 10.8 %all-to-all-start.3 = ((f32[32,8,128]{2,1,0:T(8,128)}), f32[32,8,128]{2,1,0:T(8,128)S(1)}, u32[]{:S(2)}, u32[]{:S(2)}) async-start(f32[32,8,128]{2,1,0:T(8,128)} %bitcast.12), calls=%async_computation.3 | async-start | bytes 262144 | tf_op jit(solution)/shard_map/all_to_all | solution.py:52
  105.2 1.9 %collective-permute-start.5 = (bf16[12,6144]{1,0:T(8,128)(2,1)}, bf16[12,6144]{1,0:T(8,128)(2,1)S(1)}, u32[]{:S(2)}, u32[]{:S(2)}) collective-permute-start(bf16[12,6144]{1,0:T(8,128)(2,1)} %collective-permute-done.2), channel_id=1, source_target_pairs={{0,0},{1,256},{2,451},{3,195},{4,452},{5,196},{6,391},{7,135},{8,3... | collective-permute-start | bytes 442376 | tf_op jit(solution)/shard_map/ppermute | solution.py:255
  107.1 1.9 %collective-permute-start.6 = (bf16[12,6144]{1,0:T(8,128)(2,1)}, bf16[12,6144]{1,0:T(8,128)(2,1)}, u32[]{:S(2)}, u32[]{:S(2)}) collective-permute-start(bf16[12,6144]{1,0:T(8,128)(2,1)} %collective-permute-done.3), channel_id=1, source_target_pairs={{0,256},{1,0},{2,195},{3,451},{4,196},{5,452},{6,135},{7,391},{8,1... | collective-permute-start | bytes 442376 | tf_op jit(solution)/shard_map/ppermute | solution.py:260
  109.1 0.1 pad_add_fusion.at_ref
  109.2 4.2 %collective-permute-done.5.one_ref = bf16[12,6144]{1,0:T(8,128)(2,1)S(1)} collective-permute-done((bf16[12,6144]{1,0:T(8,128)(2,1)}, bf16[12,6144]{1,0:T(8,128)(2,1)S(1)}, u32[]{:S(2)}, u32[]{:S(2)}) %collective-permute-start.5) | collective-permute-done | bytes 147488 | tf_op jit(solution)/shard_map/ppermute | solution.py:255
  113.4 1.4 collective-permute-done.6.two_ref
  114.8 6.8 %all-to-all-done.3.terms_ref = f32[32,8,128]{2,1,0:T(8,128)S(1)} async-done(((f32[32,8,128]{2,1,0:T(8,128)}), f32[32,8,128]{2,1,0:T(8,128)S(1)}, u32[]{:S(2)}, u32[]{:S(2)}) %all-to-all-start.3) | async-done | bytes 131104 | tf_op jit(solution)/shard_map/all_to_all | solution.py:52
  121.6 0.0 collective-permute-done.4.other_ref
  121.6 2.2 %update.1 = (f32[8,6144]{1,0:T(8,128)S(1)}, f32[8,6144]{1,0:T(8,128)S(1)}, f32[32,16,128]{2,1,0:T(8,128)S(1)}) custom-call(s32[2]{0:T(128)S(1)} %pad_add_fusion.at_ref, f32[32,8,128]{2,1,0:T(8,128)S(1)} %all-to-all-done.3.terms_ref, bf16[6144,128]{1,0:T(8,128)(2,1)S(1)} %bitcast.43, bf16[6144,128]{1,0:T(8,128)(2,1)S(1)} %collective-permute-done.4.other_ref, ...), custom_call_target="tpu_custom_call" | custom-call | tf_op jit(solution)/shard_map/update/pallas_call | solution.py:265
  123.8 0.0 copy-done
  123.8 0.0 copy-start.4
  123.8 0.7 copy-done.4
  124.5 0.7 copy-done.5
  125.2 0.7 copy-done.7
  125.9 10.5 %all-to-all-start.4 = ((f32[32,16,128]{2,1,0:T(8,128)}), f32[32,16,128]{2,1,0:T(8,128)S(1)}, u32[]{:S(2)}, u32[]{:S(2)}) async-start(f32[32,16,128]{2,1,0:T(8,128)} %copy-done.4), calls=%async_computation.4 | async-start | bytes 524288 | tf_op jit(solution)/shard_map/all_to_all | solution.py:52
  136.4 9.1 %all-to-all-done.4.inbox_ref = f32[32,16,128]{2,1,0:T(8,128)S(1)} async-done(((f32[32,16,128]{2,1,0:T(8,128)}), f32[32,16,128]{2,1,0:T(8,128)S(1)}, u32[]{:S(2)}, u32[]{:S(2)}) %all-to-all-start.4) | async-done | bytes 262176 | tf_op jit(solution)/shard_map/all_to_all | solution.py:52
  145.5 0.9 copy-done.6
  146.4 0.9 copy-done.8
  147.4 0.3 rows.1
  147.7 0.0 copy-start.3
  147.7 1.2 copy-done.3
  148.8 3.7 %all-to-all-start.5 = ((bf16[16,8,6144]{2,1,0:T(8,128)(2,1)}), bf16[16,8,6144]{2,1,0:T(8,128)(2,1)S(1)}, u32[]{:S(2)}, u32[]{:S(2)}) async-start(bf16[16,8,6144]{2,1,0:T(8,128)(2,1)} %copy-done.3), calls=%async_computation.5 | async-start | bytes 3145728 | tf_op jit(solution)/shard_map/all_to_all | solution.py:52
  152.6 0.0 copy-start.1
  152.6 0.5 fusion
  153.1 0.8 copy-done.1
  154.0 0.5 convolution_add_fusion
  154.5 0.1 reshape.84
  154.6 0.1 reduce_sum.19
  154.7 0.5 slice.7
  155.8 0.0 copy-done.9
  155.8 0.0 copy-done.10
  155.8 0.0 copy-done.11
  155.9 0.8 multiply_subtract_fusion
  156.7 22.5 %all-to-all-done.5.rows_ref = bf16[16,8,6144]{2,1,0:T(8,128)(2,1)S(1)} async-done(((bf16[16,8,6144]{2,1,0:T(8,128)(2,1)}), bf16[16,8,6144]{2,1,0:T(8,128)(2,1)S(1)}, u32[]{:S(2)}, u32[]{:S(2)}) %all-to-all-start.5) | async-done | bytes 1572896 | tf_op jit(solution)/shard_map/all_to_all | solution.py:52
  179.2 2.8 %collective-permute-start.7 = (bf16[16,8,6144]{2,1,0:T(8,128)(2,1)S(1)}, bf16[16,8,6144]{2,1,0:T(8,128)(2,1)S(1)}, u32[]{:S(2)}, u32[]{:S(2)}) collective-permute-start(bf16[16,8,6144]{2,1,0:T(8,128)(2,1)S(1)} %all-to-all-done.5.rows_ref), channel_id=1, source_target_pairs={{0,1},{1,0},{2,3},{3,2},{4,5},{5,4},{6,7},{7,6},{8,9},{9,8},{10,11... | collective-permute-start | bytes 4718600 | tf_op jit(solution)/shard_map/ppermute | solution.py:60
  182.0 1.3 place.2.refs_0_
  183.2 1.7 collective-permute-done.7.rows_ref
  185.0 1.3 place.3
  (16 shorter events, 0.1 us)
Async XLA Ops:
  0.6 64.2 %collective-permute-start = (bf16[256,6144]{1,0:T(8,128)(2,1)}, bf16[256,6144]{1,0:T(8,128)(2,1)}, u32[]{:S(2)}, u32[]{:S(2)}) collective-permute-start(bf16[256,6144]{1,0:T(8,128)(2,1)} %bitcast.45), channel_id=1, source_target_pairs={{0,1},{1,0},{2,3},{3,2},{4,5},{5,4},{6,7},{7,6},{8,9},{9,8},{10,11... | collective-permute-start | bytes 9437192 | tf_op jit(solution)/shard_map/ppermute | solution.py:60
  10.2 4.5 %collective-permute-start.1 = (bf16[96,128]{1,0:T(8,128)(2,1)S(1)}, bf16[96,128]{1,0:T(8,128)(2,1)S(1)}, u32[]{:S(2)}, u32[]{:S(2)}) collective-permute-start(bf16[96,128]{1,0:T(8,128)(2,1)S(1)} %get-tuple-element.50), channel_id=1, source_target_pairs={{0,1},{1,0},{2,3},{3,2},{4,5},{5,4},{6,7},{7,6},{8,9},{9,8},{10,11... | collective-permute-start | bytes 73736 | tf_op jit(solution)/shard_map/ppermute | solution.py:60
  37.5 26.8 %all-to-all-start.1 = ((bf16[16,16,24,128]{3,2,1,0:T(8,128)(2,1)}), bf16[16,16,24,128]{3,2,1,0:T(8,128)(2,1)S(1)}, u32[]{:S(2)}, u32[]{:S(2)}) async-start(bf16[16,16,24,128]{3,2,1,0:T(8,128)(2,1)} %broadcast_in_dim.62), calls=%async_computation.1 | async-start | bytes 3145728 | tf_op jit(solution)/shard_map/all_to_all | solution.py:52
  46.0 18.1 %collective-permute-start.2 = (bf16[12,6144]{1,0:T(8,128)(2,1)}, bf16[12,6144]{1,0:T(8,128)(2,1)}, u32[]{:S(2)}, u32[]{:S(2)}) collective-permute-start(bf16[12,6144]{1,0:T(8,128)(2,1)} %pack.1), channel_id=1, source_target_pairs={{0,0},{1,17},{2,30},{3,15},{4,28},{5,13},{6,26},{7,11},{8,24},{9,9... | collective-permute-start | bytes 442376 | tf_op jit(solution)/shard_map/ppermute | solution.py:236
  64.4 1.9 %copy-start.2 = (bf16[1,1,1,256,6144]{4,3,2,1,0:T(8,128)(2,1)S(1)}, bf16[1,1,1,256,6144]{4,3,2,1,0:T(8,128)(2,1)}, u32[]{:S(2)}) copy-start(bf16[1,1,1,256,6144]{4,3,2,1,0:T(8,128)(2,1)} %param.5) | copy-start | bytes 9437188
  66.3 10.3 %copy-start.12 = (bf16[12,6144]{1,0:T(8,128)(2,1)S(1)}, bf16[12,6144]{1,0:T(8,128)(2,1)}, u32[]{:S(2)}) copy-start(bf16[12,6144]{1,0:T(8,128)(2,1)} %pack.1) | copy-start | bytes 442372
  70.0 51.6 %collective-permute-start.4 = (bf16[6144,128]{1,0:T(8,128)(2,1)S(1)}, bf16[6144,128]{1,0:T(8,128)(2,1)S(1)}, u32[]{:S(2)}, u32[]{:S(2)}) collective-permute-start(bf16[6144,128]{1,0:T(8,128)(2,1)S(1)} %bitcast.42), channel_id=1, source_target_pairs={{0,1},{1,0},{2,3},{3,2},{4,5},{5,4},{6,7},{7,6},{8,9},{9,8},{10,11... | collective-permute-start | bytes 4718600 | tf_op jit(solution)/shard_map/ppermute | solution.py:60
  76.6 17.2 %collective-permute-start.3 = (bf16[12,6144]{1,0:T(8,128)(2,1)S(1)}, bf16[12,6144]{1,0:T(8,128)(2,1)}, u32[]{:S(2)}, u32[]{:S(2)}) collective-permute-start(bf16[12,6144]{1,0:T(8,128)(2,1)S(1)} %copy-done.12), channel_id=1, source_target_pairs={{0,16},{1,1},{2,14},{3,31},{4,12},{5,29},{6,10},{7,27},{8,8},{9,25... | collective-permute-start | bytes 442376 | tf_op jit(solution)/shard_map/ppermute | solution.py:254
  94.4 27.2 %all-to-all-start.3 = ((f32[32,8,128]{2,1,0:T(8,128)}), f32[32,8,128]{2,1,0:T(8,128)S(1)}, u32[]{:S(2)}, u32[]{:S(2)}) async-start(f32[32,8,128]{2,1,0:T(8,128)} %bitcast.12), calls=%async_computation.3 | async-start | bytes 262144 | tf_op jit(solution)/shard_map/all_to_all | solution.py:52
  105.2 8.2 %collective-permute-start.5 = (bf16[12,6144]{1,0:T(8,128)(2,1)}, bf16[12,6144]{1,0:T(8,128)(2,1)S(1)}, u32[]{:S(2)}, u32[]{:S(2)}) collective-permute-start(bf16[12,6144]{1,0:T(8,128)(2,1)} %collective-permute-done.2), channel_id=1, source_target_pairs={{0,0},{1,256},{2,451},{3,195},{4,452},{5,196},{6,391},{7,135},{8,3... | collective-permute-start | bytes 442376 | tf_op jit(solution)/shard_map/ppermute | solution.py:255
  107.1 7.7 %collective-permute-start.6 = (bf16[12,6144]{1,0:T(8,128)(2,1)}, bf16[12,6144]{1,0:T(8,128)(2,1)}, u32[]{:S(2)}, u32[]{:S(2)}) collective-permute-start(bf16[12,6144]{1,0:T(8,128)(2,1)} %collective-permute-done.3), channel_id=1, source_target_pairs={{0,256},{1,0},{2,195},{3,451},{4,196},{5,452},{6,135},{7,391},{8,1... | collective-permute-start | bytes 442376 | tf_op jit(solution)/shard_map/ppermute | solution.py:260
  121.6 2.2 %copy-start = (bf16[6144,128]{1,0:T(8,128)(2,1)}, bf16[6144,128]{1,0:T(8,128)(2,1)S(1)}, u32[]{:S(2)}) copy-start(bf16[6144,128]{1,0:T(8,128)(2,1)S(1)} %collective-permute-done.4.other_ref) | copy-start | bytes 4718596
  123.8 0.7 copy-start.4
  124.5 0.7 copy-start.5
  125.2 0.7 copy-start.7
  125.9 19.6 %all-to-all-start.4 = ((f32[32,16,128]{2,1,0:T(8,128)}), f32[32,16,128]{2,1,0:T(8,128)S(1)}, u32[]{:S(2)}, u32[]{:S(2)}) async-start(f32[32,16,128]{2,1,0:T(8,128)} %copy-done.4), calls=%async_computation.4 | async-start | bytes 524288 | tf_op jit(solution)/shard_map/all_to_all | solution.py:52
  145.5 0.9 copy-start.6
  146.4 0.9 copy-start.8
  147.7 1.2 copy-start.3
  148.8 30.4 %all-to-all-start.5 = ((bf16[16,8,6144]{2,1,0:T(8,128)(2,1)}), bf16[16,8,6144]{2,1,0:T(8,128)(2,1)S(1)}, u32[]{:S(2)}, u32[]{:S(2)}) async-start(bf16[16,8,6144]{2,1,0:T(8,128)(2,1)} %copy-done.3), calls=%async_computation.5 | async-start | bytes 3145728 | tf_op jit(solution)/shard_map/all_to_all | solution.py:52
  152.6 1.4 copy-start.1
  154.0 1.9 %copy-start.9 = (f32[1,4,6144]{2,1,0:T(4,128)S(1)}, f32[1,4,6144]{2,1,0:T(4,128)}, u32[]{:S(2)}) copy-start(f32[1,4,6144]{2,1,0:T(4,128)} %weights_ref) | copy-start | bytes 294916
  154.0 1.9 %copy-start.10 = (f32[1,4,6144]{2,1,0:T(4,128)S(1)}, f32[1,4,6144]{2,1,0:T(4,128)}, u32[]{:S(2)}) copy-start(f32[1,4,6144]{2,1,0:T(4,128)} %moment_ref) | copy-start | bytes 294916
  154.0 1.9 %copy-start.11 = (f32[1,4,6144]{2,1,0:T(4,128)S(1)}, f32[1,4,6144]{2,1,0:T(4,128)}, u32[]{:S(2)}) copy-start(f32[1,4,6144]{2,1,0:T(4,128)} %second_ref) | copy-start | bytes 294916
  179.2 5.8 %collective-permute-start.7 = (bf16[16,8,6144]{2,1,0:T(8,128)(2,1)S(1)}, bf16[16,8,6144]{2,1,0:T(8,128)(2,1)S(1)}, u32[]{:S(2)}, u32[]{:S(2)}) collective-permute-start(bf16[16,8,6144]{2,1,0:T(8,128)(2,1)S(1)} %all-to-all-done.5.rows_ref), channel_id=1, source_target_pairs={{0,1},{1,0},{2,3},{3,2},{4,5},{5,4},{6,7},{7,6},{8,9},{9,8},{10,11... | collective-permute-start | bytes 4718600 | tf_op jit(solution)/shard_map/ppermute | solution.py:60

commit v8 on v7

--- a/solution.py
+++ b/solution.py
@@ -1,3 +1,5 @@
+import functools
+
 import jax
 import jax.numpy as jnp
 from jax import lax
@@ -65,28 +67,6 @@
     shape[axis] = 2
     here = (jnp.arange(2) == position).reshape(shape)
     return jnp.where(here, jnp.expand_dims(mine, axis), jnp.expand_dims(other, axis))
-
-
-def pieces(values, count):
-    parts = []
-    rest = values
-    for _ in range(count):
-        part = lax.reduce_precision(rest, 8, 7)
-        parts.append(part.astype(jnp.bfloat16))
-        rest = rest - part
-    return jnp.concatenate(parts, axis=0)
-
-
-def estimate_rows(halves, core, own_basis, other_basis, count):
-    rows = halves.shape[1]
-    total = 0.0
-    for half, basis in ((core, own_basis), (1 - core, other_basis)):
-        left = pieces(lax.dynamic_index_in_dim(halves, half, 0, keepdims=False), count)
-        total = total + lax.dot_general(
-            left, basis, (((1,), (1,)), ((), ())), preferred_element_type=jnp.float32
-        )
-    total = total.reshape(count, rows, -1)
-    return jnp.sum(total, axis=0) / 256
 
 
 def moments(estimate, weights, moment, second):
@@ -166,7 +146,18 @@
             message_ref[2 * place + core, 8:16, :] = notes
 
 
-def rows_kernel(inbox_ref, update_ref, kept_ref, rows_ref, ratio_ref):
+def rows_kernel(
+    at_ref, inbox_ref, update_ref, kept_ref, rows_ref, ratio_ref, own_left_ref, other_left_ref
+):
+    sketch = inbox_ref[at_ref[2], 0:8, :]
+    swapped = jnp.concatenate([sketch[4:8], sketch[0:4]], axis=0)
+    mine_first = jnp.where(at_ref[0] == 0, sketch, swapped)
+    high = mine_first.astype(jnp.bfloat16).astype(jnp.float32)
+    rest = mine_first - high
+    middle = rest.astype(jnp.bfloat16).astype(jnp.float32)
+    parts = (high, middle, rest - middle)
+    for ref, rows in ((own_left_ref, slice(0, 4)), (other_left_ref, slice(4, 8))):
+        ref[...] = jnp.concatenate([p[rows] for p in parts], axis=0).astype(jnp.bfloat16)
     notes = inbox_ref[0, 8:16, :]
     for source in range(1, 32):
         notes = notes + inbox_ref[source, 8:16, :]
@@ -182,10 +173,10 @@
             rows_ref[place, :, part] = rows
 
 
-def place_kernel(at_ref, rows_ref, *refs):
+def place_kernel(which, at_ref, rows_ref, *refs):
     out_ref, sems = refs[-2:]
     copies = [
-        pltpu.make_async_copy(rows_ref.at[i], out_ref.at[i, at_ref[0]], sems.at[i])
+        pltpu.make_async_copy(rows_ref.at[i], out_ref.at[i, at_ref[which]], sems.at[i])
         for i in range(16)
     ]
     for copy in copies:
@@ -194,10 +185,10 @@
         copy.wait()
 
 
-def place(at, rows, *partly):
+def place(which, at, rows, *partly):
     shape = (16, 2) + rows.shape[1:]
     return pl.pallas_call(
-        place_kernel,
+        functools.partial(place_kernel, which),
         out_shape=jax.ShapeDtypeStruct(shape, rows.dtype),
         in_specs=[SMEM, VMEM] + [pl.BlockSpec(memory_space=pl.ANY)] * len(partly),
         out_specs=pl.BlockSpec(memory_space=pl.ANY),
@@ -224,6 +215,8 @@
     chip = in_order(core, mine, theirs, 0).reshape(-1, half)
     part = chip.shape[0] // 8
     piece = lax.dynamic_slice_in_dim(chip, part * outer, part, 0)
+    at = jnp.stack([core, (2 * outer + core + deep) % 16 // 8, low * 16 + deep, 1 - core])
+    piece, at = lax.optimization_barrier((piece, at.astype(jnp.int32)))
     along_z = share(piece, "z", 16)
     along_z, m_in, v_in, w_in = lax.optimization_barrier((along_z, moment, second, weights))
     state = pl.pallas_call(
@@ -231,6 +224,7 @@
         out_shape=jax.ShapeDtypeStruct((12, width), jnp.bfloat16),
         in_specs=[VMEM, VMEM, VMEM],
         out_specs=VMEM,
+        compiler_params=LIMIT,
         name="pack",
     )(m_in, v_in, w_in)
     came_one = lax.ppermute(state, ALL, along_z_moves(0))
@@ -248,14 +242,14 @@
         compiler_params=LIMIT,
         name="product",
     )(grad, other_grad, own_basis)
-    sketch, basis_sent, state, came_one = lax.optimization_barrier(
-        (sketch, own_basis, state, came_one)
-    )
+    sketch, state, came_one = lax.optimization_barrier((sketch, state, came_one))
     came_two = lax.ppermute(state, ALL, along_z_moves(1))
     state_one = lax.ppermute(came_one, ALL, in_plane_moves(0))
+    plane_terms = exchange(sketch.reshape(16, 16, half), PLANE)
+    plane_terms, came_two, basis_sent = lax.optimization_barrier(
+        (plane_terms, came_two, own_basis)
+    )
     other_basis = swap(basis_sent)
-    plane_terms = exchange(sketch.reshape(16, 16, half), PLANE)
-    plane_terms, came_two = lax.optimization_barrier((plane_terms, came_two))
     plane_sum = jnp.sum(plane_terms, axis=0)
     state_two = lax.ppermute(came_two, ALL, in_plane_moves(1))
     spread = jnp.broadcast_to(plane_sum.reshape(2, 1, 8, half), (2, 16, 8, half))
@@ -270,7 +264,7 @@
         compiler_params=LIMIT,
         name="update",
     )(
-        jnp.stack([core, (2 * outer + core + deep) % 16 // 8]).astype(jnp.int32),
+        at,
         terms,
         own_basis,
         other_basis,
@@ -278,30 +272,36 @@
         state_two,
     )
     inbox = exchange(message, PLANE + ("c",))
-    rows_out, ratio = pl.pallas_call(
+    left = jax.ShapeDtypeStruct((12, half), jnp.bfloat16)
+    rows_out, ratio, own_left, other_left = pl.pallas_call(
         rows_kernel,
         out_shape=(
             jax.ShapeDtypeStruct((16, 8, width), jnp.bfloat16),
             jax.ShapeDtypeStruct((8, 128), jnp.float32),
+            left,
+            left,
         ),
-        in_specs=[VMEM, VMEM, VMEM],
-        out_specs=(VMEM, VMEM),
+        in_specs=[SMEM, VMEM, VMEM, VMEM],
+        out_specs=(VMEM, VMEM, VMEM, VMEM),
         compiler_params=LIMIT,
         name="rows",
-    )(inbox, update8, kept8)
+    )(at, inbox, update8, kept8)
     rows_mine = exchange(rows_out, PLANE)
+    rows_mine, ratio, own_left, other_left = lax.optimization_barrier(
+        (rows_mine, ratio, own_left, other_left)
+    )
+    rows_other = swap(rows_mine)
+    gathered = place(3, at, rows_other, place(0, at, rows_mine)).reshape(1, 256, width)
 
     trust_ratio = ratio[0, 0]
-    own = lax.dynamic_index_in_dim(inbox, low * 16 + deep, 0, keepdims=False)[:8]
-    estimate = estimate_rows(own.reshape(2, 4, half), core, own_basis, other_basis, 3)[None]
+    turn = (((1,), (1,)), ((), ()))
+    estimate = lax.dot_general(own_left, own_basis, turn, preferred_element_type=jnp.float32)
+    estimate = estimate + lax.dot_general(
+        other_left, other_basis, turn, preferred_element_type=jnp.float32
+    )
+    estimate = (estimate[0:4] + estimate[4:8] + estimate[8:12])[None] / 256
     moment_new, second_new, update = moments(estimate, weights, moment, second)
     weight_new = weights - rate * trust_ratio * update
-    rows_mine, weight_new, moment_new, second_new = lax.optimization_barrier(
-        (rows_mine, weight_new, moment_new, second_new)
-    )
-    rows_other = swap(rows_mine)
-    core_at = core.astype(jnp.int32).reshape(1)
-    gathered = place(1 - core_at, rows_other, place(core_at, rows_mine)).reshape(1, 256, width)
     return (weight_new, moment_new, second_new, gathered)
 
 

time: 187 us -> 180 us (0.963)
  blocking collectives: 37 us -> 83.9 us
  waiting for transfers between devices: 60.9 us -> 27.2 us
  starting transfers between devices: 62.5 us -> 45.9 us
  local copies, waits for them, and re-layouts: 11.6 us -> 9.22 us
    all_to_all x2 -> x4, blocking collectives: 37 us -> 83.9 us  [exchange(): return lax.all_to_all(blocks, axes, 0, 0, tiled=True)]
    all_to_all x4 -> x2, waiting for transfers between devices: 38.6 us -> 4.63 us  [exchange(): return lax.all_to_all(blocks, axes, 0, 0, tiled=True)]
    all_to_all x4 -> x2, starting transfers between devices: 31.8 us -> 15 us  [exchange(): return lax.all_to_all(blocks, axes, 0, 0, tiled=True)]
    unnamed x26 -> x20, local copies, waits for them, and re-layouts: 7.42 us -> 3.58 us
  transfers between devices with their start and end apart: 12 -> 10, of which waited for: 9 -> 6; matrix products, arithmetic and copies ran while one was open for 3% -> 4% of each run, Pallas kernels for 2% -> 1%
where the time goes in v8:
time: 180 us
  blocking collectives  83.9 us (47%)
  starting transfers between devices  45.9 us (26%)
  waiting for transfers between devices  27.2 us (15%)
  Pallas kernels  9.83 us (5%)
  local copies, waits for them, and re-layouts  9.22 us (5%)
    all_to_all x4, blocking collectives, exchange(): return lax.all_to_all(blocks, axes, 0, 0, tiled=True)  83.9 us
    ppermute x4, starting transfers between devices, swap(): return lax.ppermute(block, 'c', SWAP)  19.5 us
    all_to_all x2, starting transfers between devices, exchange(): return lax.all_to_all(blocks, axes, 0, 0, tiled=True)  15 us
    ppermute x1, waiting for transfers between devices, on_device(): came_one = lax.ppermute(state, ALL, along_z_moves(0))  12.3 us
    ppermute x1, starting transfers between devices, on_device(): came_one = lax.ppermute(state, ALL, along_z_moves(0))  5.53 us
    ppermute x1, waiting for transfers between devices, on_device(): state_one = lax.ppermute(came_one, ALL, in_plane_moves(0))  5.03 us
    all_to_all x2, waiting for transfers between devices, exchange(): return lax.all_to_all(blocks, axes, 0, 0, tiled=True)  4.63 us
    pallas_call x1, Pallas kernels, on_device(): pl.pallas_call(product_kernel, out_shape=jax.ShapeDtypeStruct((grad.shape...  3.7 us
  transfers between devices with their start and end apart: 10, of which 6 were waited for; matrix products, arithmetic and copies ran while one was open for 4% of the time, Pallas kernels for 1%

profile of v8, /device:TPU:1, one launch (start us, length us, event | category | flops | bytes accessed | tf_op | source)
XLA Modules:
  0.0 179.7 jit_solution(14469879822723266003)
XLA Ops:
  0.6 8.8 %collective-permute-start.1 = (bf16[256,6144]{1,0:T(8,128)(2,1)}, bf16[256,6144]{1,0:T(8,128)(2,1)}, u32[]{:S(2)}, u32[]{:S(2)}) collective-permute-start(bf16[256,6144]{1,0:T(8,128)(2,1)} %bitcast.34), channel_id=1, source_target_pairs={{0,1},{1,0},{2,3},{3,2},{4,5},{5,4},{6,7},{7,6},{8,9},{9,8},{10,11... | collective-permute-start | bytes 9437192 | tf_op jit(solution)/shard_map/ppermute | solution.py:62
  9.4 0.8 dynamic-slice_bitcast_fusion.1
  10.2 1.9 %collective-permute-start = (bf16[96,128]{1,0:T(8,128)(2,1)S(1)}, bf16[96,128]{1,0:T(8,128)(2,1)S(1)}, u32[]{:S(2)}, u32[]{:S(2)}) collective-permute-start(bf16[96,128]{1,0:T(8,128)(2,1)S(1)} %get-tuple-element.58), channel_id=1, source_target_pairs={{0,1},{1,0},{2,3},{3,2},{4,5},{5,4},{6,7},{7,6},{8,9},{9,8},{10,11... | collective-permute-start | bytes 73736 | tf_op jit(solution)/shard_map/ppermute | solution.py:62
  12.2 0.1 pad_add_fusion.at_ref
  12.3 0.1 broadcast_in_dim.54
  12.3 0.1 broadcast_in_dim.55
  12.4 0.1 dynamic-slice.8
  12.5 2.2 %collective-permute-done = bf16[96,128]{1,0:T(8,128)(2,1)S(1)} collective-permute-done((bf16[96,128]{1,0:T(8,128)(2,1)S(1)}, bf16[96,128]{1,0:T(8,128)(2,1)S(1)}, u32[]{:S(2)}, u32[]{:S(2)}) %collective-permute-start) | collective-permute-done | bytes 24608 | tf_op jit(solution)/shard_map/ppermute | solution.py:62
  14.7 0.1 dynamic-slice_select_fusion
  14.8 21.2 %all_to_all.30 = bf16[16,24,128]{2,1,0:T(8,128)(2,1)S(1)} all-to-all(bf16[16,24,128]{2,1,0:T(8,128)(2,1)S(1)} %broadcast_in_dim.61), channel_id=1, replica_groups=mesh['yh'=2,'x'=4,'yl'=2,'z'=16,'c'=2] {'z'}, dimensions={0} | all-to-all | bytes 196608 | tf_op jit(solution)/shard_map/all_to_all | solution.py:54
  36.1 1.4 broadcast_in_dim.62
  37.5 0.0 copy-start.1
  37.5 0.0 copy-start.2
  37.5 0.0 copy-start.3
  37.5 6.9 %all-to-all-start.1 = ((bf16[16,16,24,128]{3,2,1,0:T(8,128)(2,1)}), bf16[16,16,24,128]{3,2,1,0:T(8,128)(2,1)}, u32[]{:S(2)}, u32[]{:S(2)}) async-start(bf16[16,16,24,128]{3,2,1,0:T(8,128)(2,1)} %broadcast_in_dim.62), calls=%async_computation.1 | async-start | bytes 3145728 | tf_op jit(solution)/shard_map/all_to_all | solution.py:54
  44.5 0.0 copy-done.1
  44.5 0.0 copy-done.2
  44.5 0.0 copy-done.3
  44.5 5.5 %collective-permute-start.2 = (bf16[12,6144]{1,0:T(8,128)(2,1)S(1)}, bf16[12,6144]{1,0:T(8,128)(2,1)S(1)}, u32[]{:S(2)}, u32[]{:S(2)}) collective-permute-start(bf16[12,6144]{1,0:T(8,128)(2,1)S(1)} %pack.1), channel_id=1, source_target_pairs={{0,0},{1,17},{2,30},{3,15},{4,28},{5,13},{6,26},{7,11},{8,24},{9,9... | collective-permute-start | bytes 442376 | tf_op jit(solution)/shard_map/ppermute | solution.py:230
  50.1 12.3 %collective-permute-done.2 = bf16[12,6144]{1,0:T(8,128)(2,1)S(1)} collective-permute-done((bf16[12,6144]{1,0:T(8,128)(2,1)S(1)}, bf16[12,6144]{1,0:T(8,128)(2,1)S(1)}, u32[]{:S(2)}, u32[]{:S(2)}) %collective-permute-start.2) | collective-permute-done | bytes 147488 | tf_op jit(solution)/shard_map/ppermute | solution.py:230
  62.4 0.0 copy-start.9
  62.4 2.2 %all-to-all-done.1 = bf16[16,16,24,128]{3,2,1,0:T(8,128)(2,1)} async-done(((bf16[16,16,24,128]{3,2,1,0:T(8,128)(2,1)}), bf16[16,16,24,128]{3,2,1,0:T(8,128)(2,1)}, u32[]{:S(2)}, u32[]{:S(2)}) %all-to-all-start.1) | async-done | bytes 1572896 | tf_op jit(solution)/shard_map/all_to_all | solution.py:54
  64.6 0.0 copy-done.9
  64.6 0.0 copy-start
  64.6 2.0 %copy.10 = bf16[2,16,8,24,128]{4,3,2,1,0:T(8,128)(2,1)S(1)} copy(bf16[2,16,8,24,128]{4,3,1,2,0:T(8,128)(2,1)} %bitcast.10) | data formatting | bytes 3145728 | tf_op jit(solution)/shard_map/transpose | solution.py:235
  66.6 0.0 collective-permute-done.1.other_ref
  66.6 0.4 copy-done
  67.0 3.7 %product.1 = f32[256,128]{1,0:T(8,128)S(1)} custom-call(bf16[256,6144]{1,0:T(8,128)(2,1)S(1)} %bitcast.35, bf16[256,6144]{1,0:T(8,128)(2,1)} %collective-permute-done.1.other_ref, bf16[6144,128]{1,0:T(8,128)(2,1)S(1)} %bitcast.30), custom_call_target="tpu_custom_call" | custom-call | tf_op jit(solution)/shard_map/product/pallas_call | solution.py:237
  70.7 1.3 collective-permute-start.3
  72.0 17.4 %all_to_all.31 = f32[16,16,128]{2,1,0:T(8,128)S(1)} all-to-all(f32[16,16,128]{2,1,0:T(8,128)S(1)} %bitcast.36), channel_id=1, replica_groups=mesh['yh'=2,'x'=4,'yl'=2,'z'=16,'c'=2] {'yl','yh','x'}, dimensions={0} | all-to-all | bytes 262144 | tf_op jit(solution)/shard_map/all_to_all | solution.py:54
  89.4 0.0 collective-permute-done.3
  89.4 5.6 %collective-permute-start.4 = (bf16[6144,128]{1,0:T(8,128)(2,1)S(1)}, bf16[6144,128]{1,0:T(8,128)(2,1)S(1)}, u32[]{:S(2)}, u32[]{:S(2)}) collective-permute-start(bf16[6144,128]{1,0:T(8,128)(2,1)S(1)} %bitcast.31), channel_id=1, source_target_pairs={{0,1},{1,0},{2,3},{3,2},{4,5},{5,4},{6,7},{7,6},{8,9},{9,8},{10,11... | collective-permute-start | bytes 4718600 | tf_op jit(solution)/shard_map/ppermute | solution.py:62
  95.0 0.6 broadcast_in_dim.64
  95.6 8.1 %all-to-all-start.3 = ((f32[32,8,128]{2,1,0:T(8,128)}), f32[32,8,128]{2,1,0:T(8,128)S(1)}, u32[]{:S(2)}, u32[]{:S(2)}) async-start(f32[32,8,128]{2,1,0:T(8,128)} %bitcast.38), calls=%async_computation.3 | async-start | bytes 262144 | tf_op jit(solution)/shard_map/all_to_all | solution.py:54
  103.7 2.6 %collective-permute-start.5 = (bf16[12,6144]{1,0:T(8,128)(2,1)}, bf16[12,6144]{1,0:T(8,128)(2,1)S(1)}, u32[]{:S(2)}, u32[]{:S(2)}) collective-permute-start(bf16[12,6144]{1,0:T(8,128)(2,1)} %copy-done.9), channel_id=1, source_target_pairs={{0,0},{1,256},{2,451},{3,195},{4,452},{5,196},{6,391},{7,135},{8,3... | collective-permute-start | bytes 442376 | tf_op jit(solution)/shard_map/ppermute | solution.py:247
  106.3 1.9 %collective-permute-start.6 = (bf16[12,6144]{1,0:T(8,128)(2,1)}, bf16[12,6144]{1,0:T(8,128)(2,1)S(1)}, u32[]{:S(2)}, u32[]{:S(2)}) collective-permute-start(bf16[12,6144]{1,0:T(8,128)(2,1)} %collective-permute-done.3), channel_id=1, source_target_pairs={{0,256},{1,0},{2,195},{3,451},{4,196},{5,452},{6,135},{7,391},{8,1... | collective-permute-start | bytes 442376 | tf_op jit(solution)/shard_map/ppermute | solution.py:254
  108.3 5.0 %collective-permute-done.5.one_ref = bf16[12,6144]{1,0:T(8,128)(2,1)S(1)} collective-permute-done((bf16[12,6144]{1,0:T(8,128)(2,1)}, bf16[12,6144]{1,0:T(8,128)(2,1)S(1)}, u32[]{:S(2)}, u32[]{:S(2)}) %collective-permute-start.5) | collective-permute-done | bytes 147488 | tf_op jit(solution)/shard_map/ppermute | solution.py:247
  113.3 0.0 copy-start.5
  113.3 0.7 copy-done.5
  114.0 3.0 %collective-permute-done.6.two_ref = bf16[12,6144]{1,0:T(8,128)(2,1)S(1)} collective-permute-done((bf16[12,6144]{1,0:T(8,128)(2,1)}, bf16[12,6144]{1,0:T(8,128)(2,1)S(1)}, u32[]{:S(2)}, u32[]{:S(2)}) %collective-permute-start.6) | collective-permute-done | bytes 147488 | tf_op jit(solution)/shard_map/ppermute | solution.py:254
  117.0 0.0 copy-start.7
  117.0 0.7 copy-done.7
  117.7 2.4 %all-to-all-done.3.terms_ref = f32[32,8,128]{2,1,0:T(8,128)S(1)} async-done(((f32[32,8,128]{2,1,0:T(8,128)}), f32[32,8,128]{2,1,0:T(8,128)S(1)}, u32[]{:S(2)}, u32[]{:S(2)}) %all-to-all-start.3) | async-done | bytes 131104 | tf_op jit(solution)/shard_map/all_to_all | solution.py:54
  120.1 0.0 collective-permute-done.4.other_ref
  120.1 0.0 copy-start.6
  120.1 0.9 copy-done.6
  121.0 0.0 copy-start.8
  121.0 0.9 copy-done.8
  121.9 1.6 update.1
  123.6 20.0 %all_to_all.32.inbox_ref = f32[32,16,128]{2,1,0:T(8,128)S(1)} all-to-all(f32[32,16,128]{2,1,0:T(8,128)S(1)} %get-tuple-element.43), channel_id=1, replica_groups=mesh['yh'=2,'x'=4,'yl'=2,'z'=16,'c'=2] {'yl','yh','x','c'}, dimensions={0} | all-to-all | bytes 524288 | tf_op jit(solution)/shard_map/all_to_all | solution.py:54
  143.6 0.8 rows.1
  144.5 25.3 %all_to_all.33.rows_ref = bf16[16,8,6144]{2,1,0:T(8,128)(2,1)S(1)} all-to-all(bf16[16,8,6144]{2,1,0:T(8,128)(2,1)S(1)} %get-tuple-element.46), channel_id=1, replica_groups=mesh['yh'=2,'x'=4,'yl'=2,'z'=16,'c'=2] {'yl','yh','x'}, dimensions={0} | all-to-all | bytes 3145728 | tf_op jit(solution)/shard_map/all_to_all | solution.py:54
  169.7 3.3 %collective-permute-start.7 = (bf16[16,8,6144]{2,1,0:T(8,128)(2,1)S(1)}, bf16[16,8,6144]{2,1,0:T(8,128)(2,1)S(1)}, u32[]{:S(2)}, u32[]{:S(2)}) collective-permute-start(bf16[16,8,6144]{2,1,0:T(8,128)(2,1)S(1)} %all_to_all.33.rows_ref), channel_id=1, source_target_pairs={{0,1},{1,0},{2,3},{3,2},{4,5},{5,4},{6,7},{7,6},{8,9},{9,8},{10,11... | collective-permute-start | bytes 4718600 | tf_op jit(solution)/shard_map/ppermute | solution.py:62
  173.0 1.8 %place.2.refs_0_ = bf16[16,2,8,6144]{3,2,1,0:T(8,128)(2,1)} custom-call(s32[4]{0:T(128)S(1)} %pad_add_fusion.at_ref, bf16[16,8,6144]{2,1,0:T(8,128)(2,1)S(1)} %all_to_all.33.rows_ref), custom_call_target="tpu_custom_call" | custom-call | bytes 3145728 | tf_op jit(solution)/shard_map/place/pallas_call | solution.py:190
  174.8 0.5 fusion
  175.3 0.0 copy-start.4
  175.3 0.5 slice.12
  176.5 0.5 convolution_add_fusion
  177.0 0.0 copy-done.4
  177.0 0.9 multiply_subtract_fusion
  177.9 0.0 collective-permute-done.7.rows_ref
  177.9 1.8 %place.3 = bf16[16,2,8,6144]{3,2,1,0:T(8,128)(2,1)} custom-call(s32[4]{0:T(128)S(1)} %pad_add_fusion.at_ref, bf16[16,8,6144]{2,1,0:T(8,128)(2,1)S(1)} %collective-permute-done.7.rows_ref, bf16[16,2,8,6144]{3,2,1,0:T(8,128)(2,1)} %place.2.refs_0_), custom_call_target="tpu_custom_call", output_to_operand_aliasing={{}: (2, {})} | custom-call | bytes 3145728 | tf_op jit(solution)/shard_map/place/pallas_call | solution.py:190
  (6 shorter events, 0.1 us)
Async XLA Ops:
  0.6 66.0 %collective-permute-start.1 = (bf16[256,6144]{1,0:T(8,128)(2,1)}, bf16[256,6144]{1,0:T(8,128)(2,1)}, u32[]{:S(2)}, u32[]{:S(2)}) collective-permute-start(bf16[256,6144]{1,0:T(8,128)(2,1)} %bitcast.34), channel_id=1, source_target_pairs={{0,1},{1,0},{2,3},{3,2},{4,5},{5,4},{6,7},{7,6},{8,9},{9,8},{10,11... | collective-permute-start | bytes 9437192 | tf_op jit(solution)/shard_map/ppermute | solution.py:62
  10.2 4.5 %collective-permute-start = (bf16[96,128]{1,0:T(8,128)(2,1)S(1)}, bf16[96,128]{1,0:T(8,128)(2,1)S(1)}, u32[]{:S(2)}, u32[]{:S(2)}) collective-permute-start(bf16[96,128]{1,0:T(8,128)(2,1)S(1)} %get-tuple-element.58), channel_id=1, source_target_pairs={{0,1},{1,0},{2,3},{3,2},{4,5},{5,4},{6,7},{7,6},{8,9},{9,8},{10,11... | collective-permute-start | bytes 73736 | tf_op jit(solution)/shard_map/ppermute | solution.py:62
  37.5 6.9 %copy-start.1 = (f32[1,4,6144]{2,1,0:T(4,128)S(1)}, f32[1,4,6144]{2,1,0:T(4,128)}, u32[]{:S(2)}) copy-start(f32[1,4,6144]{2,1,0:T(4,128)} %weights_ref) | copy-start | bytes 294916
  37.5 7.0 %copy-start.2 = (f32[1,4,6144]{2,1,0:T(4,128)S(1)}, f32[1,4,6144]{2,1,0:T(4,128)}, u32[]{:S(2)}) copy-start(f32[1,4,6144]{2,1,0:T(4,128)} %moment_ref) | copy-start | bytes 294916
  37.5 7.0 %copy-start.3 = (f32[1,4,6144]{2,1,0:T(4,128)S(1)}, f32[1,4,6144]{2,1,0:T(4,128)}, u32[]{:S(2)}) copy-start(f32[1,4,6144]{2,1,0:T(4,128)} %second_ref) | copy-start | bytes 294916
  37.5 27.1 %all-to-all-start.1 = ((bf16[16,16,24,128]{3,2,1,0:T(8,128)(2,1)}), bf16[16,16,24,128]{3,2,1,0:T(8,128)(2,1)}, u32[]{:S(2)}, u32[]{:S(2)}) async-start(bf16[16,16,24,128]{3,2,1,0:T(8,128)(2,1)} %broadcast_in_dim.62), calls=%async_computation.1 | async-start | bytes 3145728 | tf_op jit(solution)/shard_map/all_to_all | solution.py:54
  44.5 17.8 %collective-permute-start.2 = (bf16[12,6144]{1,0:T(8,128)(2,1)S(1)}, bf16[12,6144]{1,0:T(8,128)(2,1)S(1)}, u32[]{:S(2)}, u32[]{:S(2)}) collective-permute-start(bf16[12,6144]{1,0:T(8,128)(2,1)S(1)} %pack.1), channel_id=1, source_target_pairs={{0,0},{1,17},{2,30},{3,15},{4,28},{5,13},{6,26},{7,11},{8,24},{9,9... | collective-permute-start | bytes 442376 | tf_op jit(solution)/shard_map/ppermute | solution.py:230
  62.4 2.3 %copy-start.9 = (bf16[12,6144]{1,0:T(8,128)(2,1)}, bf16[12,6144]{1,0:T(8,128)(2,1)S(1)}, u32[]{:S(2)}) copy-start(bf16[12,6144]{1,0:T(8,128)(2,1)S(1)} %collective-permute-done.2) | copy-start | bytes 442372
  64.6 2.4 %copy-start = (bf16[1,1,1,256,6144]{4,3,2,1,0:T(8,128)(2,1)S(1)}, bf16[1,1,1,256,6144]{4,3,2,1,0:T(8,128)(2,1)}, u32[]{:S(2)}) copy-start(bf16[1,1,1,256,6144]{4,3,2,1,0:T(8,128)(2,1)} %param.5) | copy-start | bytes 9437188
  70.7 18.7 %collective-permute-start.3 = (bf16[12,6144]{1,0:T(8,128)(2,1)S(1)}, bf16[12,6144]{1,0:T(8,128)(2,1)}, u32[]{:S(2)}, u32[]{:S(2)}) collective-permute-start(bf16[12,6144]{1,0:T(8,128)(2,1)S(1)} %pack.1), channel_id=1, source_target_pairs={{0,16},{1,1},{2,14},{3,31},{4,12},{5,29},{6,10},{7,27},{8,8},{9,25... | collective-permute-start | bytes 442376 | tf_op jit(solution)/shard_map/ppermute | solution.py:246
  89.4 30.7 %collective-permute-start.4 = (bf16[6144,128]{1,0:T(8,128)(2,1)S(1)}, bf16[6144,128]{1,0:T(8,128)(2,1)S(1)}, u32[]{:S(2)}, u32[]{:S(2)}) collective-permute-start(bf16[6144,128]{1,0:T(8,128)(2,1)S(1)} %bitcast.31), channel_id=1, source_target_pairs={{0,1},{1,0},{2,3},{3,2},{4,5},{5,4},{6,7},{7,6},{8,9},{9,8},{10,11... | collective-permute-start | bytes 4718600 | tf_op jit(solution)/shard_map/ppermute | solution.py:62
  95.6 24.4 %all-to-all-start.3 = ((f32[32,8,128]{2,1,0:T(8,128)}), f32[32,8,128]{2,1,0:T(8,128)S(1)}, u32[]{:S(2)}, u32[]{:S(2)}) async-start(f32[32,8,128]{2,1,0:T(8,128)} %bitcast.38), calls=%async_computation.3 | async-start | bytes 262144 | tf_op jit(solution)/shard_map/all_to_all | solution.py:54
  103.7 9.6 %collective-permute-start.5 = (bf16[12,6144]{1,0:T(8,128)(2,1)}, bf16[12,6144]{1,0:T(8,128)(2,1)S(1)}, u32[]{:S(2)}, u32[]{:S(2)}) collective-permute-start(bf16[12,6144]{1,0:T(8,128)(2,1)} %copy-done.9), channel_id=1, source_target_pairs={{0,0},{1,256},{2,451},{3,195},{4,452},{5,196},{6,391},{7,135},{8,3... | collective-permute-start | bytes 442376 | tf_op jit(solution)/shard_map/ppermute | solution.py:247
  106.3 10.7 %collective-permute-start.6 = (bf16[12,6144]{1,0:T(8,128)(2,1)}, bf16[12,6144]{1,0:T(8,128)(2,1)S(1)}, u32[]{:S(2)}, u32[]{:S(2)}) collective-permute-start(bf16[12,6144]{1,0:T(8,128)(2,1)} %collective-permute-done.3), channel_id=1, source_target_pairs={{0,256},{1,0},{2,195},{3,451},{4,196},{5,452},{6,135},{7,391},{8,1... | collective-permute-start | bytes 442376 | tf_op jit(solution)/shard_map/ppermute | solution.py:254
  113.3 0.7 copy-start.5
  117.0 0.7 copy-start.7
  120.1 0.9 copy-start.6
  121.0 0.9 copy-start.8
  169.7 8.2 %collective-permute-start.7 = (bf16[16,8,6144]{2,1,0:T(8,128)(2,1)S(1)}, bf16[16,8,6144]{2,1,0:T(8,128)(2,1)S(1)}, u32[]{:S(2)}, u32[]{:S(2)}) collective-permute-start(bf16[16,8,6144]{2,1,0:T(8,128)(2,1)S(1)} %all_to_all.33.rows_ref), channel_id=1, source_target_pairs={{0,1},{1,0},{2,3},{3,2},{4,5},{5,4},{6,7},{7,6},{8,9},{9,8},{10,11... | collective-permute-start | bytes 4718600 | tf_op jit(solution)/shard_map/ppermute | solution.py:62
  175.3 1.7 copy-start.4

commit v9 on v8

--- a/solution.py
+++ b/solution.py
@@ -21,6 +21,7 @@
 OUTER = ("yh", "x")
 DP = ("yl", "z", "c")
 PLANE = ("yl", "yh", "x")
+X_FIRST = ("x", "yh", "yl")
 SWAP = [(0, 1), (1, 0)]
 ALL = tuple(FINE)
 
@@ -176,7 +177,11 @@
 def place_kernel(which, at_ref, rows_ref, *refs):
     out_ref, sems = refs[-2:]
     copies = [
-        pltpu.make_async_copy(rows_ref.at[i], out_ref.at[i, at_ref[which]], sems.at[i])
+        pltpu.make_async_copy(
+            rows_ref.at[i],
+            out_ref.at[i % 2 * 8 + i // 2 % 2 * 4 + i // 4, at_ref[which]],
+            sems.at[i],
+        )
         for i in range(16)
     ]
     for copy in copies:
@@ -229,10 +234,10 @@
     )(m_in, v_in, w_in)
     came_one = lax.ppermute(state, ALL, along_z_moves(0))
     other_grad = swap(grad)
-    blocks = share(along_z, PLANE, 16)
+    blocks = share(along_z, X_FIRST, 16)
     blocks, came_one = lax.optimization_barrier((blocks, came_one))
-    blocks = blocks.reshape(2, 8, 16, part, half)
-    own_basis = blocks.transpose(0, 2, 1, 3, 4).reshape(width, half)
+    blocks = blocks.reshape(4, 2, 2, 16, part, half)
+    own_basis = blocks.transpose(2, 3, 1, 0, 4, 5).reshape(width, half)
 
     sketch = pl.pallas_call(
         product_kernel,
@@ -286,7 +291,7 @@
         compiler_params=LIMIT,
         name="rows",
     )(at, inbox, update8, kept8)
-    rows_mine = exchange(rows_out, PLANE)
+    rows_mine = exchange(rows_out, X_FIRST)
     rows_mine, ratio, own_left, other_left = lax.optimization_barrier(
         (rows_mine, ratio, own_left, other_left)
     )

time: 180 us -> 180 us (level)
  blocking collectives: 83.9 us -> 79.8 us
  starting transfers between devices: 45.9 us -> 48.5 us
    all_to_all x4, blocking collectives: 83.9 us -> 79.8 us  [exchange(): return lax.all_to_all(blocks, axes, 0, 0, tiled=True)]
    ppermute x4, starting transfers between devices: 19.5 us -> 21.7 us  [swap(): return lax.ppermute(block, 'c', SWAP)]
where the time goes in v9:
time: 180 us; the launch traced here: 178 us
  blocking collectives  79.8 us (44%)
  starting transfers between devices  48.5 us (27%)
  waiting for transfers between devices  27.1 us (15%)
  Pallas kernels  9.83 us (5%)
  local copies, waits for them, and re-layouts  9.22 us (5%)
    all_to_all x4, blocking collectives, exchange(): return lax.all_to_all(blocks, axes, 0, 0, tiled=True)  79.8 us
    ppermute x4, starting transfers between devices, swap(): return lax.ppermute(block, 'c', SWAP)  21.7 us
    all_to_all x2, starting transfers between devices, exchange(): return lax.all_to_all(blocks, axes, 0, 0, tiled=True)  15.6 us
    ppermute x1, waiting for transfers between devices, on_device(): came_one = lax.ppermute(state, ALL, along_z_moves(0))  12.3 us
    ppermute x1, starting transfers between devices, on_device(): came_one = lax.ppermute(state, ALL, along_z_moves(0))  5.53 us
    ppermute x1, waiting for transfers between devices, on_device(): state_one = lax.ppermute(came_one, ALL, in_plane_moves(0))  5.12 us
    all_to_all x2, waiting for transfers between devices, exchange(): return lax.all_to_all(blocks, axes, 0, 0, tiled=True)  4.59 us
    pallas_call x1, Pallas kernels, on_device(): pl.pallas_call(product_kernel, out_shape=jax.ShapeDtypeStruct((grad.shape...  3.7 us
  transfers between devices with their start and end apart: 10, of which 6 were waited for; matrix products, arithmetic and copies ran while one was open for 4% of the time, Pallas kernels for 1%

profile of v9, /device:TPU:1, one launch (start us, length us, event | category | flops | bytes accessed | tf_op | source)
XLA Modules:
  0.0 178.1 jit_solution(16377508151781652074)
XLA Ops:
  0.6 8.8 %collective-permute-start.1 = (bf16[256,6144]{1,0:T(8,128)(2,1)}, bf16[256,6144]{1,0:T(8,128)(2,1)}, u32[]{:S(2)}, u32[]{:S(2)}) collective-permute-start(bf16[256,6144]{1,0:T(8,128)(2,1)} %bitcast.34), channel_id=1, source_target_pairs={{0,1},{1,0},{2,3},{3,2},{4,5},{5,4},{6,7},{7,6},{8,9},{9,8},{10,11... | collective-permute-start | bytes 9437192 | tf_op jit(solution)/shard_map/ppermute | solution.py:63
  9.4 0.8 dynamic-slice_bitcast_fusion.1
  10.2 1.9 %collective-permute-start = (bf16[96,128]{1,0:T(8,128)(2,1)S(1)}, bf16[96,128]{1,0:T(8,128)(2,1)S(1)}, u32[]{:S(2)}, u32[]{:S(2)}) collective-permute-start(bf16[96,128]{1,0:T(8,128)(2,1)S(1)} %get-tuple-element.58), channel_id=1, source_target_pairs={{0,1},{1,0},{2,3},{3,2},{4,5},{5,4},{6,7},{7,6},{8,9},{9,8},{10,11... | collective-permute-start | bytes 73736 | tf_op jit(solution)/shard_map/ppermute | solution.py:63
  12.2 0.1 pad_add_fusion.at_ref
  12.3 0.1 broadcast_in_dim.54
  12.3 0.1 broadcast_in_dim.55
  12.4 0.1 dynamic-slice.8
  12.5 2.2 %collective-permute-done = bf16[96,128]{1,0:T(8,128)(2,1)S(1)} collective-permute-done((bf16[96,128]{1,0:T(8,128)(2,1)S(1)}, bf16[96,128]{1,0:T(8,128)(2,1)S(1)}, u32[]{:S(2)}, u32[]{:S(2)}) %collective-permute-start) | collective-permute-done | bytes 24608 | tf_op jit(solution)/shard_map/ppermute | solution.py:63
  14.7 0.1 dynamic-slice_select_fusion
  14.8 21.2 %all_to_all.30 = bf16[16,24,128]{2,1,0:T(8,128)(2,1)S(1)} all-to-all(bf16[16,24,128]{2,1,0:T(8,128)(2,1)S(1)} %broadcast_in_dim.61), channel_id=1, replica_groups=mesh['yh'=2,'x'=4,'yl'=2,'z'=16,'c'=2] {'z'}, dimensions={0} | all-to-all | bytes 196608 | tf_op jit(solution)/shard_map/all_to_all | solution.py:55
  36.1 1.4 broadcast_in_dim.62
  37.5 0.0 copy-start.1
  37.5 0.0 copy-start.2
  37.5 0.0 copy-start.3
  37.5 6.9 %all-to-all-start.1 = ((bf16[16,16,24,128]{3,2,1,0:T(8,128)(2,1)}), bf16[16,16,24,128]{3,2,1,0:T(8,128)(2,1)}, u32[]{:S(2)}, u32[]{:S(2)}) async-start(bf16[16,16,24,128]{3,2,1,0:T(8,128)(2,1)} %broadcast_in_dim.62), calls=%async_computation.1 | async-start | bytes 3145728 | tf_op jit(solution)/shard_map/all_to_all | solution.py:55
  44.5 0.0 copy-done.1
  44.5 0.0 copy-done.2
  44.5 0.0 copy-done.3
  44.5 5.5 %collective-permute-start.2 = (bf16[12,6144]{1,0:T(8,128)(2,1)S(1)}, bf16[12,6144]{1,0:T(8,128)(2,1)S(1)}, u32[]{:S(2)}, u32[]{:S(2)}) collective-permute-start(bf16[12,6144]{1,0:T(8,128)(2,1)S(1)} %pack.1), channel_id=1, source_target_pairs={{0,0},{1,17},{2,30},{3,15},{4,28},{5,13},{6,26},{7,11},{8,24},{9,9... | collective-permute-start | bytes 442376 | tf_op jit(solution)/shard_map/ppermute | solution.py:235
  50.1 12.3 %collective-permute-done.2 = bf16[12,6144]{1,0:T(8,128)(2,1)S(1)} collective-permute-done((bf16[12,6144]{1,0:T(8,128)(2,1)S(1)}, bf16[12,6144]{1,0:T(8,128)(2,1)S(1)}, u32[]{:S(2)}, u32[]{:S(2)}) %collective-permute-start.2) | collective-permute-done | bytes 147488 | tf_op jit(solution)/shard_map/ppermute | solution.py:235
  62.4 0.0 copy-start.9
  62.4 2.0 %all-to-all-done.1 = bf16[16,16,24,128]{3,2,1,0:T(8,128)(2,1)} async-done(((bf16[16,16,24,128]{3,2,1,0:T(8,128)(2,1)}), bf16[16,16,24,128]{3,2,1,0:T(8,128)(2,1)}, u32[]{:S(2)}, u32[]{:S(2)}) %all-to-all-start.1) | async-done | bytes 1572896 | tf_op jit(solution)/shard_map/all_to_all | solution.py:55
  64.4 0.0 copy-done.9
  64.4 0.0 copy-start
  64.4 2.0 %copy.10 = bf16[2,16,2,4,24,128]{5,4,3,2,1,0:T(8,128)(2,1)S(1)} copy(bf16[2,16,2,4,24,128]{5,4,1,0,2,3:T(8,128)(2,1)} %bitcast.10) | data formatting | bytes 3145728 | tf_op jit(solution)/shard_map/transpose | solution.py:240
  66.4 0.0 collective-permute-done.1.other_ref
  66.4 0.4 copy-done
  66.8 3.7 %product.1 = f32[256,128]{1,0:T(8,128)S(1)} custom-call(bf16[256,6144]{1,0:T(8,128)(2,1)S(1)} %bitcast.35, bf16[256,6144]{1,0:T(8,128)(2,1)} %collective-permute-done.1.other_ref, bf16[6144,128]{1,0:T(8,128)(2,1)S(1)} %bitcast.30), custom_call_target="tpu_custom_call" | custom-call | tf_op jit(solution)/shard_map/product/pallas_call | solution.py:242
  70.5 1.3 collective-permute-start.3
  71.8 15.2 %all_to_all.31 = f32[16,16,128]{2,1,0:T(8,128)S(1)} all-to-all(f32[16,16,128]{2,1,0:T(8,128)S(1)} %bitcast.36), channel_id=1, replica_groups=mesh['yh'=2,'x'=4,'yl'=2,'z'=16,'c'=2] {'yl','yh','x'}, dimensions={0} | all-to-all | bytes 262144 | tf_op jit(solution)/shard_map/all_to_all | solution.py:55
  87.0 0.0 collective-permute-done.3
  87.0 6.8 %collective-permute-start.4 = (bf16[6144,128]{1,0:T(8,128)(2,1)S(1)}, bf16[6144,128]{1,0:T(8,128)(2,1)S(1)}, u32[]{:S(2)}, u32[]{:S(2)}) collective-permute-start(bf16[6144,128]{1,0:T(8,128)(2,1)S(1)} %bitcast.31), channel_id=1, source_target_pairs={{0,1},{1,0},{2,3},{3,2},{4,5},{5,4},{6,7},{7,6},{8,9},{9,8},{10,11... | collective-permute-start | bytes 4718600 | tf_op jit(solution)/shard_map/ppermute | solution.py:63
  93.8 0.6 broadcast_in_dim.64
  94.5 8.6 %all-to-all-start.3 = ((f32[32,8,128]{2,1,0:T(8,128)}), f32[32,8,128]{2,1,0:T(8,128)S(1)}, u32[]{:S(2)}, u32[]{:S(2)}) async-start(f32[32,8,128]{2,1,0:T(8,128)} %bitcast.38), calls=%async_computation.3 | async-start | bytes 262144 | tf_op jit(solution)/shard_map/all_to_all | solution.py:55
  103.1 2.5 %collective-permute-start.5 = (bf16[12,6144]{1,0:T(8,128)(2,1)}, bf16[12,6144]{1,0:T(8,128)(2,1)S(1)}, u32[]{:S(2)}, u32[]{:S(2)}) collective-permute-start(bf16[12,6144]{1,0:T(8,128)(2,1)} %copy-done.9), channel_id=1, source_target_pairs={{0,0},{1,256},{2,451},{3,195},{4,452},{5,196},{6,391},{7,135},{8,3... | collective-permute-start | bytes 442376 | tf_op jit(solution)/shard_map/ppermute | solution.py:252
  105.6 1.9 %collective-permute-start.6 = (bf16[12,6144]{1,0:T(8,128)(2,1)}, bf16[12,6144]{1,0:T(8,128)(2,1)S(1)}, u32[]{:S(2)}, u32[]{:S(2)}) collective-permute-start(bf16[12,6144]{1,0:T(8,128)(2,1)} %collective-permute-done.3), channel_id=1, source_target_pairs={{0,256},{1,0},{2,195},{3,451},{4,196},{5,452},{6,135},{7,391},{8,1... | collective-permute-start | bytes 442376 | tf_op jit(solution)/shard_map/ppermute | solution.py:259
  107.6 5.1 %collective-permute-done.5.one_ref = bf16[12,6144]{1,0:T(8,128)(2,1)S(1)} collective-permute-done((bf16[12,6144]{1,0:T(8,128)(2,1)}, bf16[12,6144]{1,0:T(8,128)(2,1)S(1)}, u32[]{:S(2)}, u32[]{:S(2)}) %collective-permute-start.5) | collective-permute-done | bytes 147488 | tf_op jit(solution)/shard_map/ppermute | solution.py:252
  112.7 0.0 copy-start.5
  112.7 0.7 copy-done.5
  113.4 2.9 %collective-permute-done.6.two_ref = bf16[12,6144]{1,0:T(8,128)(2,1)S(1)} collective-permute-done((bf16[12,6144]{1,0:T(8,128)(2,1)}, bf16[12,6144]{1,0:T(8,128)(2,1)S(1)}, u32[]{:S(2)}, u32[]{:S(2)}) %collective-permute-start.6) | collective-permute-done | bytes 147488 | tf_op jit(solution)/shard_map/ppermute | solution.py:259
  116.2 0.0 copy-start.7
  116.2 0.7 copy-done.7
  116.9 2.6 %all-to-all-done.3.terms_ref = f32[32,8,128]{2,1,0:T(8,128)S(1)} async-done(((f32[32,8,128]{2,1,0:T(8,128)}), f32[32,8,128]{2,1,0:T(8,128)S(1)}, u32[]{:S(2)}, u32[]{:S(2)}) %all-to-all-start.3) | async-done | bytes 131104 | tf_op jit(solution)/shard_map/all_to_all | solution.py:55
  119.5 0.0 collective-permute-done.4.other_ref
  119.5 0.0 copy-start.6
  119.5 0.9 copy-done.6
  120.4 0.0 copy-start.8
  120.4 0.9 copy-done.8
  121.3 1.6 update.1
  123.0 19.1 %all_to_all.32.inbox_ref = f32[32,16,128]{2,1,0:T(8,128)S(1)} all-to-all(f32[32,16,128]{2,1,0:T(8,128)S(1)} %get-tuple-element.43), channel_id=1, replica_groups=mesh['yh'=2,'x'=4,'yl'=2,'z'=16,'c'=2] {'yl','yh','x','c'}, dimensions={0} | all-to-all | bytes 524288 | tf_op jit(solution)/shard_map/all_to_all | solution.py:55
  142.1 0.8 rows.1
  142.9 24.2 %all_to_all.33.rows_ref = bf16[16,8,6144]{2,1,0:T(8,128)(2,1)S(1)} all-to-all(bf16[16,8,6144]{2,1,0:T(8,128)(2,1)S(1)} %get-tuple-element.46), channel_id=1, replica_groups=mesh['yh'=2,'x'=4,'yl'=2,'z'=16,'c'=2] {'x','yh','yl'}, dimensions={0} | all-to-all | bytes 3145728 | tf_op jit(solution)/shard_map/all_to_all | solution.py:55
  167.2 4.2 %collective-permute-start.7 = (bf16[16,8,6144]{2,1,0:T(8,128)(2,1)S(1)}, bf16[16,8,6144]{2,1,0:T(8,128)(2,1)S(1)}, u32[]{:S(2)}, u32[]{:S(2)}) collective-permute-start(bf16[16,8,6144]{2,1,0:T(8,128)(2,1)S(1)} %all_to_all.33.rows_ref), channel_id=1, source_target_pairs={{0,1},{1,0},{2,3},{3,2},{4,5},{5,4},{6,7},{7,6},{8,9},{9,8},{10,11... | collective-permute-start | bytes 4718600 | tf_op jit(solution)/shard_map/ppermute | solution.py:63
  171.3 1.8 %place.2.refs_0_ = bf16[16,2,8,6144]{3,2,1,0:T(8,128)(2,1)} custom-call(s32[4]{0:T(128)S(1)} %pad_add_fusion.at_ref, bf16[16,8,6144]{2,1,0:T(8,128)(2,1)S(1)} %all_to_all.33.rows_ref), custom_call_target="tpu_custom_call" | custom-call | bytes 3145728 | tf_op jit(solution)/shard_map/place/pallas_call | solution.py:195
  173.2 0.5 fusion
  173.7 0.0 copy-start.4
  173.7 0.5 slice.12
  174.9 0.5 convolution_add_fusion
  175.4 0.0 copy-done.4
  175.4 0.9 multiply_subtract_fusion
  176.3 0.0 collective-permute-done.7.rows_ref
  176.3 1.8 %place.3 = bf16[16,2,8,6144]{3,2,1,0:T(8,128)(2,1)} custom-call(s32[4]{0:T(128)S(1)} %pad_add_fusion.at_ref, bf16[16,8,6144]{2,1,0:T(8,128)(2,1)S(1)} %collective-permute-done.7.rows_ref, bf16[16,2,8,6144]{3,2,1,0:T(8,128)(2,1)} %place.2.refs_0_), custom_call_target="tpu_custom_call", output_to_operand_aliasing={{}: (2, {})} | custom-call | bytes 3145728 | tf_op jit(solution)/shard_map/place/pallas_call | solution.py:195
  (6 shorter events, 0.1 us)
Async XLA Ops:
  0.6 65.8 %collective-permute-start.1 = (bf16[256,6144]{1,0:T(8,128)(2,1)}, bf16[256,6144]{1,0:T(8,128)(2,1)}, u32[]{:S(2)}, u32[]{:S(2)}) collective-permute-start(bf16[256,6144]{1,0:T(8,128)(2,1)} %bitcast.34), channel_id=1, source_target_pairs={{0,1},{1,0},{2,3},{3,2},{4,5},{5,4},{6,7},{7,6},{8,9},{9,8},{10,11... | collective-permute-start | bytes 9437192 | tf_op jit(solution)/shard_map/ppermute | solution.py:63
  10.2 4.5 %collective-permute-start = (bf16[96,128]{1,0:T(8,128)(2,1)S(1)}, bf16[96,128]{1,0:T(8,128)(2,1)S(1)}, u32[]{:S(2)}, u32[]{:S(2)}) collective-permute-start(bf16[96,128]{1,0:T(8,128)(2,1)S(1)} %get-tuple-element.58), channel_id=1, source_target_pairs={{0,1},{1,0},{2,3},{3,2},{4,5},{5,4},{6,7},{7,6},{8,9},{9,8},{10,11... | collective-permute-start | bytes 73736 | tf_op jit(solution)/shard_map/ppermute | solution.py:63
  37.5 6.9 %copy-start.1 = (f32[1,4,6144]{2,1,0:T(4,128)S(1)}, f32[1,4,6144]{2,1,0:T(4,128)}, u32[]{:S(2)}) copy-start(f32[1,4,6144]{2,1,0:T(4,128)} %weights_ref) | copy-start | bytes 294916
  37.5 7.0 %copy-start.2 = (f32[1,4,6144]{2,1,0:T(4,128)S(1)}, f32[1,4,6144]{2,1,0:T(4,128)}, u32[]{:S(2)}) copy-start(f32[1,4,6144]{2,1,0:T(4,128)} %moment_ref) | copy-start | bytes 294916
  37.5 7.0 %copy-start.3 = (f32[1,4,6144]{2,1,0:T(4,128)S(1)}, f32[1,4,6144]{2,1,0:T(4,128)}, u32[]{:S(2)}) copy-start(f32[1,4,6144]{2,1,0:T(4,128)} %second_ref) | copy-start | bytes 294916
  37.5 26.9 %all-to-all-start.1 = ((bf16[16,16,24,128]{3,2,1,0:T(8,128)(2,1)}), bf16[16,16,24,128]{3,2,1,0:T(8,128)(2,1)}, u32[]{:S(2)}, u32[]{:S(2)}) async-start(bf16[16,16,24,128]{3,2,1,0:T(8,128)(2,1)} %broadcast_in_dim.62), calls=%async_computation.1 | async-start | bytes 3145728 | tf_op jit(solution)/shard_map/all_to_all | solution.py:55
  44.5 17.8 %collective-permute-start.2 = (bf16[12,6144]{1,0:T(8,128)(2,1)S(1)}, bf16[12,6144]{1,0:T(8,128)(2,1)S(1)}, u32[]{:S(2)}, u32[]{:S(2)}) collective-permute-start(bf16[12,6144]{1,0:T(8,128)(2,1)S(1)} %pack.1), channel_id=1, source_target_pairs={{0,0},{1,17},{2,30},{3,15},{4,28},{5,13},{6,26},{7,11},{8,24},{9,9... | collective-permute-start | bytes 442376 | tf_op jit(solution)/shard_map/ppermute | solution.py:235
  62.4 2.0 %copy-start.9 = (bf16[12,6144]{1,0:T(8,128)(2,1)}, bf16[12,6144]{1,0:T(8,128)(2,1)S(1)}, u32[]{:S(2)}) copy-start(bf16[12,6144]{1,0:T(8,128)(2,1)S(1)} %collective-permute-done.2) | copy-start | bytes 442372
  64.4 2.4 %copy-start = (bf16[1,1,1,256,6144]{4,3,2,1,0:T(8,128)(2,1)S(1)}, bf16[1,1,1,256,6144]{4,3,2,1,0:T(8,128)(2,1)}, u32[]{:S(2)}) copy-start(bf16[1,1,1,256,6144]{4,3,2,1,0:T(8,128)(2,1)} %param.5) | copy-start | bytes 9437188
  70.5 16.5 %collective-permute-start.3 = (bf16[12,6144]{1,0:T(8,128)(2,1)S(1)}, bf16[12,6144]{1,0:T(8,128)(2,1)}, u32[]{:S(2)}, u32[]{:S(2)}) collective-permute-start(bf16[12,6144]{1,0:T(8,128)(2,1)S(1)} %pack.1), channel_id=1, source_target_pairs={{0,16},{1,1},{2,14},{3,31},{4,12},{5,29},{6,10},{7,27},{8,8},{9,25... | collective-permute-start | bytes 442376 | tf_op jit(solution)/shard_map/ppermute | solution.py:251
  87.0 32.5 %collective-permute-start.4 = (bf16[6144,128]{1,0:T(8,128)(2,1)S(1)}, bf16[6144,128]{1,0:T(8,128)(2,1)S(1)}, u32[]{:S(2)}, u32[]{:S(2)}) collective-permute-start(bf16[6144,128]{1,0:T(8,128)(2,1)S(1)} %bitcast.31), channel_id=1, source_target_pairs={{0,1},{1,0},{2,3},{3,2},{4,5},{5,4},{6,7},{7,6},{8,9},{9,8},{10,11... | collective-permute-start | bytes 4718600 | tf_op jit(solution)/shard_map/ppermute | solution.py:63
  94.5 25.0 %all-to-all-start.3 = ((f32[32,8,128]{2,1,0:T(8,128)}), f32[32,8,128]{2,1,0:T(8,128)S(1)}, u32[]{:S(2)}, u32[]{:S(2)}) async-start(f32[32,8,128]{2,1,0:T(8,128)} %bitcast.38), calls=%async_computation.3 | async-start | bytes 262144 | tf_op jit(solution)/shard_map/all_to_all | solution.py:55
  103.1 9.6 %collective-permute-start.5 = (bf16[12,6144]{1,0:T(8,128)(2,1)}, bf16[12,6144]{1,0:T(8,128)(2,1)S(1)}, u32[]{:S(2)}, u32[]{:S(2)}) collective-permute-start(bf16[12,6144]{1,0:T(8,128)(2,1)} %copy-done.9), channel_id=1, source_target_pairs={{0,0},{1,256},{2,451},{3,195},{4,452},{5,196},{6,391},{7,135},{8,3... | collective-permute-start | bytes 442376 | tf_op jit(solution)/shard_map/ppermute | solution.py:252
  105.6 10.6 %collective-permute-start.6 = (bf16[12,6144]{1,0:T(8,128)(2,1)}, bf16[12,6144]{1,0:T(8,128)(2,1)S(1)}, u32[]{:S(2)}, u32[]{:S(2)}) collective-permute-start(bf16[12,6144]{1,0:T(8,128)(2,1)} %collective-permute-done.3), channel_id=1, source_target_pairs={{0,256},{1,0},{2,195},{3,451},{4,196},{5,452},{6,135},{7,391},{8,1... | collective-permute-start | bytes 442376 | tf_op jit(solution)/shard_map/ppermute | solution.py:259
  112.7 0.7 copy-start.5
  116.2 0.7 copy-start.7
  119.5 0.9 copy-start.6
  120.4 0.9 copy-start.8
  167.2 9.1 %collective-permute-start.7 = (bf16[16,8,6144]{2,1,0:T(8,128)(2,1)S(1)}, bf16[16,8,6144]{2,1,0:T(8,128)(2,1)S(1)}, u32[]{:S(2)}, u32[]{:S(2)}) collective-permute-start(bf16[16,8,6144]{2,1,0:T(8,128)(2,1)S(1)} %all_to_all.33.rows_ref), channel_id=1, source_target_pairs={{0,1},{1,0},{2,3},{3,2},{4,5},{5,4},{6,7},{7,6},{8,9},{9,8},{10,11... | collective-permute-start | bytes 4718600 | tf_op jit(solution)/shard_map/ppermute | solution.py:63
  173.7 1.7 copy-start.4

commit v10 on v9

--- a/solution.py
+++ b/solution.py
@@ -251,8 +251,8 @@
     came_two = lax.ppermute(state, ALL, along_z_moves(1))
     state_one = lax.ppermute(came_one, ALL, in_plane_moves(0))
     plane_terms = exchange(sketch.reshape(16, 16, half), PLANE)
-    plane_terms, came_two, basis_sent = lax.optimization_barrier(
-        (plane_terms, came_two, own_basis)
+    plane_terms, came_two, state_one, basis_sent = lax.optimization_barrier(
+        (plane_terms, came_two, state_one, own_basis)
     )
     other_basis = swap(basis_sent)
     plane_sum = jnp.sum(plane_terms, axis=0)

time: 180 us -> 177 us (0.983)
  blocking collectives: 79.8 us -> 67.8 us
  starting transfers between devices: 48.5 us -> 55 us
  waiting for transfers between devices: 27.1 us -> 30.1 us
    all_to_all x4, blocking collectives: 79.8 us -> 67.8 us  [exchange(): return lax.all_to_all(blocks, axes, 0, 0, tiled=True)]
    ppermute x1, starting transfers between devices: 2.54 us -> 11.2 us  [on_device(): state_one = lax.ppermute(came_one, ALL, in_plane_moves(0))]
    ppermute x1, waiting for transfers between devices: 5.12 us -> 0.01 us  [on_device(): state_one = lax.ppermute(came_one, ALL, in_plane_moves(0))]
    all_to_all x2, waiting for transfers between devices: 4.59 us -> 9.62 us  [exchange(): return lax.all_to_all(blocks, axes, 0, 0, tiled=True)]
    ppermute x1, waiting for transfers between devices: 2.86 us -> 5.97 us  [on_device(): state_two = lax.ppermute(came_two, ALL, in_plane_moves(1))]
  transfers between devices with their start and end apart: 10 -> 10, of which waited for: 6 -> 5; matrix products, arithmetic and copies ran while one was open for 4% -> 4% of each run, Pallas kernels for 1% -> 1%
where the time goes in v10:
time: 177 us; the launch traced here: 176 us
  blocking collectives  67.8 us (38%)
  starting transfers between devices  55 us (31%)
  waiting for transfers between devices  30.1 us (17%)
  local copies, waits for them, and re-layouts  9.88 us (6%)
  Pallas kernels  9.83 us (6%)
    all_to_all x4, blocking collectives, exchange(): return lax.all_to_all(blocks, axes, 0, 0, tiled=True)  67.8 us
    ppermute x4, starting transfers between devices, swap(): return lax.ppermute(block, 'c', SWAP)  21.1 us
    all_to_all x2, starting transfers between devices, exchange(): return lax.all_to_all(blocks, axes, 0, 0, tiled=True)  14.4 us
    ppermute x1, waiting for transfers between devices, on_device(): came_one = lax.ppermute(state, ALL, along_z_moves(0))  12.3 us
    ppermute x1, starting transfers between devices, on_device(): state_one = lax.ppermute(came_one, ALL, in_plane_moves(0))  11.2 us
    all_to_all x2, waiting for transfers between devices, exchange(): return lax.all_to_all(blocks, axes, 0, 0, tiled=True)  9.62 us
    ppermute x1, waiting for transfers between devices, on_device(): state_two = lax.ppermute(came_two, ALL, in_plane_moves(1))  5.97 us
    ppermute x1, starting transfers between devices, on_device(): came_one = lax.ppermute(state, ALL, along_z_moves(0))  5.53 us
  transfers between devices with their start and end apart: 10, of which 5 were waited for; matrix products, arithmetic and copies ran while one was open for 4% of the time, Pallas kernels for 1%

profile of v10, /device:TPU:1, one launch (start us, length us, event | category | flops | bytes accessed | tf_op | source)
XLA Modules:
  0.0 176.2 jit_solution(3594915816627614346)
XLA Ops:
  0.6 8.8 %collective-permute-start.1 = (bf16[256,6144]{1,0:T(8,128)(2,1)}, bf16[256,6144]{1,0:T(8,128)(2,1)}, u32[]{:S(2)}, u32[]{:S(2)}) collective-permute-start(bf16[256,6144]{1,0:T(8,128)(2,1)} %bitcast.34), channel_id=1, source_target_pairs={{0,1},{1,0},{2,3},{3,2},{4,5},{5,4},{6,7},{7,6},{8,9},{9,8},{10,11... | collective-permute-start | bytes 9437192 | tf_op jit(solution)/shard_map/ppermute | solution.py:63
  9.4 0.8 dynamic-slice_bitcast_fusion.1
  10.2 1.9 %collective-permute-start = (bf16[96,128]{1,0:T(8,128)(2,1)S(1)}, bf16[96,128]{1,0:T(8,128)(2,1)S(1)}, u32[]{:S(2)}, u32[]{:S(2)}) collective-permute-start(bf16[96,128]{1,0:T(8,128)(2,1)S(1)} %get-tuple-element.60), channel_id=1, source_target_pairs={{0,1},{1,0},{2,3},{3,2},{4,5},{5,4},{6,7},{7,6},{8,9},{9,8},{10,11... | collective-permute-start | bytes 73736 | tf_op jit(solution)/shard_map/ppermute | solution.py:63
  12.2 0.1 pad_add_fusion.at_ref
  12.3 0.1 broadcast_in_dim.54
  12.3 0.1 broadcast_in_dim.55
  12.4 0.1 dynamic-slice.8
  12.5 2.2 %collective-permute-done = bf16[96,128]{1,0:T(8,128)(2,1)S(1)} collective-permute-done((bf16[96,128]{1,0:T(8,128)(2,1)S(1)}, bf16[96,128]{1,0:T(8,128)(2,1)S(1)}, u32[]{:S(2)}, u32[]{:S(2)}) %collective-permute-start) | collective-permute-done | bytes 24608 | tf_op jit(solution)/shard_map/ppermute | solution.py:63
  14.7 0.1 dynamic-slice_select_fusion
  14.8 21.2 %all_to_all.30 = bf16[16,24,128]{2,1,0:T(8,128)(2,1)S(1)} all-to-all(bf16[16,24,128]{2,1,0:T(8,128)(2,1)S(1)} %broadcast_in_dim.61), channel_id=1, replica_groups=mesh['yh'=2,'x'=4,'yl'=2,'z'=16,'c'=2] {'z'}, dimensions={0} | all-to-all | bytes 196608 | tf_op jit(solution)/shard_map/all_to_all | solution.py:55
  36.1 1.4 broadcast_in_dim.62
  37.5 0.0 copy-start.1
  37.5 0.0 copy-start.2
  37.5 0.0 copy-start.3
  37.5 6.9 %all-to-all-start.1 = ((bf16[16,16,24,128]{3,2,1,0:T(8,128)(2,1)}), bf16[16,16,24,128]{3,2,1,0:T(8,128)(2,1)}, u32[]{:S(2)}, u32[]{:S(2)}) async-start(bf16[16,16,24,128]{3,2,1,0:T(8,128)(2,1)} %broadcast_in_dim.62), calls=%async_computation.1 | async-start | bytes 3145728 | tf_op jit(solution)/shard_map/all_to_all | solution.py:55
  44.5 0.0 copy-done.1
  44.5 0.0 copy-done.2
  44.5 0.0 copy-done.3
  44.5 5.5 %collective-permute-start.2 = (bf16[12,6144]{1,0:T(8,128)(2,1)S(1)}, bf16[12,6144]{1,0:T(8,128)(2,1)S(1)}, u32[]{:S(2)}, u32[]{:S(2)}) collective-permute-start(bf16[12,6144]{1,0:T(8,128)(2,1)S(1)} %pack.1), channel_id=1, source_target_pairs={{0,0},{1,17},{2,30},{3,15},{4,28},{5,13},{6,26},{7,11},{8,24},{9,9... | collective-permute-start | bytes 442376 | tf_op jit(solution)/shard_map/ppermute | solution.py:235
  50.1 12.3 %collective-permute-done.2 = bf16[12,6144]{1,0:T(8,128)(2,1)S(1)} collective-permute-done((bf16[12,6144]{1,0:T(8,128)(2,1)S(1)}, bf16[12,6144]{1,0:T(8,128)(2,1)S(1)}, u32[]{:S(2)}, u32[]{:S(2)}) %collective-permute-start.2) | collective-permute-done | bytes 147488 | tf_op jit(solution)/shard_map/ppermute | solution.py:235
  62.4 2.0 %all-to-all-done.1 = bf16[16,16,24,128]{3,2,1,0:T(8,128)(2,1)} async-done(((bf16[16,16,24,128]{3,2,1,0:T(8,128)(2,1)}), bf16[16,16,24,128]{3,2,1,0:T(8,128)(2,1)}, u32[]{:S(2)}, u32[]{:S(2)}) %all-to-all-start.1) | async-done | bytes 1572896 | tf_op jit(solution)/shard_map/all_to_all | solution.py:55
  64.4 0.0 copy-start
  64.4 2.0 %copy.10 = bf16[2,16,2,4,24,128]{5,4,3,2,1,0:T(8,128)(2,1)S(1)} copy(bf16[2,16,2,4,24,128]{5,4,1,0,2,3:T(8,128)(2,1)} %bitcast.10) | data formatting | bytes 3145728 | tf_op jit(solution)/shard_map/transpose | solution.py:240
  66.4 0.0 collective-permute-done.1.other_ref
  66.4 0.4 copy-done
  66.8 3.7 %product.1 = f32[256,128]{1,0:T(8,128)S(1)} custom-call(bf16[256,6144]{1,0:T(8,128)(2,1)S(1)} %bitcast.35, bf16[256,6144]{1,0:T(8,128)(2,1)} %collective-permute-done.1.other_ref, bf16[6144,128]{1,0:T(8,128)(2,1)S(1)} %bitcast.30), custom_call_target="tpu_custom_call" | custom-call | tf_op jit(solution)/shard_map/product/pallas_call | solution.py:242
  70.5 0.7 collective-permute-start.3
  71.1 11.2 %collective-permute-start.4 = (bf16[12,6144]{1,0:T(8,128)(2,1)S(1)}, bf16[12,6144]{1,0:T(8,128)(2,1)S(1)}, u32[]{:S(2)}, u32[]{:S(2)}) collective-permute-start(bf16[12,6144]{1,0:T(8,128)(2,1)S(1)} %collective-permute-done.2), channel_id=1, source_target_pairs={{0,0},{1,256},{2,451},{3,195},{4,452},{5,196},{6,391},{7,135},{8,3... | collective-permute-start | bytes 442376 | tf_op jit(solution)/shard_map/ppermute | solution.py:252
  82.4 9.9 %all_to_all.31 = f32[16,16,128]{2,1,0:T(8,128)S(1)} all-to-all(f32[16,16,128]{2,1,0:T(8,128)S(1)} %bitcast.36), channel_id=1, replica_groups=mesh['yh'=2,'x'=4,'yl'=2,'z'=16,'c'=2] {'yl','yh','x'}, dimensions={0} | all-to-all | bytes 262144 | tf_op jit(solution)/shard_map/all_to_all | solution.py:55
  92.2 0.0 collective-permute-done.3
  92.2 0.0 copy-start.9
  92.2 0.7 copy-done.9
  92.9 0.0 collective-permute-done.4.one_ref
  92.9 0.0 copy-start.5
  92.9 0.7 copy-done.5
  93.6 6.2 %collective-permute-start.5 = (bf16[6144,128]{1,0:T(8,128)(2,1)S(1)}, bf16[6144,128]{1,0:T(8,128)(2,1)S(1)}, u32[]{:S(2)}, u32[]{:S(2)}) collective-permute-start(bf16[6144,128]{1,0:T(8,128)(2,1)S(1)} %bitcast.31), channel_id=1, source_target_pairs={{0,1},{1,0},{2,3},{3,2},{4,5},{5,4},{6,7},{7,6},{8,9},{9,8},{10,11... | collective-permute-start | bytes 4718600 | tf_op jit(solution)/shard_map/ppermute | solution.py:63
  99.8 0.6 broadcast_in_dim.64
  100.4 7.5 %all-to-all-start.3 = ((f32[32,8,128]{2,1,0:T(8,128)}), f32[32,8,128]{2,1,0:T(8,128)S(1)}, u32[]{:S(2)}, u32[]{:S(2)}) async-start(f32[32,8,128]{2,1,0:T(8,128)} %bitcast.38), calls=%async_computation.3 | async-start | bytes 262144 | tf_op jit(solution)/shard_map/all_to_all | solution.py:55
  107.9 2.1 %collective-permute-start.6 = (bf16[12,6144]{1,0:T(8,128)(2,1)}, bf16[12,6144]{1,0:T(8,128)(2,1)S(1)}, u32[]{:S(2)}, u32[]{:S(2)}) collective-permute-start(bf16[12,6144]{1,0:T(8,128)(2,1)} %copy-done.9), channel_id=1, source_target_pairs={{0,256},{1,0},{2,195},{3,451},{4,196},{5,452},{6,135},{7,391},{8,1... | collective-permute-start | bytes 442376 | tf_op jit(solution)/shard_map/ppermute | solution.py:259
  110.1 6.0 %collective-permute-done.6.two_ref = bf16[12,6144]{1,0:T(8,128)(2,1)S(1)} collective-permute-done((bf16[12,6144]{1,0:T(8,128)(2,1)}, bf16[12,6144]{1,0:T(8,128)(2,1)S(1)}, u32[]{:S(2)}, u32[]{:S(2)}) %collective-permute-start.6) | collective-permute-done | bytes 147488 | tf_op jit(solution)/shard_map/ppermute | solution.py:259
  116.0 0.0 copy-start.7
  116.0 0.7 copy-done.7
  116.7 7.6 %all-to-all-done.3.terms_ref = f32[32,8,128]{2,1,0:T(8,128)S(1)} async-done(((f32[32,8,128]{2,1,0:T(8,128)}), f32[32,8,128]{2,1,0:T(8,128)S(1)}, u32[]{:S(2)}, u32[]{:S(2)}) %all-to-all-start.3) | async-done | bytes 131104 | tf_op jit(solution)/shard_map/all_to_all | solution.py:55
  124.3 0.0 collective-permute-done.5.other_ref
  124.3 0.0 copy-start.6
  124.3 0.9 copy-done.6
  125.2 0.0 copy-start.8
  125.2 0.9 copy-done.8
  126.1 1.6 update.1
  127.8 12.5 %all_to_all.32.inbox_ref = f32[32,16,128]{2,1,0:T(8,128)S(1)} all-to-all(f32[32,16,128]{2,1,0:T(8,128)S(1)} %get-tuple-element.45), channel_id=1, replica_groups=mesh['yh'=2,'x'=4,'yl'=2,'z'=16,'c'=2] {'yl','yh','x','c'}, dimensions={0} | all-to-all | bytes 524288 | tf_op jit(solution)/shard_map/all_to_all | solution.py:55
  140.3 0.8 rows.1
  141.1 24.2 %all_to_all.33.rows_ref = bf16[16,8,6144]{2,1,0:T(8,128)(2,1)S(1)} all-to-all(bf16[16,8,6144]{2,1,0:T(8,128)(2,1)S(1)} %get-tuple-element.48), channel_id=1, replica_groups=mesh['yh'=2,'x'=4,'yl'=2,'z'=16,'c'=2] {'x','yh','yl'}, dimensions={0} | all-to-all | bytes 3145728 | tf_op jit(solution)/shard_map/all_to_all | solution.py:55
  165.3 4.2 %collective-permute-start.7 = (bf16[16,8,6144]{2,1,0:T(8,128)(2,1)S(1)}, bf16[16,8,6144]{2,1,0:T(8,128)(2,1)S(1)}, u32[]{:S(2)}, u32[]{:S(2)}) collective-permute-start(bf16[16,8,6144]{2,1,0:T(8,128)(2,1)S(1)} %all_to_all.33.rows_ref), channel_id=1, source_target_pairs={{0,1},{1,0},{2,3},{3,2},{4,5},{5,4},{6,7},{7,6},{8,9},{9,8},{10,11... | collective-permute-start | bytes 4718600 | tf_op jit(solution)/shard_map/ppermute | solution.py:63
  169.5 1.8 %place.2.refs_0_ = bf16[16,2,8,6144]{3,2,1,0:T(8,128)(2,1)} custom-call(s32[4]{0:T(128)S(1)} %pad_add_fusion.at_ref, bf16[16,8,6144]{2,1,0:T(8,128)(2,1)S(1)} %all_to_all.33.rows_ref), custom_call_target="tpu_custom_call" | custom-call | bytes 3145728 | tf_op jit(solution)/shard_map/place/pallas_call | solution.py:195
  171.3 0.5 fusion
  171.8 0.0 copy-start.4
  171.8 0.5 slice.12
  173.0 0.5 convolution_add_fusion
  173.5 0.0 copy-done.4
  173.5 0.9 multiply_subtract_fusion
  174.4 0.0 collective-permute-done.7.rows_ref
  174.4 1.8 %place.3 = bf16[16,2,8,6144]{3,2,1,0:T(8,128)(2,1)} custom-call(s32[4]{0:T(128)S(1)} %pad_add_fusion.at_ref, bf16[16,8,6144]{2,1,0:T(8,128)(2,1)S(1)} %collective-permute-done.7.rows_ref, bf16[16,2,8,6144]{3,2,1,0:T(8,128)(2,1)} %place.2.refs_0_), custom_call_target="tpu_custom_call", output_to_operand_aliasing={{}: (2, {})} | custom-call | bytes 3145728 | tf_op jit(solution)/shard_map/place/pallas_call | solution.py:195
  (6 shorter events, 0.1 us)
Async XLA Ops:
  0.6 65.8 %collective-permute-start.1 = (bf16[256,6144]{1,0:T(8,128)(2,1)}, bf16[256,6144]{1,0:T(8,128)(2,1)}, u32[]{:S(2)}, u32[]{:S(2)}) collective-permute-start(bf16[256,6144]{1,0:T(8,128)(2,1)} %bitcast.34), channel_id=1, source_target_pairs={{0,1},{1,0},{2,3},{3,2},{4,5},{5,4},{6,7},{7,6},{8,9},{9,8},{10,11... | collective-permute-start | bytes 9437192 | tf_op jit(solution)/shard_map/ppermute | solution.py:63
  10.2 4.5 %collective-permute-start = (bf16[96,128]{1,0:T(8,128)(2,1)S(1)}, bf16[96,128]{1,0:T(8,128)(2,1)S(1)}, u32[]{:S(2)}, u32[]{:S(2)}) collective-permute-start(bf16[96,128]{1,0:T(8,128)(2,1)S(1)} %get-tuple-element.60), channel_id=1, source_target_pairs={{0,1},{1,0},{2,3},{3,2},{4,5},{5,4},{6,7},{7,6},{8,9},{9,8},{10,11... | collective-permute-start | bytes 73736 | tf_op jit(solution)/shard_map/ppermute | solution.py:63
  37.5 6.9 %copy-start.1 = (f32[1,4,6144]{2,1,0:T(4,128)S(1)}, f32[1,4,6144]{2,1,0:T(4,128)}, u32[]{:S(2)}) copy-start(f32[1,4,6144]{2,1,0:T(4,128)} %weights_ref) | copy-start | bytes 294916
  37.5 7.0 %copy-start.2 = (f32[1,4,6144]{2,1,0:T(4,128)S(1)}, f32[1,4,6144]{2,1,0:T(4,128)}, u32[]{:S(2)}) copy-start(f32[1,4,6144]{2,1,0:T(4,128)} %moment_ref) | copy-start | bytes 294916
  37.5 7.0 %copy-start.3 = (f32[1,4,6144]{2,1,0:T(4,128)S(1)}, f32[1,4,6144]{2,1,0:T(4,128)}, u32[]{:S(2)}) copy-start(f32[1,4,6144]{2,1,0:T(4,128)} %second_ref) | copy-start | bytes 294916
  37.5 26.9 %all-to-all-start.1 = ((bf16[16,16,24,128]{3,2,1,0:T(8,128)(2,1)}), bf16[16,16,24,128]{3,2,1,0:T(8,128)(2,1)}, u32[]{:S(2)}, u32[]{:S(2)}) async-start(bf16[16,16,24,128]{3,2,1,0:T(8,128)(2,1)} %broadcast_in_dim.62), calls=%async_computation.1 | async-start | bytes 3145728 | tf_op jit(solution)/shard_map/all_to_all | solution.py:55
  44.5 17.8 %collective-permute-start.2 = (bf16[12,6144]{1,0:T(8,128)(2,1)S(1)}, bf16[12,6144]{1,0:T(8,128)(2,1)S(1)}, u32[]{:S(2)}, u32[]{:S(2)}) collective-permute-start(bf16[12,6144]{1,0:T(8,128)(2,1)S(1)} %pack.1), channel_id=1, source_target_pairs={{0,0},{1,17},{2,30},{3,15},{4,28},{5,13},{6,26},{7,11},{8,24},{9,9... | collective-permute-start | bytes 442376 | tf_op jit(solution)/shard_map/ppermute | solution.py:235
  64.4 2.4 %copy-start = (bf16[1,1,1,256,6144]{4,3,2,1,0:T(8,128)(2,1)S(1)}, bf16[1,1,1,256,6144]{4,3,2,1,0:T(8,128)(2,1)}, u32[]{:S(2)}) copy-start(bf16[1,1,1,256,6144]{4,3,2,1,0:T(8,128)(2,1)} %param.5) | copy-start | bytes 9437188
  70.5 21.8 %collective-permute-start.3 = (bf16[12,6144]{1,0:T(8,128)(2,1)S(1)}, bf16[12,6144]{1,0:T(8,128)(2,1)S(1)}, u32[]{:S(2)}, u32[]{:S(2)}) collective-permute-start(bf16[12,6144]{1,0:T(8,128)(2,1)S(1)} %pack.1), channel_id=1, source_target_pairs={{0,16},{1,1},{2,14},{3,31},{4,12},{5,29},{6,10},{7,27},{8,8},{9,25... | collective-permute-start | bytes 442376 | tf_op jit(solution)/shard_map/ppermute | solution.py:251
  71.1 21.8 %collective-permute-start.4 = (bf16[12,6144]{1,0:T(8,128)(2,1)S(1)}, bf16[12,6144]{1,0:T(8,128)(2,1)S(1)}, u32[]{:S(2)}, u32[]{:S(2)}) collective-permute-start(bf16[12,6144]{1,0:T(8,128)(2,1)S(1)} %collective-permute-done.2), channel_id=1, source_target_pairs={{0,0},{1,256},{2,451},{3,195},{4,452},{5,196},{6,391},{7,135},{8,3... | collective-permute-start | bytes 442376 | tf_op jit(solution)/shard_map/ppermute | solution.py:252
  92.2 0.7 copy-start.9
  92.9 0.7 copy-start.5
  93.6 30.7 %collective-permute-start.5 = (bf16[6144,128]{1,0:T(8,128)(2,1)S(1)}, bf16[6144,128]{1,0:T(8,128)(2,1)S(1)}, u32[]{:S(2)}, u32[]{:S(2)}) collective-permute-start(bf16[6144,128]{1,0:T(8,128)(2,1)S(1)} %bitcast.31), channel_id=1, source_target_pairs={{0,1},{1,0},{2,3},{3,2},{4,5},{5,4},{6,7},{7,6},{8,9},{9,8},{10,11... | collective-permute-start | bytes 4718600 | tf_op jit(solution)/shard_map/ppermute | solution.py:63
  100.4 23.8 %all-to-all-start.3 = ((f32[32,8,128]{2,1,0:T(8,128)}), f32[32,8,128]{2,1,0:T(8,128)S(1)}, u32[]{:S(2)}, u32[]{:S(2)}) async-start(f32[32,8,128]{2,1,0:T(8,128)} %bitcast.38), calls=%async_computation.3 | async-start | bytes 262144 | tf_op jit(solution)/shard_map/all_to_all | solution.py:55
  107.9 8.1 %collective-permute-start.6 = (bf16[12,6144]{1,0:T(8,128)(2,1)}, bf16[12,6144]{1,0:T(8,128)(2,1)S(1)}, u32[]{:S(2)}, u32[]{:S(2)}) collective-permute-start(bf16[12,6144]{1,0:T(8,128)(2,1)} %copy-done.9), channel_id=1, source_target_pairs={{0,256},{1,0},{2,195},{3,451},{4,196},{5,452},{6,135},{7,391},{8,1... | collective-permute-start | bytes 442376 | tf_op jit(solution)/shard_map/ppermute | solution.py:259
  116.0 0.7 copy-start.7
  124.3 0.9 copy-start.6
  125.2 0.9 copy-start.8
  165.3 9.1 %collective-permute-start.7 = (bf16[16,8,6144]{2,1,0:T(8,128)(2,1)S(1)}, bf16[16,8,6144]{2,1,0:T(8,128)(2,1)S(1)}, u32[]{:S(2)}, u32[]{:S(2)}) collective-permute-start(bf16[16,8,6144]{2,1,0:T(8,128)(2,1)S(1)} %all_to_all.33.rows_ref), channel_id=1, source_target_pairs={{0,1},{1,0},{2,3},{3,2},{4,5},{5,4},{6,7},{7,6},{8,9},{9,8},{10,11... | collective-permute-start | bytes 4718600 | tf_op jit(solution)/shard_map/ppermute | solution.py:63
  171.8 1.7 copy-start.4
